TPU v7x, 32 devices: a whole 2x2x4 slice. The times are simulated.
32 devices in a mesh: cfg: 2 (over y), tm: 8 (over z, x), space: 2 (over core).
Axes of the slice: x: 2, y: 2, z: 4, core: 2. Of those that a mesh axis runs over, the one named last changes fastest.
Arguments:
- vectors: bfloat16 [16, 2, 3, 8, 4, 16, 128], P(('cfg', 'tm'), None, None, 'space'), parts along dimension 0, may hold values from -6 to 6
- gauge_links: float32 [16, 3, 2, 3, 3, 8, 4, 16], P(('cfg', 'tm'), None, None, None, None, 'space'), parts along dimension 0, may hold values from -2.5 to 2.5
- perambulators: bfloat16 [16, 8, 4, 128, 256], P(('cfg', 'tm')), parts along dimension 0, may hold values from -0.375 to 0.375
- momenta: int32 [8, 3], replicated, may hold values from -2 to 2
- displacements: int32 [8], replicated, may hold values from 0 to 3, as said below
Outputs:
- elementals: bfloat16 [16, 8, 128, 256], P(('cfg', 'tm'), None, 'space'), parts along dimension 0
- correlators: float32 [8, 16, 8], P(None, ('cfg', 'tm')), parts along dimension 1
There are 2 independent parts, one for each index of `cfg`. A program takes and returns all parts, laid end to end along the dimension named above; an argument that names none is the same for every part. Nothing has to cross between parts.
Inputs may be any that keep to these rules, and one draw needn't show every extreme that they name: `displacements`: each of the values 0, 1, 2, 3 appears exactly 2 times.
All inputs are finite; a program needn't handle non-finite values.
Results may differ from a plain program's by a relative error of at most 0.0075.
Values may be sent and summed in bfloat16 or wider, within the bound.
No kernel may reach another device: no remote copies, remote signals or barrier semaphores. Data moves between devices by JAX's collectives and lax.ppermute only.
A program may use at most 64 MiB of HBM per device.

v0:
```python
import functools
import math

import jax
import jax.numpy as jnp
from jax import lax
from jax.experimental import pallas as pl
from jax.experimental.pallas import tpu as pltpu
from jax.sharding import PartitionSpec as P

ROWS = 16
UNROLL = 8
VALUES = (2, 3, 1, 0)


def pick_operator(disp_ref, value, last):
    count = disp_ref.shape[0]
    first_seen = jnp.int32(count)
    last_seen = jnp.int32(-1)
    for o in range(count):
        hit = disp_ref[o] == value
        first_seen = jnp.where(hit, jnp.minimum(first_seen, o), first_seen)
        last_seen = jnp.where(hit, o, last_seen)
    return jnp.where(last == 0, first_seen, last_seen)


def link_product(entry, field, adjoint):
    real_rows, imag_rows = [], []
    for a in range(3):
        real_sum = imag_sum = None
        for b in range(3):
            if adjoint:
                u_real, u_imag = entry(0, b, a), entry(1, b, a)
                real_term = u_real * field[b] + u_imag * field[3 + b]
                imag_term = u_real * field[3 + b] - u_imag * field[b]
            else:
                u_real, u_imag = entry(0, a, b), entry(1, a, b)
                real_term = u_real * field[b] - u_imag * field[3 + b]
                imag_term = u_real * field[3 + b] + u_imag * field[b]
            real_sum = real_term if real_sum is None else real_sum + real_term
            imag_sum = imag_term if imag_sum is None else imag_sum + imag_term
        real_rows.append(real_sum)
        imag_rows.append(imag_sum)
    return real_rows + imag_rows


def elemental_kernel(
    norm_factor,
    disp_hbm,
    mom_hbm,
    own_hbm,
    other_hbm,
    own_links_hbm,
    other_links_hbm,
    phi_ref,
    disp_ref,
    mom_ref,
    own_ref,
    other_ref,
    own_links_ref,
    other_links_ref,
    vt_ref,
    links_ref,
    back_ref,
    left_ref,
    right_ref,
    sems,
):
    half_x, ny, nz, eigen = own_ref.shape[1:]
    nx = 2 * half_x
    lanes = nx * nz
    count = len(VALUES)
    side = lax.axis_index("space")
    z_at = lax.broadcasted_iota(jnp.int32, (ROWS, lanes), 1) % nz
    pairs = (
        (disp_hbm, disp_ref),
        (mom_hbm, mom_ref),
        (own_links_hbm, own_links_ref),
        (other_links_hbm, other_links_ref),
        (own_hbm, own_ref),
        (other_hbm, other_ref),
    )
    copies = [pltpu.make_async_copy(s, d, sems.at[k]) for k, (s, d) in enumerate(pairs)]
    for copy in copies:
        copy.start()

    def z_ahead(value):
        return jnp.where(
            z_at[: value.shape[0]] == nz - 1,
            pltpu.roll(value, nz - 1, 1),
            pltpu.roll(value, lanes - 1, 1),
        )

    def z_behind(value):
        return jnp.where(
            z_at[: value.shape[0]] == 0,
            pltpu.roll(value, lanes - (nz - 1), 1),
            pltpu.roll(value, 1, 1),
        )

    copies[0].wait()
    copies[1].wait()
    kinds = 2 * count
    operators = disp_ref.shape[1]
    row = lax.broadcasted_iota(jnp.int32, (kinds, operators), 0)
    at = lax.broadcasted_iota(jnp.int32, (kinds, operators), 1).astype(jnp.float32)
    value = jnp.zeros((kinds, operators), jnp.int32)
    for slot, wanted in enumerate(VALUES):
        value = jnp.where(row // 2 == slot, wanted, value)
    hit = jnp.broadcast_to(disp_ref[...], (kinds, operators)) == value
    first = jnp.min(jnp.where(hit, at, operators), axis=1, keepdims=True)
    last = jnp.max(jnp.where(hit, at, -1.0), axis=1, keepdims=True)
    chosen = at == jnp.where(side == 0, first, last)
    momenta = mom_ref[...].astype(jnp.float32)
    steps = []
    for k, scale in enumerate((nz // nx, nz // ny, 1)):
        spread_out = jnp.broadcast_to(momenta[k : k + 1], (kinds, operators))
        total = jnp.sum(jnp.where(chosen, spread_out, 0.0), axis=1, keepdims=True)
        steps.append(total.astype(jnp.int32) * scale)
    lane = lax.broadcasted_iota(jnp.int32, (kinds, lanes), 1)
    kind = lax.broadcasted_iota(jnp.int32, (kinds, lanes), 0)
    x_true = (lane // nz + half_x * side) % nx
    plane = steps[0] * x_true + steps[2] * (lane % nz) - (kind % 2) * (nz // 4)
    waves = []
    for y in range(ny):
        turns = ((plane + steps[1] * y + nz // 2) & (nz - 1)) - nz // 2
        waves.append(jnp.cos(turns.astype(jnp.float32) * (2.0 * math.pi / nz)).T)

    copies[2].wait()
    copies[3].wait()
    pieces = [own_links_ref[:, x] for x in range(half_x)]
    pieces += [other_links_ref[:, x] for x in range(half_x)]
    links = jnp.concatenate(pieces, axis=-1)
    links_ref[...] = links
    for row in range(18):
        back_ref[row] = pltpu.roll(links[row], nz, 1)
        back_ref[18 + row] = z_behind(links[36 + row])

    copies[4].wait()
    copies[5].wait()

    def lay_out(y):
        field = []
        for c in range(6):
            blocks = [own_ref[c, x, y] for x in range(half_x)]
            blocks += [other_ref[c, x, y] for x in range(half_x)]
            field.append(jnp.concatenate(blocks, axis=0).astype(jnp.float32))
            vt_ref[c, y] = field[c].T
        for slot in range(count):
            cosine = jnp.broadcast_to(waves[y][:, 2 * slot : 2 * slot + 1], (lanes, eigen))
            sine = jnp.broadcast_to(waves[y][:, 2 * slot + 1 : 2 * slot + 2], (lanes, eigen))
            for a in range(3):
                real = field[a] * cosine - field[3 + a] * sine
                imag = field[a] * sine + field[3 + a] * cosine
                base = (y * 6 + 2 * a) * lanes
                left_ref[slot, pl.ds(base, lanes), :] = real.astype(jnp.bfloat16)
                left_ref[slot, pl.ds(base + lanes, lanes), :] = imag.astype(jnp.bfloat16)

    def fields(y):
        y_ahead = (y + 1) % ny
        y_behind = (y + ny - 1) % ny

        def chunk(e):
            rows = pl.ds(pl.multiple_of(e * ROWS, ROWS), ROWS)
            lower = pl.ds(pl.multiple_of(e * ROWS + eigen, ROWS), ROWS)

            def entries(ref, base, at):
                return lambda part, a, b: ref[base + part * 9 + a * 3 + b, pl.ds(at, 1), :]

            def put(value, moved):
                slot = VALUES.index(value)
                for a in range(3):
                    even = pl.ds((y * 6 + 2 * a) * lanes, lanes)
                    odd = pl.ds((y * 6 + 2 * a + 1) * lanes, lanes)
                    real = moved[a].astype(jnp.bfloat16)
                    imag = moved[3 + a].astype(jnp.bfloat16)
                    right_ref[slot, rows, even] = real
                    right_ref[slot, rows, odd] = imag
                    right_ref[slot, lower, even] = imag
                    right_ref[slot, lower, odd] = -real

            field = [vt_ref[c, y, rows, :] for c in range(6)]
            ahead = [pltpu.roll(f, lanes - nz, 1) for f in field]
            moved = link_product(entries(links_ref, 0, y), ahead, False)
            put(1, moved)
            total = moved
            ahead = [vt_ref[c, y_ahead, rows, :] for c in range(6)]
            moved = link_product(entries(links_ref, 18, y), ahead, False)
            put(2, moved)
            total = [p + q for p, q in zip(total, moved)]
            ahead = [z_ahead(f) for f in field]
            moved = link_product(entries(links_ref, 36, y), ahead, False)
            put(3, moved)
            total = [p + q for p, q in zip(total, moved)]
            behind = [pltpu.roll(f, nz, 1) for f in field]
            moved = link_product(entries(back_ref, 0, y), behind, True)
            total = [p + q for p, q in zip(total, moved)]
            behind = [vt_ref[c, y_behind, rows, :] for c in range(6)]
            moved = link_product(entries(links_ref, 18, y_behind), behind, True)
            total = [p + q for p, q in zip(total, moved)]
            behind = [z_behind(f) for f in field]
            moved = link_product(entries(back_ref, 18, y), behind, True)
            total = [p + q for p, q in zip(total, moved)]
            put(0, [f - t * (1.0 / 6.0) for f, t in zip(field, total)])

        lax.fori_loop(0, eigen // ROWS, lambda e, c: (chunk(e), c)[1], 0, unroll=UNROLL)

    for y in range(ny):
        lay_out(y)
    for y in range(ny):
        fields(y)
    for slot in range(count):
        total = jnp.dot(right_ref[slot], left_ref[slot], preferred_element_type=jnp.float32)
        total = (total * norm_factor).astype(jnp.bfloat16)
        phi_ref[slot] = jnp.concatenate([total[:eigen], total[eigen:]], axis=1)


def elementals(norm_factor, displacements, momenta, own, other, own_links, other_links):
    half_x, ny, nz, eigen = own.shape[1:]
    lanes = 2 * half_x * nz
    count = len(VALUES)
    vmem = pl.BlockSpec(memory_space=pltpu.VMEM)
    anywhere = pl.BlockSpec(memory_space=pl.ANY)
    operands = (displacements, momenta, own, other, own_links, other_links)
    return pl.pallas_call(
        functools.partial(elemental_kernel, norm_factor),
        out_shape=jax.ShapeDtypeStruct((count, eigen, 2 * eigen), jnp.bfloat16),
        in_specs=[anywhere] * 6,
        out_specs=vmem,
        scratch_shapes=[pltpu.VMEM(p.shape, p.dtype) for p in operands]
        + [
            pltpu.VMEM((6, ny, eigen, lanes), jnp.float32),
            pltpu.VMEM((54, ny, lanes), jnp.float32),
            pltpu.VMEM((36, ny, lanes), jnp.float32),
            pltpu.VMEM((count, 6 * ny * lanes, eigen), jnp.bfloat16),
            pltpu.VMEM((count, 2 * eigen, 6 * ny * lanes), jnp.bfloat16),
            pltpu.SemaphoreType.DMA((6,)),
        ],
        compiler_params=pltpu.CompilerParams(vmem_limit_bytes=40 * 1024 * 1024),
        cost_estimate=pl.CostEstimate(
            flops=count * 2 * 6 * ny * lanes * eigen * 2 * eigen,
            bytes_accessed=2 * own.size * 2,
            transcendentals=0,
        ),
        name="elementals",
    )(*operands)


def separation(index, ring):
    if not ring:
        return jnp.int32(index)
    count = lax.axis_size("tm")
    me = lax.axis_index("tm")
    place = jnp.where(me % 2 == 0, me // 2, count - (me + 1) // 2)
    hops = (index + 1) // 2 if index % 2 == 1 else -(index // 2)
    at = (place - hops + count) % count
    owner = jnp.where(at < count // 2, 2 * at, 2 * (count - at) - 1)
    return (me - owner + count) % count


def add_to_table(table, product, slot, column):
    total = jnp.sum(jnp.sum(product, axis=0, keepdims=True), axis=1, keepdims=True)
    total = total * (1.0 / product.shape[0])
    row_at = lax.broadcasted_iota(jnp.int32, table.shape, 0)
    column_at = lax.broadcasted_iota(jnp.int32, table.shape, 1)
    return table + jnp.where((row_at == slot) & (column_at == column), total, 0.0)


def sandwich_kernel(made, met, halves, ring, *refs):
    refs = list(refs)
    table_ref = refs.pop(0)
    if made:
        phi_ref, peram_hbm = refs.pop(0), refs.pop(0)
    if met:
        before_ref = refs.pop(0)
        arrival_refs = [refs.pop(0) for _ in range(2 if halves else len(met))]
    table_out = refs.pop(0)
    if made:
        out_ref, peram_ref, mixed_ref, sems = refs
        copies = []
        for k, index in enumerate(made):
            copy = pltpu.make_async_copy(
                peram_hbm.at[separation(index, ring)], peram_ref.at[k], sems.at[k]
            )
            copy.start()
            copies.append(copy)
    table = table_ref[...]
    if met:
        slots, eigen = before_ref.shape[1:3]
        for k, index in enumerate(met):
            column = separation(index, ring)
            for slot in range(slots):
                if halves:
                    rows = arrival_refs[slot // (slots // 2)][slot % (slots // 2)]
                else:
                    rows = arrival_refs[k][slot]
                product = rows.astype(jnp.float32) * before_ref[k, slot]
                table = add_to_table(table, product, slot, column)
    if made:
        slots, eigen, _ = phi_ref.shape
        spins = peram_ref.shape[1]
        blocks = []
        for slot in range(slots):
            rows = phi_ref[slot]
            turned = jnp.concatenate([-rows[:, eigen:], rows[:, :eigen]], axis=1)
            blocks.append(jnp.concatenate([rows, turned], axis=0))
        for k, index in enumerate(made):
            copies[k].wait()
            flipped, weights = [], []
            for a in range(spins):
                peram = peram_ref[k, a]
                real, imag = peram[:, :eigen], peram[:, eigen:]
                flipped.append(jnp.concatenate([real.T, imag.T], axis=1))
                weights.append(jnp.concatenate([real, -imag], axis=1))
                weights.append(jnp.concatenate([imag, real], axis=1))
            flipped = jnp.concatenate(flipped, axis=0)
            weights = jnp.concatenate(weights, axis=0)
            for slot in range(slots):
                mixed = jnp.dot(flipped, blocks[slot], preferred_element_type=jnp.float32)
                mixed = mixed.astype(jnp.bfloat16)
                for a in range(spins):
                    mixed_ref[
                        slot * eigen : (slot + 1) * eigen, 2 * eigen * a : 2 * eigen * (a + 1)
                    ] = mixed[a * eigen : (a + 1) * eigen]
            result = jnp.dot(mixed_ref[...], weights, preferred_element_type=jnp.float32)
            result = result.reshape(slots, eigen, 2 * eigen)
            if index == 0:
                for slot in range(slots):
                    product = phi_ref[slot].astype(jnp.float32) * result[slot]
                    table = add_to_table(table, product, slot, 0)
            else:
                out_ref[k - (made[0] == 0)] = result
    table_out[...] = table


def sandwich_step(table, phi, perambulators, made, before, arrivals, met, ring):
    slots, eigen, columns = phi.shape
    separations, spins = perambulators.shape[:2]
    vmem = pl.BlockSpec(memory_space=pltpu.VMEM)
    halves = len(arrivals) > len(met)
    operands, specs = [table], [vmem]
    shapes, scratch = [jax.ShapeDtypeStruct(table.shape, table.dtype)], []
    if made:
        operands += [phi, perambulators]
        specs += [vmem, pl.BlockSpec(memory_space=pl.ANY)]
        kept = len([k for k in made if k > 0])
        shapes.append(jax.ShapeDtypeStruct((kept, slots, eigen, columns), jnp.float32))
        scratch = [
            pltpu.VMEM((len(made),) + perambulators.shape[1:], perambulators.dtype),
            pltpu.VMEM((slots * eigen, spins * columns), jnp.bfloat16),
            pltpu.SemaphoreType.DMA((len(made),)),
        ]
    if met:
        operands += [before] + list(arrivals)
        specs += [vmem] * (1 + len(arrivals))
    work = 4 * spins * slots * eigen * columns * columns
    return pl.pallas_call(
        functools.partial(sandwich_kernel, tuple(made), tuple(met), halves, ring),
        out_shape=tuple(shapes),
        in_specs=specs,
        out_specs=(vmem,) * len(shapes),
        scratch_shapes=scratch,
        compiler_params=pltpu.CompilerParams(vmem_limit_bytes=24 * 1024 * 1024),
        cost_estimate=pl.CostEstimate(
            flops=len(made) * work + 1000,
            bytes_accessed=len(made) * 2 * spins * eigen * columns + 1000,
            transcendentals=0,
        ),
        name="sandwich" + "".join(str(k) for k in made) + "_meet" + "".join(str(k) for k in met),
    )(*operands)


def turn_kernel(phi_ref, kept_ref, given_ref, whole_ref):
    slots, eigen, _ = phi_ref.shape
    half = eigen // 2
    side = lax.axis_index("space")
    for slot in range(slots):
        rows = phi_ref[slot]
        whole_ref[slot] = jnp.concatenate([rows[:, :eigen].T, rows[:, eigen:].T], axis=1)
    mine = pl.ds(pl.multiple_of(side * half, half), half)
    others = pl.ds(pl.multiple_of((1 - side) * half, half), half)
    kept_ref[...] = whole_ref[:, mine, :]
    given_ref[...] = whole_ref[:, others, :]


def turn(phi):
    slots, eigen, columns = phi.shape
    vmem = pl.BlockSpec(memory_space=pltpu.VMEM)
    half = jax.ShapeDtypeStruct((slots, eigen // 2, columns), phi.dtype)
    return pl.pallas_call(
        turn_kernel,
        out_shape=(half, half),
        in_specs=[vmem],
        out_specs=(vmem, vmem),
        scratch_shapes=[pltpu.VMEM(phi.shape, phi.dtype)],
        cost_estimate=pl.CostEstimate(flops=1000, bytes_accessed=4 * phi.size, transcendentals=0),
        name="turn",
    )(phi)


def order_kernel(source_ref, kept_ref, taken_ref, out_ref):
    slots = kept_ref.shape[0]
    for o in range(out_ref.shape[0]):
        at = source_ref[o]

        @pl.when(at < slots)
        def _(at=at, o=o):
            out_ref[o] = kept_ref[at]

        @pl.when(at >= slots)
        def _(at=at, o=o):
            out_ref[o] = taken_ref[at - slots]


def order(source, kept, taken):
    vmem = pl.BlockSpec(memory_space=pltpu.VMEM)
    shape = (2 * kept.shape[0],) + kept.shape[1:]
    return pl.pallas_call(
        order_kernel,
        out_shape=jax.ShapeDtypeStruct(shape, kept.dtype),
        in_specs=[pl.BlockSpec(memory_space=pltpu.SMEM), vmem, vmem],
        out_specs=vmem,
        cost_estimate=pl.CostEstimate(flops=1000, bytes_accessed=8 * kept.size, transcendentals=0),
        name="order",
    )(source, kept, taken)


def body(vectors, gauge_links, perambulators, momenta, displacements):
    side = lax.axis_index("space")
    swap = [(0, 1), (1, 0)]
    half_x, ny, nz, eigen = vectors.shape[3:]
    own = vectors.reshape((6, half_x, ny, nz, eigen))
    own_links = gauge_links.reshape((54, half_x, ny, nz))
    other = lax.ppermute(own, "space", swap)
    other_links = lax.ppermute(own_links, "space", swap)
    norm_factor = 1.0 / math.sqrt(6.0 * 2 * half_x * ny * nz)
    operators = momenta.shape[0]
    phi = elementals(
        norm_factor, displacements.reshape((1, operators)), momenta.T, own, other, own_links, other_links
    )
    slots = phi.shape[0]

    count = lax.axis_size("tm")
    peram = perambulators[0]
    separations = peram.shape[0]
    ring = count == separations
    if ring:
        around = list(range(0, count, 2)) + list(range(count - 1, 0, -2))
        ahead = [(around[k], around[(k + 1) % count]) for k in range(count)]
        behind = [(b, a) for a, b in ahead]
        one_way = [phi]
        other_way = [phi]
        arrivals = [None]
        for _ in range((separations - 2) // 2):
            one_way.append(lax.ppermute(one_way[-1], "tm", ahead))
            other_way.append(lax.ppermute(other_way[-1], "tm", behind))
            arrivals += [one_way[-1], other_way[-1]]
        last = [
            lax.ppermute(one_way[-1][: slots // 2], "tm", ahead),
            lax.ppermute(other_way[-1][slots // 2 :], "tm", behind),
        ]
    else:
        arrivals = [phi]
        for _ in range(separations - 1):
            arrivals.append(lax.ppermute(arrivals[-1], "tm", [(i, (i + 1) % count) for i in range(count)]))
        last = [arrivals[-1][: slots // 2], arrivals[-1][slots // 2 :]]

    table = jnp.zeros((slots, separations), jnp.float32)
    before, met, came = None, [], []
    for first in range(1, separations, 2):
        made = [k for k in (first, first + 1) if k < separations]
        if first == 1:
            made = [0] + made
        table, sands = sandwich_step(table, phi, peram, made, before, came, met, ring)
        before, met = sands, [k for k in made if k > 0]
        came = last if len(met) == 1 else [arrivals[k] for k in met]
    (table,) = sandwich_step(table, phi, peram, [], before, came, met, ring)
    other_table = lax.ppermute(table, "space", swap)

    number = jnp.arange(operators)
    earlier = (displacements[:, None] == displacements[None, :]) & (number[None, :] < number[:, None])
    mine = jnp.sum(earlier.astype(jnp.int32), axis=1) == side
    slot_of = jnp.zeros((operators,), jnp.int32)
    for slot, value in enumerate(VALUES):
        slot_of = jnp.where(displacements == value, slot, slot_of)
    source = slot_of + jnp.where(mine, 0, slots)
    own_place = (source[:, None] == jnp.arange(slots)[None, :])[:, :, None]
    other_place = (source[:, None] == slots + jnp.arange(slots)[None, :])[:, :, None]
    correlators = jnp.sum(
        jnp.where(own_place, table[None], 0.0) + jnp.where(other_place, other_table[None], 0.0), axis=1
    )
    kept, given = turn(phi)
    taken = lax.ppermute(given, "space", swap)
    rows = order(source, kept, taken)
    return (rows[None], correlators[:, None, :])


def solution(mesh):
    return jax.shard_map(
        body,
        mesh=mesh,
        in_specs=(
            P(("cfg", "tm"), None, None, "space", None, None, None),
            P(("cfg", "tm"), None, None, None, None, "space", None, None),
            P(("cfg", "tm"), None, None, None, None),
            P(),
            P(),
        ),
        out_specs=(P(("cfg", "tm"), None, "space", None), P(None, ("cfg", "tm"), None)),
        check_vma=False,
    )
```

profile of v0, /device:TPU:1, one launch (start us, length us, event | category | flops | bytes accessed | tf_op | source)
XLA Modules:
  0.0 57.5 jit_solution(1884212167943828531)
XLA Ops:
  0.8 0.5 collective-permute-start.1
  1.2 2.1 %collective-permute-done.1.other_links_hbm = f32[54,4,4,16]{3,2,1,0:T(4,128)S(1)} collective-permute-done((f32[54,4,4,16]{3,2,1,0:T(4,128)}, f32[54,4,4,16]{3,2,1,0:T(4,128)S(1)}, u32[]{:S(2)}, u32[]{:S(2)}) %collective-permute-start.1) | collective-permute-done | bytes 55328 | tf_op jit(solution)/shard_map/ppermute | solution.py:435
  3.3 0.7 %copy-done.3 = s32[8]{0:T(128)S(1)} copy-done((s32[8]{0:T(128)S(1)}, s32[8]{0:T(128)}, u32[]{:S(2)}) %copy-start.3) | copy-done | bytes 56
  3.9 1.0 %copy-done.5 = f32[1,3,2,3,3,4,4,16]{7,6,5,4,3,2,1,0:T(4,128)S(1)} copy-done((f32[1,3,2,3,3,4,4,16]{7,6,5,4,3,2,1,0:T(4,128)S(1)}, f32[1,3,2,3,3,4,4,16]{7,6,5,4,3,2,1,0:T(4,128)}, u32[]{:S(2)}) %copy-start.5) | copy-done | bytes 55320
  4.9 1.0 %copy-done.6 = bf16[1,2,3,4,4,16,128]{6,5,4,3,2,1,0:T(8,128)(2,1)S(1)} copy-done((bf16[1,2,3,4,4,16,128]{6,5,4,3,2,1,0:T(8,128)(2,1)S(1)}, bf16[1,2,3,4,4,16,128]{6,5,4,3,2,1,0:T(8,128)(2,1)}, u32[]{:S(2)}) %copy-start.6) | copy-done | bytes 393240
  5.9 0.7 %copy-done.9 = s32[8,3]{0,1:T(4,128)S(1)} copy-done((s32[8,3]{0,1:T(4,128)S(1)}, s32[8,3]{0,1:T(4,128)}, u32[]{:S(2)}) %copy-start.9) | copy-done | bytes 120
  6.6 10.0 %elementals.1.phi_ref.refs_1_ = bf16[4,128,256]{2,1,0:T(8,128)(2,1)S(1)} custom-call(s32[1,8]{1,0:T(1,128)S(1)} %bitcast.13, s32[3,8]{1,0:T(4,128)S(1)} %bitcast.18, bf16[6,4,4,16,128]{4,3,2,1,0:T(8,128)(2,1)S(1)} %bitcast.17, bf16[6,4,4,16,128]{4,3,2,1,0:T(8,128)(2,1)S(1)} %collective-permute-done.other_hbm, f32[54,4,4,16]{3,2,1,0:T(4,128)S(1)} %bitcast.15, ...), custom_call_target="tpu_custom_call" | custom-call | flops 805306368 | bytes 786432 | tf_op jit(solution)/shard_map/elementals/pallas_call | solution.py:225
  16.7 2.5 %collective-permute-start.3 = (bf16[4,128,256]{2,1,0:T(8,128)(2,1)S(1)}, bf16[4,128,256]{2,1,0:T(8,128)(2,1)S(1)}, u32[]{:S(2)}, u32[]{:S(2)}) collective-permute-start(bf16[4,128,256]{2,1,0:T(8,128)(2,1)S(1)} %elementals.1.phi_ref.refs_1_), channel_id=1, source_target_pairs={{0,4},{4,8},{8,12},{12,14},{14,10},{10,6},{6,2},{2,0},{1,5},{5,9},... | collective-permute-start | bytes 786440 | tf_op jit(solution)/shard_map/ppermute | solution.py:455
  19.1 0.2 convert_reduce_fusion
  19.3 6.2 %collective-permute-done.3.refs_4_ = bf16[4,128,256]{2,1,0:T(8,128)(2,1)S(1)} collective-permute-done((bf16[4,128,256]{2,1,0:T(8,128)(2,1)S(1)}, bf16[4,128,256]{2,1,0:T(8,128)(2,1)S(1)}, u32[]{:S(2)}, u32[]{:S(2)}) %collective-permute-start.3) | collective-permute-done | bytes 262176 | tf_op jit(solution)/shard_map/ppermute | solution.py:455
  25.5 1.2 %collective-permute-start.5 = (bf16[4,128,256]{2,1,0:T(8,128)(2,1)S(1)}, bf16[4,128,256]{2,1,0:T(8,128)(2,1)S(1)}, u32[]{:S(2)}, u32[]{:S(2)}) collective-permute-start(bf16[4,128,256]{2,1,0:T(8,128)(2,1)S(1)} %collective-permute-done.3.refs_4_), channel_id=1, source_target_pairs={{0,4},{4,8},{8,12},{12,14},{14,10},{10,6},{6,2},{2,0},{1,5},{5,9},... | collective-permute-start | bytes 786440 | tf_op jit(solution)/shard_map/ppermute | solution.py:455
  26.8 0.7 %copy-done.7 = bf16[4,128,256]{2,1,0:T(8,128)(2,1)} copy-done((bf16[4,128,256]{2,1,0:T(8,128)(2,1)}, bf16[4,128,256]{2,1,0:T(8,128)(2,1)S(1)}, u32[]{:S(2)}) %copy-start.7) | copy-done | bytes 262168
  27.5 0.2 collective-permute-start.6
  27.7 4.8 %collective-permute-done.5.refs_4_ = bf16[4,128,256]{2,1,0:T(8,128)(2,1)S(1)} collective-permute-done((bf16[4,128,256]{2,1,0:T(8,128)(2,1)S(1)}, bf16[4,128,256]{2,1,0:T(8,128)(2,1)S(1)}, u32[]{:S(2)}, u32[]{:S(2)}) %collective-permute-start.5) | collective-permute-done | bytes 262176 | tf_op jit(solution)/shard_map/ppermute | solution.py:455
  32.6 0.9 %collective-permute-start.7 = (bf16[4,128,256]{2,1,0:T(8,128)(2,1)S(1)}, bf16[4,128,256]{2,1,0:T(8,128)(2,1)S(1)}, u32[]{:S(2)}, u32[]{:S(2)}) collective-permute-start(bf16[4,128,256]{2,1,0:T(8,128)(2,1)S(1)} %collective-permute-done.5.refs_4_), channel_id=1, source_target_pairs={{0,4},{4,8},{8,12},{12,14},{14,10},{10,6},{6,2},{2,0},{1,5},{5,9},... | collective-permute-start | bytes 786440 | tf_op jit(solution)/shard_map/ppermute | solution.py:455
  33.5 0.6 %collective-permute-done.6.refs_5_ = bf16[4,128,256]{2,1,0:T(8,128)(2,1)S(1)} collective-permute-done((bf16[4,128,256]{2,1,0:T(8,128)(2,1)}, bf16[4,128,256]{2,1,0:T(8,128)(2,1)S(1)}, u32[]{:S(2)}, u32[]{:S(2)}) %collective-permute-start.6) | collective-permute-done | bytes 262176 | tf_op jit(solution)/shard_map/ppermute | solution.py:456
  34.1 0.6 collective-permute-start.8
  34.8 1.8 %turn.1 = (bf16[4,64,256]{2,1,0:T(8,128)(2,1)}, bf16[4,64,256]{2,1,0:T(8,128)(2,1)}) custom-call(bf16[4,128,256]{2,1,0:T(8,128)(2,1)} %copy-done.1), custom_call_target="tpu_custom_call" | custom-call | flops 1000 | bytes 524288 | tf_op jit(solution)/shard_map/turn/pallas_call | solution.py:390
  36.6 2.2 %collective-permute-start.2 = (bf16[4,64,256]{2,1,0:T(8,128)(2,1)}, bf16[4,64,256]{2,1,0:T(8,128)(2,1)S(1)}, u32[]{:S(2)}, u32[]{:S(2)}) collective-permute-start(bf16[4,64,256]{2,1,0:T(8,128)(2,1)} %get-tuple-element.13), channel_id=1, source_target_pairs={{0,1},{1,0},{2,3},{3,2},{4,5},{5,4},{6,7},{7,6},{8,9},{9,8},{10,11... | collective-permute-start | bytes 393224 | tf_op jit(solution)/shard_map/ppermute | solution.py:493
  38.8 0.9 %copy-done.2 = bf16[4,128,256]{2,1,0:T(8,128)(2,1)S(1)} copy-done((bf16[4,128,256]{2,1,0:T(8,128)(2,1)S(1)}, bf16[4,128,256]{2,1,0:T(8,128)(2,1)}, u32[]{:S(2)}) %copy-start.2) | copy-done | bytes 262168
  39.8 3.7 %sandwich012_meet.1 = (f32[4,8]{1,0:T(4,128)S(1)}, f32[2,4,128,256]{3,2,1,0:T(8,128)S(1)}) custom-call(f32[4,8]{1,0:T(4,128)S(1)} %broadcast_in_dim.75.refs_0_, bf16[4,128,256]{2,1,0:T(8,128)(2,1)S(1)} %copy-done.2, bf16[8,4,128,256]{3,2,1,0:T(8,128)(2,1)S(1)} %bitcast.9), custom_call_target="tpu_custom_call" | custom-call | flops 1610613760 | bytes 787432 | tf_op jit(solution)/shard_map/sandwich012_meet/pallas_call | solution.py:357
  43.5 3.5 %sandwich34_meet12.1 = (f32[4,8]{1,0:T(4,128)S(1)}, f32[2,4,128,256]{3,2,1,0:T(8,128)S(1)}) custom-call(f32[4,8]{1,0:T(4,128)S(1)} %get-tuple-element.14.refs_0_, bf16[4,128,256]{2,1,0:T(8,128)(2,1)S(1)} %copy-done.2, bf16[8,4,128,256]{3,2,1,0:T(8,128)(2,1)S(1)} %bitcast.10, f32[2,4,128,256]{3,2,1,0:T(8,128)S(1)} %get-tuple-element.15.refs_3_, ...), custom_call_target="tpu_custom_call" | custom-call | flops 1073742848 | bytes 525288 | tf_op jit(solution)/shard_map/sandwich34_meet12/pallas_call | solution.py:357
  47.1 1.2 %collective-permute-start.10 = (bf16[2,128,256]{2,1,0:T(8,128)(2,1)S(1)}, bf16[2,128,256]{2,1,0:T(8,128)(2,1)S(1)}, u32[]{:S(2)}, u32[]{:S(2)}) collective-permute-start(bf16[2,128,256]{2,1,0:T(8,128)(2,1)S(1)} %slice.9), channel_id=1, source_target_pairs={{4,0},{8,4},{12,8},{14,12},{10,14},{6,10},{2,6},{0,2},{5,1},{9,5},... | collective-permute-start | bytes 393224 | tf_op jit(solution)/shard_map/ppermute | solution.py:460
  48.3 0.4 collective-permute-start.9
  48.6 2.6 %sandwich56_meet34.1 = (f32[4,8]{1,0:T(4,128)S(1)}, f32[2,4,128,256]{3,2,1,0:T(8,128)S(1)}) custom-call(f32[4,8]{1,0:T(4,128)S(1)} %get-tuple-element.16.refs_0_, bf16[4,128,256]{2,1,0:T(8,128)(2,1)S(1)} %copy-done.2, bf16[8,4,128,256]{3,2,1,0:T(8,128)(2,1)S(1)} %bitcast.11, f32[2,4,128,256]{3,2,1,0:T(8,128)S(1)} %get-tuple-element.17.refs_3_, ...), custom_call_target="tpu_custom_call" | custom-call | flops 1073742848 | bytes 525288 | tf_op jit(solution)/shard_map/sandwich56_meet34/pallas_call | solution.py:357
  51.2 1.4 %sandwich7_meet56.1 = (f32[4,8]{1,0:T(4,128)S(1)}, f32[1,4,128,256]{3,2,1,0:T(8,128)S(1)}) custom-call(f32[4,8]{1,0:T(4,128)S(1)} %get-tuple-element.18.refs_0_, bf16[4,128,256]{2,1,0:T(8,128)(2,1)S(1)} %copy-done.2, bf16[8,4,128,256]{3,2,1,0:T(8,128)(2,1)S(1)} %bitcast.12, f32[2,4,128,256]{3,2,1,0:T(8,128)S(1)} %get-tuple-element.19.refs_3_, ...), custom_call_target="tpu_custom_call" | custom-call | flops 536871936 | bytes 263144 | tf_op jit(solution)/shard_map/sandwich7_meet56/pallas_call | solution.py:357
  52.7 0.4 collective-permute-done.9.refs_2_
  53.1 0.2 sandwich_meet7.1
  53.3 1.1 %collective-permute-start.11 = (f32[4,8]{1,0:T(4,128)S(1)}, f32[4,8]{1,0:T(4,128)S(1)}, u32[]{:S(2)}, u32[]{:S(2)}) collective-permute-start(f32[4,8]{1,0:T(4,128)S(1)} %sandwich_meet7.1), channel_id=1, source_target_pairs={{0,1},{1,0},{2,3},{3,2},{4,5},{5,4},{6,7},{7,6},{8,9},{9,8},{10,11... | collective-permute-start | bytes 392 | tf_op jit(solution)/shard_map/ppermute | solution.py:478
  54.4 0.6 %copy-done.10 = bf16[4,64,256]{2,1,0:T(8,128)(2,1)} copy-done((bf16[4,64,256]{2,1,0:T(8,128)(2,1)}, bf16[4,64,256]{2,1,0:T(8,128)(2,1)S(1)}, u32[]{:S(2)}) %copy-start.10) | copy-done | bytes 131096
  55.1 1.8 %order.1 = bf16[8,64,256]{2,1,0:T(8,128)(2,1)} custom-call(s32[8]{0:T(128)} %copy-done.11, bf16[4,64,256]{2,1,0:T(8,128)(2,1)} %get-tuple-element.12.kept_ref, bf16[4,64,256]{2,1,0:T(8,128)(2,1)} %copy-done.10), custom_call_target="tpu_custom_call" | custom-call | flops 1000 | bytes 524288 | tf_op jit(solution)/shard_map/order/pallas_call | solution.py:418
  56.9 0.7 %add_reduce_fusion = f32[8,8]{1,0:T(8,128)} fusion(f32[4,8]{1,0:T(4,128)S(1)} %collective-permute-done.11, f32[4,8]{1,0:T(4,128)S(1)} %sandwich_meet7.1, pred[8,4]{0,1:T(4,128)(4,1)S(1)} %get-tuple-element.27, pred[8,4]{0,1:T(4,128)(4,1)S(1)} %get-tuple-element.26), kind=kLoop, calls=%fused_computation | loop fusion | flops 960 | bytes 576 | tf_op jit(solution)/shard_map/reduce_sum | solution.py:489
  (32 shorter events, 0.3 us)
Async XLA Ops:
  0.6 38.2 %copy-start = (bf16[1,8,4,128,256]{4,3,2,1,0:T(8,128)(2,1)S(1)}, bf16[1,8,4,128,256]{4,3,2,1,0:T(8,128)(2,1)}, u32[]{:S(2)}) copy-start(bf16[1,8,4,128,256]{4,3,2,1,0:T(8,128)(2,1)} %param.7) | copy-start | bytes 6291460
  0.6 2.6 %collective-permute-start = (bf16[6,4,4,16,128]{4,3,2,1,0:T(8,128)(2,1)}, bf16[6,4,4,16,128]{4,3,2,1,0:T(8,128)(2,1)S(1)}, u32[]{:S(2)}, u32[]{:S(2)}) collective-permute-start(bf16[6,4,4,16,128]{4,3,2,1,0:T(8,128)(2,1)} %bitcast.16), channel_id=1, source_target_pairs={{0,1},{1,0},{2,3},{3,2},{4,5},{5,4},{6,7},{7,6},{8,9},{9,8},{10,11... | collective-permute-start | bytes 1179656 | tf_op jit(solution)/shard_map/ppermute | solution.py:434
  0.8 2.5 %collective-permute-start.1 = (f32[54,4,4,16]{3,2,1,0:T(4,128)}, f32[54,4,4,16]{3,2,1,0:T(4,128)S(1)}, u32[]{:S(2)}, u32[]{:S(2)}) collective-permute-start(f32[54,4,4,16]{3,2,1,0:T(4,128)} %bitcast.14), channel_id=1, source_target_pairs={{0,1},{1,0},{2,3},{3,2},{4,5},{5,4},{6,7},{7,6},{8,9},{9,8},{10,11... | collective-permute-start | bytes 165896 | tf_op jit(solution)/shard_map/ppermute | solution.py:435
  3.3 0.7 %copy-start.3 = (s32[8]{0:T(128)S(1)}, s32[8]{0:T(128)}, u32[]{:S(2)}) copy-start(s32[8]{0:T(128)} %param.9) | copy-start | bytes 100
  3.9 1.0 %copy-start.5 = (f32[1,3,2,3,3,4,4,16]{7,6,5,4,3,2,1,0:T(4,128)S(1)}, f32[1,3,2,3,3,4,4,16]{7,6,5,4,3,2,1,0:T(4,128)}, u32[]{:S(2)}) copy-start(f32[1,3,2,3,3,4,4,16]{7,6,5,4,3,2,1,0:T(4,128)} %param.6) | copy-start | bytes 165892
  4.9 1.0 %copy-start.6 = (bf16[1,2,3,4,4,16,128]{6,5,4,3,2,1,0:T(8,128)(2,1)S(1)}, bf16[1,2,3,4,4,16,128]{6,5,4,3,2,1,0:T(8,128)(2,1)}, u32[]{:S(2)}) copy-start(bf16[1,2,3,4,4,16,128]{6,5,4,3,2,1,0:T(8,128)(2,1)} %param.5) | copy-start | bytes 1179652
  5.9 0.7 %copy-start.9 = (s32[8,3]{0,1:T(4,128)S(1)}, s32[8,3]{0,1:T(4,128)}, u32[]{:S(2)}) copy-start(s32[8,3]{0,1:T(4,128)} %param.8) | copy-start | bytes 292
  6.6 21.1 %copy-start.4 = (s32[8]{0:T(128)S(1)}, s32[8]{0:T(128)}, u32[]{:S(2)}) copy-start(s32[8]{0:T(128)} %param.9) | copy-start | bytes 100
  16.7 18.1 %copy-start.1 = (bf16[4,128,256]{2,1,0:T(8,128)(2,1)}, bf16[4,128,256]{2,1,0:T(8,128)(2,1)S(1)}, u32[]{:S(2)}) copy-start(bf16[4,128,256]{2,1,0:T(8,128)(2,1)S(1)} %elementals.1.phi_ref.refs_1_) | copy-start | bytes 786436
  16.7 8.9 %collective-permute-start.3 = (bf16[4,128,256]{2,1,0:T(8,128)(2,1)S(1)}, bf16[4,128,256]{2,1,0:T(8,128)(2,1)S(1)}, u32[]{:S(2)}, u32[]{:S(2)}) collective-permute-start(bf16[4,128,256]{2,1,0:T(8,128)(2,1)S(1)} %elementals.1.phi_ref.refs_1_), channel_id=1, source_target_pairs={{0,4},{4,8},{8,12},{12,14},{14,10},{10,6},{6,2},{2,0},{1,5},{5,9},... | collective-permute-start | bytes 786440 | tf_op jit(solution)/shard_map/ppermute | solution.py:455
  19.1 8.3 %collective-permute-start.4 = (bf16[4,128,256]{2,1,0:T(8,128)(2,1)S(1)}, bf16[4,128,256]{2,1,0:T(8,128)(2,1)}, u32[]{:S(2)}, u32[]{:S(2)}) collective-permute-start(bf16[4,128,256]{2,1,0:T(8,128)(2,1)S(1)} %elementals.1.phi_ref.refs_1_), channel_id=1, source_target_pairs={{4,0},{8,4},{12,8},{14,12},{10,14},{6,10},{2,6},{0,2},{5,1},{9,5},... | collective-permute-start | bytes 786440 | tf_op jit(solution)/shard_map/ppermute | solution.py:456
  25.5 7.1 %collective-permute-start.5 = (bf16[4,128,256]{2,1,0:T(8,128)(2,1)S(1)}, bf16[4,128,256]{2,1,0:T(8,128)(2,1)S(1)}, u32[]{:S(2)}, u32[]{:S(2)}) collective-permute-start(bf16[4,128,256]{2,1,0:T(8,128)(2,1)S(1)} %collective-permute-done.3.refs_4_), channel_id=1, source_target_pairs={{0,4},{4,8},{8,12},{12,14},{14,10},{10,6},{6,2},{2,0},{1,5},{5,9},... | collective-permute-start | bytes 786440 | tf_op jit(solution)/shard_map/ppermute | solution.py:455
  26.8 0.7 %copy-start.7 = (bf16[4,128,256]{2,1,0:T(8,128)(2,1)}, bf16[4,128,256]{2,1,0:T(8,128)(2,1)S(1)}, u32[]{:S(2)}) copy-start(bf16[4,128,256]{2,1,0:T(8,128)(2,1)S(1)} %collective-permute-done.3.refs_4_) | copy-start | bytes 786436
  27.5 6.6 %collective-permute-start.6 = (bf16[4,128,256]{2,1,0:T(8,128)(2,1)}, bf16[4,128,256]{2,1,0:T(8,128)(2,1)S(1)}, u32[]{:S(2)}, u32[]{:S(2)}) collective-permute-start(bf16[4,128,256]{2,1,0:T(8,128)(2,1)} %collective-permute-done.4.refs_5_), channel_id=1, source_target_pairs={{4,0},{8,4},{12,8},{14,12},{10,14},{6,10},{2,6},{0,2},{5,1},{9,5},... | collective-permute-start | bytes 786440 | tf_op jit(solution)/shard_map/ppermute | solution.py:456
  27.7 15.7 %copy-start.11 = (s32[8]{0:T(128)}, s32[8]{0:T(128)S(1)}, u32[]{:S(2)}) copy-start(s32[8]{0:T(128)S(1)} %fusion.1.source_ref) | copy-start | bytes 100
  32.6 15.7 %collective-permute-start.7 = (bf16[4,128,256]{2,1,0:T(8,128)(2,1)S(1)}, bf16[4,128,256]{2,1,0:T(8,128)(2,1)S(1)}, u32[]{:S(2)}, u32[]{:S(2)}) collective-permute-start(bf16[4,128,256]{2,1,0:T(8,128)(2,1)S(1)} %collective-permute-done.5.refs_4_), channel_id=1, source_target_pairs={{0,4},{4,8},{8,12},{12,14},{14,10},{10,6},{6,2},{2,0},{1,5},{5,9},... | collective-permute-start | bytes 786440 | tf_op jit(solution)/shard_map/ppermute | solution.py:455
  34.1 12.9 %collective-permute-start.8 = (bf16[4,128,256]{2,1,0:T(8,128)(2,1)S(1)}, bf16[4,128,256]{2,1,0:T(8,128)(2,1)S(1)}, u32[]{:S(2)}, u32[]{:S(2)}) collective-permute-start(bf16[4,128,256]{2,1,0:T(8,128)(2,1)S(1)} %collective-permute-done.6.refs_5_), channel_id=1, source_target_pairs={{4,0},{8,4},{12,8},{14,12},{10,14},{6,10},{2,6},{0,2},{5,1},{9,5},... | collective-permute-start | bytes 786440 | tf_op jit(solution)/shard_map/ppermute | solution.py:456
  36.6 17.9 %collective-permute-start.2 = (bf16[4,64,256]{2,1,0:T(8,128)(2,1)}, bf16[4,64,256]{2,1,0:T(8,128)(2,1)S(1)}, u32[]{:S(2)}, u32[]{:S(2)}) collective-permute-start(bf16[4,64,256]{2,1,0:T(8,128)(2,1)} %get-tuple-element.13), channel_id=1, source_target_pairs={{0,1},{1,0},{2,3},{3,2},{4,5},{5,4},{6,7},{7,6},{8,9},{9,8},{10,11... | collective-permute-start | bytes 393224 | tf_op jit(solution)/shard_map/ppermute | solution.py:493
  38.8 1.0 %copy-start.2 = (bf16[4,128,256]{2,1,0:T(8,128)(2,1)S(1)}, bf16[4,128,256]{2,1,0:T(8,128)(2,1)}, u32[]{:S(2)}) copy-start(bf16[4,128,256]{2,1,0:T(8,128)(2,1)} %copy-done.1) | copy-start | bytes 786436
  39.8 3.7 %copy-start.8 = (bf16[4,128,256]{2,1,0:T(8,128)(2,1)S(1)}, bf16[4,128,256]{2,1,0:T(8,128)(2,1)}, u32[]{:S(2)}) copy-start(bf16[4,128,256]{2,1,0:T(8,128)(2,1)} %copy-done.7) | copy-start | bytes 786436
  47.1 5.6 %collective-permute-start.10 = (bf16[2,128,256]{2,1,0:T(8,128)(2,1)S(1)}, bf16[2,128,256]{2,1,0:T(8,128)(2,1)S(1)}, u32[]{:S(2)}, u32[]{:S(2)}) collective-permute-start(bf16[2,128,256]{2,1,0:T(8,128)(2,1)S(1)} %slice.9), channel_id=1, source_target_pairs={{4,0},{8,4},{12,8},{14,12},{10,14},{6,10},{2,6},{0,2},{5,1},{9,5},... | collective-permute-start | bytes 393224 | tf_op jit(solution)/shard_map/ppermute | solution.py:460
  48.3 4.9 %collective-permute-start.9 = (bf16[2,128,256]{2,1,0:T(8,128)(2,1)S(1)}, bf16[2,128,256]{2,1,0:T(8,128)(2,1)S(1)}, u32[]{:S(2)}, u32[]{:S(2)}) collective-permute-start(bf16[2,128,256]{2,1,0:T(8,128)(2,1)S(1)} %slice.8), channel_id=1, source_target_pairs={{0,4},{4,8},{8,12},{12,14},{14,10},{10,6},{6,2},{2,0},{1,5},{5,9},... | collective-permute-start | bytes 393224 | tf_op jit(solution)/shard_map/ppermute | solution.py:459
  53.3 3.6 %collective-permute-start.11 = (f32[4,8]{1,0:T(4,128)S(1)}, f32[4,8]{1,0:T(4,128)S(1)}, u32[]{:S(2)}, u32[]{:S(2)}) collective-permute-start(f32[4,8]{1,0:T(4,128)S(1)} %sandwich_meet7.1), channel_id=1, source_target_pairs={{0,1},{1,0},{2,3},{3,2},{4,5},{5,4},{6,7},{7,6},{8,9},{9,8},{10,11... | collective-permute-start | bytes 392 | tf_op jit(solution)/shard_map/ppermute | solution.py:478
  54.4 0.6 %copy-start.10 = (bf16[4,64,256]{2,1,0:T(8,128)(2,1)}, bf16[4,64,256]{2,1,0:T(8,128)(2,1)S(1)}, u32[]{:S(2)}) copy-start(bf16[4,64,256]{2,1,0:T(8,128)(2,1)S(1)} %collective-permute-done.2.taken_ref) | copy-start | bytes 393220
where the time goes:
time: 57.9 us; the launch traced here: 57.5 us
  Pallas kernels  25 us (43%)
  waiting for transfers between devices  14.2 us (25%)
  starting transfers between devices  10.9 us (19%)
  local copies, waits for them, and re-layouts  5.69 us (10%)
  other arithmetic  0.94 us (2%)
  between operations  0.77 us (1%)
    pallas_call x5, Pallas kernels, sandwich_step(): pl.pallas_call(functools.partial(sandwich_kernel, tuple(made), tuple(met)...  11.4 us
    ppermute x3, waiting for transfers between devices, body(): one_way.append(lax.ppermute(one_way[-1], 'tm', ahead))  11.1 us
    pallas_call x1, Pallas kernels, elementals(): pl.pallas_call(functools.partial(elemental_kernel, norm_factor), out_shap...  10 us
    unnamed x24, local copies, waits for them, and re-layouts  5.67 us
    ppermute x3, starting transfers between devices, body(): one_way.append(lax.ppermute(one_way[-1], 'tm', ahead))  4.56 us
    ppermute x1, starting transfers between devices, body(): taken = lax.ppermute(given, 'space', swap)  2.25 us
    ppermute x1, waiting for transfers between devices, body(): other_links = lax.ppermute(own_links, 'space', swap)  2.06 us
    pallas_call x1, Pallas kernels, turn(): pl.pallas_call(turn_kernel, out_shape=(half, half), in_specs=[vmem], out_...  1.81 us
  transfers between devices with their start and end apart: 12, of which 5 were waited for; matrix products, arithmetic and copies ran while one was open for 0% of the time, Pallas kernels for 26%

commit v1 on v0

--- a/solution.py
+++ b/solution.py
@@ -220,7 +220,7 @@
     lanes = 2 * half_x * nz
     count = len(VALUES)
     vmem = pl.BlockSpec(memory_space=pltpu.VMEM)
-    anywhere = pl.BlockSpec(memory_space=pl.ANY)
+    anywhere = pl.BlockSpec(memory_space=pltpu.HBM)
     operands = (displacements, momenta, own, other, own_links, other_links)
     return pl.pallas_call(
         functools.partial(elemental_kernel, norm_factor),
@@ -236,7 +236,7 @@
             pltpu.VMEM((count, 2 * eigen, 6 * ny * lanes), jnp.bfloat16),
             pltpu.SemaphoreType.DMA((6,)),
         ],
-        compiler_params=pltpu.CompilerParams(vmem_limit_bytes=40 * 1024 * 1024),
+        compiler_params=pltpu.CompilerParams(vmem_limit_bytes=60 * 1024 * 1024),
         cost_estimate=pl.CostEstimate(
             flops=count * 2 * 6 * ny * lanes * eigen * 2 * eigen,
             bytes_accessed=2 * own.size * 2,
@@ -342,7 +342,7 @@
     shapes, scratch = [jax.ShapeDtypeStruct(table.shape, table.dtype)], []
     if made:
         operands += [phi, perambulators]
-        specs += [vmem, pl.BlockSpec(memory_space=pl.ANY)]
+        specs += [vmem, pl.BlockSpec(memory_space=pltpu.HBM)]
         kept = len([k for k in made if k > 0])
         shapes.append(jax.ShapeDtypeStruct((kept, slots, eigen, columns), jnp.float32))
         scratch = [
@@ -425,6 +425,12 @@
     )(source, kept, taken)
 
 
+def ring_pairs(count):
+    around = list(range(0, count, 2)) + list(range(count - 1 - count % 2, 0, -2))
+    ahead = [(around[k], around[(k + 1) % count]) for k in range(count)]
+    return ahead, [(b, a) for a, b in ahead]
+
+
 def body(vectors, gauge_links, perambulators, momenta, displacements):
     side = lax.axis_index("space")
     swap = [(0, 1), (1, 0)]
@@ -444,39 +450,6 @@
     peram = perambulators[0]
     separations = peram.shape[0]
     ring = count == separations
-    if ring:
-        around = list(range(0, count, 2)) + list(range(count - 1, 0, -2))
-        ahead = [(around[k], around[(k + 1) % count]) for k in range(count)]
-        behind = [(b, a) for a, b in ahead]
-        one_way = [phi]
-        other_way = [phi]
-        arrivals = [None]
-        for _ in range((separations - 2) // 2):
-            one_way.append(lax.ppermute(one_way[-1], "tm", ahead))
-            other_way.append(lax.ppermute(other_way[-1], "tm", behind))
-            arrivals += [one_way[-1], other_way[-1]]
-        last = [
-            lax.ppermute(one_way[-1][: slots // 2], "tm", ahead),
-            lax.ppermute(other_way[-1][slots // 2 :], "tm", behind),
-        ]
-    else:
-        arrivals = [phi]
-        for _ in range(separations - 1):
-            arrivals.append(lax.ppermute(arrivals[-1], "tm", [(i, (i + 1) % count) for i in range(count)]))
-        last = [arrivals[-1][: slots // 2], arrivals[-1][slots // 2 :]]
-
-    table = jnp.zeros((slots, separations), jnp.float32)
-    before, met, came = None, [], []
-    for first in range(1, separations, 2):
-        made = [k for k in (first, first + 1) if k < separations]
-        if first == 1:
-            made = [0] + made
-        table, sands = sandwich_step(table, phi, peram, made, before, came, met, ring)
-        before, met = sands, [k for k in made if k > 0]
-        came = last if len(met) == 1 else [arrivals[k] for k in met]
-    (table,) = sandwich_step(table, phi, peram, [], before, came, met, ring)
-    other_table = lax.ppermute(table, "space", swap)
-
     number = jnp.arange(operators)
     earlier = (displacements[:, None] == displacements[None, :]) & (number[None, :] < number[:, None])
     mine = jnp.sum(earlier.astype(jnp.int32), axis=1) == side
@@ -486,12 +459,49 @@
     source = slot_of + jnp.where(mine, 0, slots)
     own_place = (source[:, None] == jnp.arange(slots)[None, :])[:, :, None]
     other_place = (source[:, None] == slots + jnp.arange(slots)[None, :])[:, :, None]
+
+    table = jnp.zeros((slots, separations), jnp.float32)
+    one_way = other_way = phi
+    before, met, came = None, [], []
+    ahead, behind = ring_pairs(count)
+    kept, given = turn(phi)
+    for first in range(1, separations, 2):
+        made = [k for k in (first, first + 1) if k < separations]
+        final = len(made) == 1
+        if ring and final:
+            arrivals = [
+                lax.ppermute(one_way[: slots // 2], "tm", ahead),
+                lax.ppermute(other_way[slots // 2 :], "tm", behind),
+            ]
+        elif ring:
+            one_way = lax.ppermute(one_way, "tm", ahead)
+            other_way = lax.ppermute(other_way, "tm", behind)
+            arrivals = [one_way, other_way]
+        else:
+            arrivals = []
+            for _ in made:
+                one_way = lax.ppermute(one_way, "tm", [(i, (i + 1) % count) for i in range(count)])
+                arrivals.append(one_way)
+            if final:
+                arrivals = [one_way[: slots // 2], one_way[slots // 2 :]]
+        worked = [0] + made if first == 1 else made
+        table, sands = sandwich_step(table, phi, peram, worked, before, came, met, ring)
+        before, met, came = sands, made, arrivals
+        if first == 1:
+            table, kept, given = lax.optimization_barrier((table, kept, given))
+            taken = lax.ppermute(given, "space", swap)
+        if first == 5:
+            rows = order(source, kept, taken)
+            table, rows = lax.optimization_barrier((table, rows))
+        if not final:
+            one_way, other_way, table = lax.optimization_barrier((one_way, other_way, table))
+            came = [one_way, other_way] if ring else arrivals
+    (table,) = sandwich_step(table, phi, peram, [], before, came, met, ring)
+    other_table = lax.ppermute(table, "space", swap)
+
     correlators = jnp.sum(
         jnp.where(own_place, table[None], 0.0) + jnp.where(other_place, other_table[None], 0.0), axis=1
     )
-    kept, given = turn(phi)
-    taken = lax.ppermute(given, "space", swap)
-    rows = order(source, kept, taken)
     return (rows[None], correlators[:, None, :])
 
 

time: 57.9 us -> 51.6 us (0.89)
  waiting for transfers between devices: 14.2 us -> 4.65 us
  starting transfers between devices: 10.9 us -> 12.6 us
  local copies, waits for them, and re-layouts: 5.69 us -> 6.95 us
    ppermute x8, waiting for transfers between devices: 12.2 us -> 1.84 us  [the longest x1 0.93 us: body(): lax.ppermute(one_way[:slots // 2], 'tm', ahead)]
    ppermute x1, starting transfers between devices: 1.14 us -> 2.97 us  [body(): other_table = lax.ppermute(table, 'space', swap)]
    unnamed x24, local copies, waits for them, and re-layouts: 5.67 us -> 6.92 us
    pallas_call x5, Pallas kernels: 11.4 us -> 10.4 us  [sandwich_step(): pl.pallas_call(functools.partial(sandwich_kernel, tuple(made), tuple(met)...]
    ppermute x1, waiting for transfers between devices: 0.01 us -> 0.74 us  [body(): other_table = lax.ppermute(table, 'space', swap)]
    pallas_call x1, Pallas kernels: 10 us -> 10.7 us  [elementals(): pl.pallas_call(functools.partial(elemental_kernel, norm_factor), out_shap...]
  transfers between devices with their start and end apart: 12 -> 12, of which waited for: 5 -> 4; matrix products, arithmetic and copies ran while one was open for 0% -> 2% of each run, Pallas kernels for 26% -> 27%
where the time goes in v1:
time: 51.6 us; the launch traced here: 51.1 us
  Pallas kernels  24.7 us (48%)
  starting transfers between devices  12.6 us (24%)
  local copies, waits for them, and re-layouts  6.95 us (13%)
  waiting for transfers between devices  4.65 us (9%)
  other arithmetic  1.44 us (3%)
  between operations  0.75 us (1%)
    pallas_call x1, Pallas kernels, elementals(): pl.pallas_call(functools.partial(elemental_kernel, norm_factor), out_shap...  10.7 us
    pallas_call x5, Pallas kernels, sandwich_step(): pl.pallas_call(functools.partial(sandwich_kernel, tuple(made), tuple(met)...  10.4 us
    unnamed x24, local copies, waits for them, and re-layouts  6.92 us
    ppermute x3, starting transfers between devices, body(): one_way = lax.ppermute(one_way, 'tm', ahead)  5.09 us
    ppermute x1, starting transfers between devices, body(): other_table = lax.ppermute(table, 'space', swap)  2.97 us
    ppermute x1, waiting for transfers between devices, body(): other_links = lax.ppermute(own_links, 'space', swap)  2.06 us
    ppermute x1, starting transfers between devices, body(): taken = lax.ppermute(given, 'space', swap)  1.9 us
    pallas_call x1, Pallas kernels, turn(): pl.pallas_call(turn_kernel, out_shape=(half, half), in_specs=[vmem], out_...  1.84 us
  transfers between devices with their start and end apart: 12, of which 4 were waited for; matrix products, arithmetic and copies ran while one was open for 2% of the time, Pallas kernels for 27%

profile of v1, /device:TPU:1, one launch (start us, length us, event | category | flops | bytes accessed | tf_op | source)
XLA Modules:
  0.0 51.1 jit_solution(8884794076307043435)
XLA Ops:
  0.8 0.5 collective-permute-start.1
  1.2 2.1 %collective-permute-done.1.other_links_hbm = f32[54,4,4,16]{3,2,1,0:T(4,128)S(1)} collective-permute-done((f32[54,4,4,16]{3,2,1,0:T(4,128)}, f32[54,4,4,16]{3,2,1,0:T(4,128)S(1)}, u32[]{:S(2)}, u32[]{:S(2)}) %collective-permute-start.1) | collective-permute-done | bytes 55328 | tf_op jit(solution)/shard_map/ppermute | solution.py:441
  3.3 0.8 %copy-done.10 = f32[54,4,4,16]{3,2,1,0:T(4,128)} copy-done((f32[54,4,4,16]{3,2,1,0:T(4,128)}, f32[54,4,4,16]{3,2,1,0:T(4,128)S(1)}, u32[]{:S(2)}) %copy-start.10) | copy-done | bytes 55320
  4.2 10.7 %elementals.1.refs_1_.phi_ref = bf16[4,128,256]{2,1,0:T(8,128)(2,1)} custom-call(s32[1,8]{1,0:T(1,128)} %bitcast.15, s32[3,8]{1,0:T(4,128)} %bitcast.20, bf16[6,4,4,16,128]{4,3,2,1,0:T(8,128)(2,1)} %bitcast.19, bf16[6,4,4,16,128]{4,3,2,1,0:T(8,128)(2,1)} %copy-done.11, f32[54,4,4,16]{3,2,1,0:T(4,128)} %bitcast.17, f32[54,4,4,16]{3,2,1,0:T(4,128)} %copy-done.10), custom_call_target="tpu_custom_call" | custom-call | flops 805306368 | bytes 786432 | tf_op jit(solution)/shard_map/elementals/pallas_call | solution.py:225
  14.9 2.5 %collective-permute-start.2 = (bf16[4,128,256]{2,1,0:T(8,128)(2,1)}, bf16[4,128,256]{2,1,0:T(8,128)(2,1)S(1)}, u32[]{:S(2)}, u32[]{:S(2)}) collective-permute-start(bf16[4,128,256]{2,1,0:T(8,128)(2,1)} %elementals.1.refs_1_.phi_ref), channel_id=1, source_target_pairs={{0,4},{4,8},{8,12},{12,14},{14,10},{10,6},{6,2},{2,0},{1,5},{5,9},... | collective-permute-start | bytes 786440 | tf_op jit(solution)/shard_map/ppermute | solution.py:477
  17.3 0.2 collective-permute-start.3
  17.5 1.8 %turn.1 = (bf16[4,64,256]{2,1,0:T(8,128)(2,1)}, bf16[4,64,256]{2,1,0:T(8,128)(2,1)}) custom-call(bf16[4,128,256]{2,1,0:T(8,128)(2,1)} %elementals.1.refs_1_.phi_ref), custom_call_target="tpu_custom_call" | custom-call | flops 1000 | bytes 524288 | tf_op jit(solution)/shard_map/turn/pallas_call | solution.py:390
  19.3 0.9 %copy-done.1 = bf16[4,128,256]{2,1,0:T(8,128)(2,1)S(1)} copy-done((bf16[4,128,256]{2,1,0:T(8,128)(2,1)S(1)}, bf16[4,128,256]{2,1,0:T(8,128)(2,1)}, u32[]{:S(2)}) %copy-start.1) | copy-done | bytes 262168
  20.3 3.7 %sandwich012_meet.1 = (f32[4,8]{1,0:T(4,128)S(1)}, f32[2,4,128,256]{3,2,1,0:T(8,128)S(1)}) custom-call(f32[4,8]{1,0:T(4,128)S(1)} %broadcast_in_dim.67.refs_0_, bf16[4,128,256]{2,1,0:T(8,128)(2,1)S(1)} %copy-done.1, bf16[8,4,128,256]{3,2,1,0:T(8,128)(2,1)S(1)} %bitcast.9), custom_call_target="tpu_custom_call" | custom-call | flops 1610613760 | bytes 787432 | tf_op jit(solution)/shard_map/sandwich012_meet/pallas_call | solution.py:357
  24.0 1.0 %copy-done.5 = f32[2,4,128,256]{3,2,1,0:T(8,128)} copy-done((f32[2,4,128,256]{3,2,1,0:T(8,128)}, f32[2,4,128,256]{3,2,1,0:T(8,128)S(1)}, u32[]{:S(2)}) %copy-start.5) | copy-done | bytes 1048600
  25.0 1.3 %collective-permute-start.4 = (bf16[4,128,256]{2,1,0:T(8,128)(2,1)S(1)}, bf16[4,128,256]{2,1,0:T(8,128)(2,1)S(1)}, u32[]{:S(2)}, u32[]{:S(2)}) collective-permute-start(bf16[4,128,256]{2,1,0:T(8,128)(2,1)S(1)} %collective-permute-done.2.refs_4_), channel_id=1, source_target_pairs={{0,4},{4,8},{8,12},{12,14},{14,10},{10,6},{6,2},{2,0},{1,5},{5,9},... | collective-permute-start | bytes 786440 | tf_op jit(solution)/shard_map/ppermute | solution.py:477
  26.3 0.2 collective-permute-start.5
  26.4 0.2 convert_reduce_fusion
  26.6 1.9 %collective-permute-start.6 = (bf16[4,64,256]{2,1,0:T(8,128)(2,1)}, bf16[4,64,256]{2,1,0:T(8,128)(2,1)S(1)}, u32[]{:S(2)}, u32[]{:S(2)}) collective-permute-start(bf16[4,64,256]{2,1,0:T(8,128)(2,1)} %get-tuple-element.41), channel_id=1, source_target_pairs={{0,1},{1,0},{2,3},{3,2},{4,5},{5,4},{6,7},{7,6},{8,9},{9,8},{10,11... | collective-permute-start | bytes 393224 | tf_op jit(solution)/shard_map/ppermute | solution.py:492
  28.5 1.2 %copy-done.6 = f32[2,4,128,256]{3,2,1,0:T(8,128)S(1)} copy-done((f32[2,4,128,256]{3,2,1,0:T(8,128)S(1)}, f32[2,4,128,256]{3,2,1,0:T(8,128)}, u32[]{:S(2)}) %copy-start.6) | copy-done | bytes 1048600
  29.8 2.6 %sandwich34_meet12.1 = (f32[4,8]{1,0:T(4,128)S(1)}, f32[2,4,128,256]{3,2,1,0:T(8,128)S(1)}) custom-call(f32[4,8]{1,0:T(4,128)S(1)} %get-tuple-element.32.refs_0_, bf16[4,128,256]{2,1,0:T(8,128)(2,1)S(1)} %copy-done.2, bf16[8,4,128,256]{3,2,1,0:T(8,128)(2,1)S(1)} %bitcast.10, f32[2,4,128,256]{3,2,1,0:T(8,128)S(1)} %copy-done.6, ...), custom_call_target="tpu_custom_call" | custom-call | flops 1073742848 | bytes 525288 | tf_op jit(solution)/shard_map/sandwich34_meet12/pallas_call | solution.py:357
  32.4 1.0 %copy-done.3 = f32[2,4,128,256]{3,2,1,0:T(8,128)} copy-done((f32[2,4,128,256]{3,2,1,0:T(8,128)}, f32[2,4,128,256]{3,2,1,0:T(8,128)S(1)}, u32[]{:S(2)}) %copy-start.3) | copy-done | bytes 1048600
  33.4 1.3 %collective-permute-start.7 = (bf16[4,128,256]{2,1,0:T(8,128)(2,1)S(1)}, bf16[4,128,256]{2,1,0:T(8,128)(2,1)S(1)}, u32[]{:S(2)}, u32[]{:S(2)}) collective-permute-start(bf16[4,128,256]{2,1,0:T(8,128)(2,1)S(1)} %collective-permute-done.4.refs_4_), channel_id=1, source_target_pairs={{0,4},{4,8},{8,12},{12,14},{14,10},{10,6},{6,2},{2,0},{1,5},{5,9},... | collective-permute-start | bytes 786440 | tf_op jit(solution)/shard_map/ppermute | solution.py:477
  34.7 0.2 collective-permute-start.8
  34.8 0.5 %fusion.1.source_ref = s32[8]{0:T(128)} fusion(s32[8]{0:T(128)S(1)} %copy-done.9, s32[8]{0:T(128)S(1)} %convert_reduce_fusion, s32[]{:T(128)S(6)} %axis_index.12), kind=kLoop, calls=%fused_computation.10 | loop fusion | flops 72 | bytes 100 | tf_op jit(solution)/shard_map/add | solution.py:459
  35.3 0.6 %copy-done.7 = bf16[4,64,256]{2,1,0:T(8,128)(2,1)} copy-done((bf16[4,64,256]{2,1,0:T(8,128)(2,1)}, bf16[4,64,256]{2,1,0:T(8,128)(2,1)S(1)}, u32[]{:S(2)}) %copy-start.7) | copy-done | bytes 131096
  36.0 1.8 %order.1 = bf16[8,64,256]{2,1,0:T(8,128)(2,1)} custom-call(s32[8]{0:T(128)} %fusion.1.source_ref, bf16[4,64,256]{2,1,0:T(8,128)(2,1)} %get-tuple-element.40.kept_ref, bf16[4,64,256]{2,1,0:T(8,128)(2,1)} %copy-done.7), custom_call_target="tpu_custom_call" | custom-call | flops 1000 | bytes 524288 | tf_op jit(solution)/shard_map/order/pallas_call | solution.py:418
  37.8 1.2 %copy-done.4 = f32[2,4,128,256]{3,2,1,0:T(8,128)S(1)} copy-done((f32[2,4,128,256]{3,2,1,0:T(8,128)S(1)}, f32[2,4,128,256]{3,2,1,0:T(8,128)}, u32[]{:S(2)}) %copy-start.4) | copy-done | bytes 1048600
  39.0 2.6 %sandwich56_meet34.1 = (f32[4,8]{1,0:T(4,128)S(1)}, f32[2,4,128,256]{3,2,1,0:T(8,128)S(1)}) custom-call(f32[4,8]{1,0:T(4,128)S(1)} %get-tuple-element.35.refs_0_, bf16[4,128,256]{2,1,0:T(8,128)(2,1)S(1)} %copy-done.2, bf16[8,4,128,256]{3,2,1,0:T(8,128)(2,1)S(1)} %bitcast.11, f32[2,4,128,256]{3,2,1,0:T(8,128)S(1)} %copy-done.4, ...), custom_call_target="tpu_custom_call" | custom-call | flops 1073742848 | bytes 525288 | tf_op jit(solution)/shard_map/sandwich56_meet34/pallas_call | solution.py:357
  41.6 0.9 %collective-permute-start.10 = (bf16[2,128,256]{2,1,0:T(8,128)(2,1)S(1)}, bf16[2,128,256]{2,1,0:T(8,128)(2,1)S(1)}, u32[]{:S(2)}, u32[]{:S(2)}) collective-permute-start(bf16[2,128,256]{2,1,0:T(8,128)(2,1)S(1)} %slice.7), channel_id=1, source_target_pairs={{4,0},{8,4},{12,8},{14,12},{10,14},{6,10},{2,6},{0,2},{5,1},{9,5},... | collective-permute-start | bytes 393224 | tf_op jit(solution)/shard_map/ppermute | solution.py:474
  42.6 0.7 %collective-permute-start.9 = (bf16[2,128,256]{2,1,0:T(8,128)(2,1)S(1)}, bf16[2,128,256]{2,1,0:T(8,128)(2,1)S(1)}, u32[]{:S(2)}, u32[]{:S(2)}) collective-permute-start(bf16[2,128,256]{2,1,0:T(8,128)(2,1)S(1)} %slice.6), channel_id=1, source_target_pairs={{0,4},{4,8},{8,12},{12,14},{14,10},{10,6},{6,2},{2,0},{1,5},{5,9},... | collective-permute-start | bytes 393224 | tf_op jit(solution)/shard_map/ppermute | solution.py:473
  43.2 1.4 %sandwich7_meet56.1 = (f32[4,8]{1,0:T(4,128)S(1)}, f32[1,4,128,256]{3,2,1,0:T(8,128)S(1)}) custom-call(f32[4,8]{1,0:T(4,128)S(1)} %get-tuple-element.44.refs_0_, bf16[4,128,256]{2,1,0:T(8,128)(2,1)S(1)} %copy-done.2, bf16[8,4,128,256]{3,2,1,0:T(8,128)(2,1)S(1)} %bitcast.12, f32[2,4,128,256]{3,2,1,0:T(8,128)S(1)} %get-tuple-element.45.refs_3_, ...), custom_call_target="tpu_custom_call" | custom-call | flops 536871936 | bytes 263144 | tf_op jit(solution)/shard_map/sandwich7_meet56/pallas_call | solution.py:357
  44.6 0.9 %collective-permute-done.10.refs_3_ = bf16[2,128,256]{2,1,0:T(8,128)(2,1)S(1)} collective-permute-done((bf16[2,128,256]{2,1,0:T(8,128)(2,1)S(1)}, bf16[2,128,256]{2,1,0:T(8,128)(2,1)S(1)}, u32[]{:S(2)}, u32[]{:S(2)}) %collective-permute-start.10) | collective-permute-done | bytes 131104 | tf_op jit(solution)/shard_map/ppermute | solution.py:474
  45.5 0.9 %collective-permute-done.9.refs_2_ = bf16[2,128,256]{2,1,0:T(8,128)(2,1)S(1)} collective-permute-done((bf16[2,128,256]{2,1,0:T(8,128)(2,1)S(1)}, bf16[2,128,256]{2,1,0:T(8,128)(2,1)S(1)}, u32[]{:S(2)}, u32[]{:S(2)}) %collective-permute-start.9) | collective-permute-done | bytes 131104 | tf_op jit(solution)/shard_map/ppermute | solution.py:473
  46.6 3.0 %collective-permute-start.11 = (f32[4,8]{1,0:T(4,128)S(1)}, f32[4,8]{1,0:T(4,128)S(1)}, u32[]{:S(2)}, u32[]{:S(2)}) collective-permute-start(f32[4,8]{1,0:T(4,128)S(1)} %sandwich_meet7.1), channel_id=1, source_target_pairs={{0,1},{1,0},{2,3},{3,2},{4,5},{5,4},{6,7},{7,6},{8,9},{9,8},{10,11... | collective-permute-start | bytes 392 | tf_op jit(solution)/shard_map/ppermute | solution.py:500
  49.6 0.7 %collective-permute-done.11 = f32[4,8]{1,0:T(4,128)S(1)} collective-permute-done((f32[4,8]{1,0:T(4,128)S(1)}, f32[4,8]{1,0:T(4,128)S(1)}, u32[]{:S(2)}, u32[]{:S(2)}) %collective-permute-start.11) | collective-permute-done | bytes 160 | tf_op jit(solution)/shard_map/ppermute | solution.py:500
  50.4 0.7 %add_reduce_fusion = f32[8,8]{1,0:T(8,128)} fusion(f32[4,8]{1,0:T(4,128)S(1)} %collective-permute-done.11, f32[4,8]{1,0:T(4,128)S(1)} %sandwich_meet7.1, pred[8,4]{0,1:T(4,128)(4,1)S(1)} %get-tuple-element.55, pred[8,4]{0,1:T(4,128)(4,1)S(1)} %get-tuple-element.54), kind=kLoop, calls=%fused_computation | loop fusion | flops 960 | bytes 576 | tf_op jit(solution)/shard_map/reduce_sum | solution.py:502
  (32 shorter events, 0.6 us)
Async XLA Ops:
  0.6 18.7 %copy-start = (bf16[1,8,4,128,256]{4,3,2,1,0:T(8,128)(2,1)S(1)}, bf16[1,8,4,128,256]{4,3,2,1,0:T(8,128)(2,1)}, u32[]{:S(2)}) copy-start(bf16[1,8,4,128,256]{4,3,2,1,0:T(8,128)(2,1)} %param.7) | copy-start | bytes 6291460
  0.6 2.6 %collective-permute-start = (bf16[6,4,4,16,128]{4,3,2,1,0:T(8,128)(2,1)}, bf16[6,4,4,16,128]{4,3,2,1,0:T(8,128)(2,1)S(1)}, u32[]{:S(2)}, u32[]{:S(2)}) collective-permute-start(bf16[6,4,4,16,128]{4,3,2,1,0:T(8,128)(2,1)} %bitcast.18), channel_id=1, source_target_pairs={{0,1},{1,0},{2,3},{3,2},{4,5},{5,4},{6,7},{7,6},{8,9},{9,8},{10,11... | collective-permute-start | bytes 1179656 | tf_op jit(solution)/shard_map/ppermute | solution.py:440
  0.8 2.5 %collective-permute-start.1 = (f32[54,4,4,16]{3,2,1,0:T(4,128)}, f32[54,4,4,16]{3,2,1,0:T(4,128)S(1)}, u32[]{:S(2)}, u32[]{:S(2)}) collective-permute-start(f32[54,4,4,16]{3,2,1,0:T(4,128)} %bitcast.16), channel_id=1, source_target_pairs={{0,1},{1,0},{2,3},{3,2},{4,5},{5,4},{6,7},{7,6},{8,9},{9,8},{10,11... | collective-permute-start | bytes 165896 | tf_op jit(solution)/shard_map/ppermute | solution.py:441
  3.3 0.8 %copy-start.10 = (f32[54,4,4,16]{3,2,1,0:T(4,128)}, f32[54,4,4,16]{3,2,1,0:T(4,128)S(1)}, u32[]{:S(2)}) copy-start(f32[54,4,4,16]{3,2,1,0:T(4,128)S(1)} %collective-permute-done.1.other_links_hbm) | copy-start | bytes 165892
  3.3 0.9 %copy-start.11 = (bf16[6,4,4,16,128]{4,3,2,1,0:T(8,128)(2,1)}, bf16[6,4,4,16,128]{4,3,2,1,0:T(8,128)(2,1)S(1)}, u32[]{:S(2)}) copy-start(bf16[6,4,4,16,128]{4,3,2,1,0:T(8,128)(2,1)S(1)} %collective-permute-done.other_hbm) | copy-start | bytes 1179652
  14.9 10.1 %collective-permute-start.2 = (bf16[4,128,256]{2,1,0:T(8,128)(2,1)}, bf16[4,128,256]{2,1,0:T(8,128)(2,1)S(1)}, u32[]{:S(2)}, u32[]{:S(2)}) collective-permute-start(bf16[4,128,256]{2,1,0:T(8,128)(2,1)} %elementals.1.refs_1_.phi_ref), channel_id=1, source_target_pairs={{0,4},{4,8},{8,12},{12,14},{14,10},{10,6},{6,2},{2,0},{1,5},{5,9},... | collective-permute-start | bytes 786440 | tf_op jit(solution)/shard_map/ppermute | solution.py:477
  17.3 7.7 %collective-permute-start.3 = (bf16[4,128,256]{2,1,0:T(8,128)(2,1)}, bf16[4,128,256]{2,1,0:T(8,128)(2,1)S(1)}, u32[]{:S(2)}, u32[]{:S(2)}) collective-permute-start(bf16[4,128,256]{2,1,0:T(8,128)(2,1)} %elementals.1.refs_1_.phi_ref), channel_id=1, source_target_pairs={{4,0},{8,4},{12,8},{14,12},{10,14},{6,10},{2,6},{0,2},{5,1},{9,5},... | collective-permute-start | bytes 786440 | tf_op jit(solution)/shard_map/ppermute | solution.py:478
  19.3 1.0 %copy-start.1 = (bf16[4,128,256]{2,1,0:T(8,128)(2,1)S(1)}, bf16[4,128,256]{2,1,0:T(8,128)(2,1)}, u32[]{:S(2)}) copy-start(bf16[4,128,256]{2,1,0:T(8,128)(2,1)} %elementals.1.refs_1_.phi_ref) | copy-start | bytes 786436
  20.3 6.2 %copy-start.9 = (s32[8]{0:T(128)S(1)}, s32[8]{0:T(128)}, u32[]{:S(2)}) copy-start(s32[8]{0:T(128)} %param.9) | copy-start | bytes 100
  20.3 8.2 %copy-start.2 = (bf16[4,128,256]{2,1,0:T(8,128)(2,1)S(1)}, bf16[4,128,256]{2,1,0:T(8,128)(2,1)}, u32[]{:S(2)}) copy-start(bf16[4,128,256]{2,1,0:T(8,128)(2,1)} %elementals.1.refs_1_.phi_ref) | copy-start | bytes 786436
  24.0 1.0 %copy-start.5 = (f32[2,4,128,256]{3,2,1,0:T(8,128)}, f32[2,4,128,256]{3,2,1,0:T(8,128)S(1)}, u32[]{:S(2)}) copy-start(f32[2,4,128,256]{3,2,1,0:T(8,128)S(1)} %get-tuple-element.33.refs_3_) | copy-start | bytes 3145732
  25.0 8.4 %collective-permute-start.4 = (bf16[4,128,256]{2,1,0:T(8,128)(2,1)S(1)}, bf16[4,128,256]{2,1,0:T(8,128)(2,1)S(1)}, u32[]{:S(2)}, u32[]{:S(2)}) collective-permute-start(bf16[4,128,256]{2,1,0:T(8,128)(2,1)S(1)} %collective-permute-done.2.refs_4_), channel_id=1, source_target_pairs={{0,4},{4,8},{8,12},{12,14},{14,10},{10,6},{6,2},{2,0},{1,5},{5,9},... | collective-permute-start | bytes 786440 | tf_op jit(solution)/shard_map/ppermute | solution.py:477
  26.3 7.1 %collective-permute-start.5 = (bf16[4,128,256]{2,1,0:T(8,128)(2,1)S(1)}, bf16[4,128,256]{2,1,0:T(8,128)(2,1)S(1)}, u32[]{:S(2)}, u32[]{:S(2)}) collective-permute-start(bf16[4,128,256]{2,1,0:T(8,128)(2,1)S(1)} %collective-permute-done.3.refs_5_), channel_id=1, source_target_pairs={{4,0},{8,4},{12,8},{14,12},{10,14},{6,10},{2,6},{0,2},{5,1},{9,5},... | collective-permute-start | bytes 786440 | tf_op jit(solution)/shard_map/ppermute | solution.py:478
  26.6 8.7 %collective-permute-start.6 = (bf16[4,64,256]{2,1,0:T(8,128)(2,1)}, bf16[4,64,256]{2,1,0:T(8,128)(2,1)S(1)}, u32[]{:S(2)}, u32[]{:S(2)}) collective-permute-start(bf16[4,64,256]{2,1,0:T(8,128)(2,1)} %get-tuple-element.41), channel_id=1, source_target_pairs={{0,1},{1,0},{2,3},{3,2},{4,5},{5,4},{6,7},{7,6},{8,9},{9,8},{10,11... | collective-permute-start | bytes 393224 | tf_op jit(solution)/shard_map/ppermute | solution.py:492
  28.5 1.2 %copy-start.6 = (f32[2,4,128,256]{3,2,1,0:T(8,128)S(1)}, f32[2,4,128,256]{3,2,1,0:T(8,128)}, u32[]{:S(2)}) copy-start(f32[2,4,128,256]{3,2,1,0:T(8,128)} %copy-done.5) | copy-start | bytes 3145732
  32.4 1.0 %copy-start.3 = (f32[2,4,128,256]{3,2,1,0:T(8,128)}, f32[2,4,128,256]{3,2,1,0:T(8,128)S(1)}, u32[]{:S(2)}) copy-start(f32[2,4,128,256]{3,2,1,0:T(8,128)S(1)} %get-tuple-element.36.refs_3_) | copy-start | bytes 3145732
  33.4 8.3 %collective-permute-start.7 = (bf16[4,128,256]{2,1,0:T(8,128)(2,1)S(1)}, bf16[4,128,256]{2,1,0:T(8,128)(2,1)S(1)}, u32[]{:S(2)}, u32[]{:S(2)}) collective-permute-start(bf16[4,128,256]{2,1,0:T(8,128)(2,1)S(1)} %collective-permute-done.4.refs_4_), channel_id=1, source_target_pairs={{0,4},{4,8},{8,12},{12,14},{14,10},{10,6},{6,2},{2,0},{1,5},{5,9},... | collective-permute-start | bytes 786440 | tf_op jit(solution)/shard_map/ppermute | solution.py:477
  34.7 7.0 %collective-permute-start.8 = (bf16[4,128,256]{2,1,0:T(8,128)(2,1)S(1)}, bf16[4,128,256]{2,1,0:T(8,128)(2,1)S(1)}, u32[]{:S(2)}, u32[]{:S(2)}) collective-permute-start(bf16[4,128,256]{2,1,0:T(8,128)(2,1)S(1)} %collective-permute-done.5.refs_5_), channel_id=1, source_target_pairs={{4,0},{8,4},{12,8},{14,12},{10,14},{6,10},{2,6},{0,2},{5,1},{9,5},... | collective-permute-start | bytes 786440 | tf_op jit(solution)/shard_map/ppermute | solution.py:478
  35.3 0.6 %copy-start.7 = (bf16[4,64,256]{2,1,0:T(8,128)(2,1)}, bf16[4,64,256]{2,1,0:T(8,128)(2,1)S(1)}, u32[]{:S(2)}) copy-start(bf16[4,64,256]{2,1,0:T(8,128)(2,1)S(1)} %collective-permute-done.6.taken_ref) | copy-start | bytes 393220
  37.8 1.2 %copy-start.4 = (f32[2,4,128,256]{3,2,1,0:T(8,128)S(1)}, f32[2,4,128,256]{3,2,1,0:T(8,128)}, u32[]{:S(2)}) copy-start(f32[2,4,128,256]{3,2,1,0:T(8,128)} %copy-done.3) | copy-start | bytes 3145732
  41.6 3.9 %collective-permute-start.10 = (bf16[2,128,256]{2,1,0:T(8,128)(2,1)S(1)}, bf16[2,128,256]{2,1,0:T(8,128)(2,1)S(1)}, u32[]{:S(2)}, u32[]{:S(2)}) collective-permute-start(bf16[2,128,256]{2,1,0:T(8,128)(2,1)S(1)} %slice.7), channel_id=1, source_target_pairs={{4,0},{8,4},{12,8},{14,12},{10,14},{6,10},{2,6},{0,2},{5,1},{9,5},... | collective-permute-start | bytes 393224 | tf_op jit(solution)/shard_map/ppermute | solution.py:474
  42.6 3.9 %collective-permute-start.9 = (bf16[2,128,256]{2,1,0:T(8,128)(2,1)S(1)}, bf16[2,128,256]{2,1,0:T(8,128)(2,1)S(1)}, u32[]{:S(2)}, u32[]{:S(2)}) collective-permute-start(bf16[2,128,256]{2,1,0:T(8,128)(2,1)S(1)} %slice.6), channel_id=1, source_target_pairs={{0,4},{4,8},{8,12},{12,14},{14,10},{10,6},{6,2},{2,0},{1,5},{5,9},... | collective-permute-start | bytes 393224 | tf_op jit(solution)/shard_map/ppermute | solution.py:473
  43.2 6.3 %copy-start.8 = (s32[8]{0:T(128)S(1)}, s32[8]{0:T(128)}, u32[]{:S(2)}) copy-start(s32[8]{0:T(128)} %fusion.1.source_ref) | copy-start | bytes 100
  46.6 3.8 %collective-permute-start.11 = (f32[4,8]{1,0:T(4,128)S(1)}, f32[4,8]{1,0:T(4,128)S(1)}, u32[]{:S(2)}, u32[]{:S(2)}) collective-permute-start(f32[4,8]{1,0:T(4,128)S(1)} %sandwich_meet7.1), channel_id=1, source_target_pairs={{0,1},{1,0},{2,3},{3,2},{4,5},{5,4},{6,7},{7,6},{8,9},{9,8},{10,11... | collective-permute-start | bytes 392 | tf_op jit(solution)/shard_map/ppermute | solution.py:500

commit v2 on v1

--- a/solution.py
+++ b/solution.py
@@ -236,7 +236,7 @@
             pltpu.VMEM((count, 2 * eigen, 6 * ny * lanes), jnp.bfloat16),
             pltpu.SemaphoreType.DMA((6,)),
         ],
-        compiler_params=pltpu.CompilerParams(vmem_limit_bytes=60 * 1024 * 1024),
+        compiler_params=pltpu.CompilerParams(vmem_limit_bytes=65000 * 1024),
         cost_estimate=pl.CostEstimate(
             flops=count * 2 * 6 * ny * lanes * eigen * 2 * eigen,
             bytes_accessed=2 * own.size * 2,
@@ -246,16 +246,24 @@
     )(*operands)
 
 
+def slice_behind(hops):
+    count = lax.axis_size("tm")
+    me = lax.axis_index("tm")
+    place = jnp.where(me % 2 == 0, me // 2, count - (me + 1) // 2)
+    at = (place - hops + count) % count
+    return jnp.where(at < count // 2, 2 * at, 2 * (count - at) - 1)
+
+
+def apart(sink, source):
+    count = lax.axis_size("tm")
+    return (sink - source + count) % count
+
+
 def separation(index, ring):
     if not ring:
         return jnp.int32(index)
-    count = lax.axis_size("tm")
-    me = lax.axis_index("tm")
-    place = jnp.where(me % 2 == 0, me // 2, count - (me + 1) // 2)
     hops = (index + 1) // 2 if index % 2 == 1 else -(index // 2)
-    at = (place - hops + count) % count
-    owner = jnp.where(at < count // 2, 2 * at, 2 * (count - at) - 1)
-    return (me - owner + count) % count
+    return apart(lax.axis_index("tm"), slice_behind(hops))
 
 
 def add_to_table(table, product, slot, column):
@@ -266,14 +274,86 @@
     return table + jnp.where((row_at == slot) & (column_at == column), total, 0.0)
 
 
-def sandwich_kernel(made, met, halves, ring, *refs):
+def elemental_blocks(phi_ref):
+    slots, eigen, _ = phi_ref.shape
+    blocks = []
+    for slot in range(slots):
+        rows = phi_ref[slot]
+        turned = jnp.concatenate([-rows[:, eigen:], rows[:, :eigen]], axis=1)
+        blocks.append(jnp.concatenate([rows, turned], axis=0))
+    return blocks
+
+
+def sandwich_block(blocks, perams, mixed_ref):
+    spins, eigen = len(perams), perams[0].shape[0]
+    flipped, weights = [], []
+    for peram in perams:
+        real, imag = peram[:, :eigen], peram[:, eigen:]
+        flipped.append(jnp.concatenate([real.T, imag.T], axis=1))
+        weights.append(jnp.concatenate([real, -imag], axis=1))
+        weights.append(jnp.concatenate([imag, real], axis=1))
+    flipped = jnp.concatenate(flipped, axis=0)
+    weights = jnp.concatenate(weights, axis=0)
+    for slot, block in enumerate(blocks):
+        mixed = jnp.dot(flipped, block, preferred_element_type=jnp.float32)
+        mixed = mixed.astype(jnp.bfloat16)
+        for a in range(spins):
+            mixed_ref[
+                slot * eigen : (slot + 1) * eigen, 2 * eigen * a : 2 * eigen * (a + 1)
+            ] = mixed[a * eigen : (a + 1) * eigen]
+    result = jnp.dot(
+        mixed_ref[:, : 2 * eigen * spins], weights, preferred_element_type=jnp.float32
+    )
+    return result.reshape(len(blocks), eigen, 2 * eigen)
+
+
+def far_kernel(behind_ref, ahead_ref, first_ref, second_ref, back_out, on_out, mixed_ref):
+    count = lax.axis_size("tm")
+    behind = slice_behind(count // 4)
+    ahead = slice_behind(-(count // 4))
+    for sink_ref, source_ref, peram_ref, out, column in (
+        (behind_ref, ahead_ref, first_ref, back_out, apart(behind, ahead)),
+        (ahead_ref, behind_ref, second_ref, on_out, apart(ahead, behind)),
+    ):
+        perams = [peram_ref[a] for a in range(peram_ref.shape[0])]
+        result = sandwich_block(elemental_blocks(sink_ref), perams, mixed_ref)
+        table = jnp.zeros(out.shape, jnp.float32)
+        for slot in range(sink_ref.shape[0]):
+            product = source_ref[slot].astype(jnp.float32) * result[slot]
+            table = add_to_table(table, product, slot, column)
+        out[...] = table
+
+
+def far(behind, ahead, first, second, separations):
+    slots, eigen, columns = behind.shape
+    spins = first.shape[0]
+    vmem = pl.BlockSpec(memory_space=pltpu.VMEM)
+    table = jax.ShapeDtypeStruct((slots, separations), jnp.float32)
+    return pl.pallas_call(
+        far_kernel,
+        out_shape=(table, table),
+        in_specs=[vmem] * 4,
+        out_specs=(vmem, vmem),
+        scratch_shapes=[pltpu.VMEM((slots * eigen, spins * columns), jnp.bfloat16)],
+        compiler_params=pltpu.CompilerParams(vmem_limit_bytes=16 * 1024 * 1024),
+        cost_estimate=pl.CostEstimate(
+            flops=8 * spins * slots * eigen * columns * columns,
+            bytes_accessed=4 * behind.size,
+            transcendentals=0,
+        ),
+        name="far",
+    )(behind, ahead, first, second)
+
+
+def sandwich_kernel(made, met, ring, extra, *refs):
     refs = list(refs)
     table_ref = refs.pop(0)
+    extra_refs = [refs.pop(0) for _ in range(extra)]
     if made:
         phi_ref, peram_hbm = refs.pop(0), refs.pop(0)
     if met:
         before_ref = refs.pop(0)
-        arrival_refs = [refs.pop(0) for _ in range(2 if halves else len(met))]
+        arrival_refs = [refs.pop(0) for _ in range(len(met))]
     table_out = refs.pop(0)
     if made:
         out_ref, peram_ref, mixed_ref, sems = refs
@@ -285,45 +365,23 @@
             copy.start()
             copies.append(copy)
     table = table_ref[...]
+    for extra_ref in extra_refs:
+        table = table + extra_ref[...]
     if met:
         slots, eigen = before_ref.shape[1:3]
         for k, index in enumerate(met):
             column = separation(index, ring)
             for slot in range(slots):
-                if halves:
-                    rows = arrival_refs[slot // (slots // 2)][slot % (slots // 2)]
-                else:
-                    rows = arrival_refs[k][slot]
+                rows = arrival_refs[k][slot]
                 product = rows.astype(jnp.float32) * before_ref[k, slot]
                 table = add_to_table(table, product, slot, column)
     if made:
         slots, eigen, _ = phi_ref.shape
-        spins = peram_ref.shape[1]
-        blocks = []
-        for slot in range(slots):
-            rows = phi_ref[slot]
-            turned = jnp.concatenate([-rows[:, eigen:], rows[:, :eigen]], axis=1)
-            blocks.append(jnp.concatenate([rows, turned], axis=0))
+        blocks = elemental_blocks(phi_ref)
         for k, index in enumerate(made):
             copies[k].wait()
-            flipped, weights = [], []
-            for a in range(spins):
-                peram = peram_ref[k, a]
-                real, imag = peram[:, :eigen], peram[:, eigen:]
-                flipped.append(jnp.concatenate([real.T, imag.T], axis=1))
-                weights.append(jnp.concatenate([real, -imag], axis=1))
-                weights.append(jnp.concatenate([imag, real], axis=1))
-            flipped = jnp.concatenate(flipped, axis=0)
-            weights = jnp.concatenate(weights, axis=0)
-            for slot in range(slots):
-                mixed = jnp.dot(flipped, blocks[slot], preferred_element_type=jnp.float32)
-                mixed = mixed.astype(jnp.bfloat16)
-                for a in range(spins):
-                    mixed_ref[
-                        slot * eigen : (slot + 1) * eigen, 2 * eigen * a : 2 * eigen * (a + 1)
-                    ] = mixed[a * eigen : (a + 1) * eigen]
-            result = jnp.dot(mixed_ref[...], weights, preferred_element_type=jnp.float32)
-            result = result.reshape(slots, eigen, 2 * eigen)
+            perams = [peram_ref[k, a] for a in range(peram_ref.shape[1])]
+            result = sandwich_block(blocks, perams, mixed_ref)
             if index == 0:
                 for slot in range(slots):
                     product = phi_ref[slot].astype(jnp.float32) * result[slot]
@@ -333,12 +391,11 @@
     table_out[...] = table
 
 
-def sandwich_step(table, phi, perambulators, made, before, arrivals, met, ring):
+def sandwich_step(table, phi, perambulators, made, before, arrivals, met, ring, extra=()):
     slots, eigen, columns = phi.shape
     separations, spins = perambulators.shape[:2]
     vmem = pl.BlockSpec(memory_space=pltpu.VMEM)
-    halves = len(arrivals) > len(met)
-    operands, specs = [table], [vmem]
+    operands, specs = [table, *extra], [vmem] * (1 + len(extra))
     shapes, scratch = [jax.ShapeDtypeStruct(table.shape, table.dtype)], []
     if made:
         operands += [phi, perambulators]
@@ -355,12 +412,12 @@
         specs += [vmem] * (1 + len(arrivals))
     work = 4 * spins * slots * eigen * columns * columns
     return pl.pallas_call(
-        functools.partial(sandwich_kernel, tuple(made), tuple(met), halves, ring),
+        functools.partial(sandwich_kernel, tuple(made), tuple(met), ring, len(extra)),
         out_shape=tuple(shapes),
         in_specs=specs,
         out_specs=(vmem,) * len(shapes),
         scratch_shapes=scratch,
-        compiler_params=pltpu.CompilerParams(vmem_limit_bytes=24 * 1024 * 1024),
+        compiler_params=pltpu.CompilerParams(vmem_limit_bytes=16 * 1024 * 1024),
         cost_estimate=pl.CostEstimate(
             flops=len(made) * work + 1000,
             bytes_accessed=len(made) * 2 * spins * eigen * columns + 1000,
@@ -370,7 +427,7 @@
     )(*operands)
 
 
-def turn_kernel(phi_ref, kept_ref, given_ref, whole_ref):
+def turn_kernel(disp_ref, phi_ref, kept_ref, given_ref, place_out, own_out, other_out, whole_ref):
     slots, eigen, _ = phi_ref.shape
     half = eigen // 2
     side = lax.axis_index("space")
@@ -381,58 +438,98 @@
     others = pl.ds(pl.multiple_of((1 - side) * half, half), half)
     kept_ref[...] = whole_ref[:, mine, :]
     given_ref[...] = whole_ref[:, others, :]
-
-
-def turn(phi):
+    column = lax.broadcasted_iota(jnp.int32, own_out.shape, 1)
+    row = lax.broadcasted_iota(jnp.int32, own_out.shape, 0)
+    for k, (out, last) in enumerate(((own_out, side), (other_out, 1 - side))):
+        table = jnp.zeros(out.shape, jnp.float32)
+        for slot, value in enumerate(VALUES):
+            o = pick_operator(disp_ref, value, last)
+            place_out[k * slots + slot] = o
+            table = table + jnp.where((row == slot) & (column == o), 1.0, 0.0)
+        out[...] = table
+
+
+def turn(displacements, phi):
     slots, eigen, columns = phi.shape
     vmem = pl.BlockSpec(memory_space=pltpu.VMEM)
+    smem = pl.BlockSpec(memory_space=pltpu.SMEM)
     half = jax.ShapeDtypeStruct((slots, eigen // 2, columns), phi.dtype)
+    table = jax.ShapeDtypeStruct((slots, displacements.shape[0]), jnp.float32)
     return pl.pallas_call(
         turn_kernel,
-        out_shape=(half, half),
-        in_specs=[vmem],
-        out_specs=(vmem, vmem),
+        out_shape=(half, half, jax.ShapeDtypeStruct((2 * slots,), jnp.int32), table, table),
+        in_specs=[smem, vmem],
+        out_specs=(vmem, vmem, smem, vmem, vmem),
         scratch_shapes=[pltpu.VMEM(phi.shape, phi.dtype)],
+        compiler_params=pltpu.CompilerParams(vmem_limit_bytes=4 * 1024 * 1024),
         cost_estimate=pl.CostEstimate(flops=1000, bytes_accessed=4 * phi.size, transcendentals=0),
         name="turn",
-    )(phi)
-
-
-def order_kernel(source_ref, kept_ref, taken_ref, out_ref):
+    )(displacements, phi)
+
+
+def opposite_kernel(peram_hbm, first_ref, second_ref, sems):
+    count = lax.axis_size("tm")
+    opposite = apart(lax.axis_index("tm"), slice_behind(count // 2))
+    spins = first_ref.shape[0]
+    copies = []
+    for k, out in enumerate((first_ref, second_ref)):
+        rows = peram_hbm.at[opposite, pl.ds(k * spins, spins)]
+        copies.append(pltpu.make_async_copy(rows, out, sems.at[k]))
+        copies[-1].start()
+    for copy in copies:
+        copy.wait()
+
+
+def opposite_perambulators(perambulators):
+    vmem = pl.BlockSpec(memory_space=pltpu.VMEM)
+    half = (perambulators.shape[1] // 2,) + perambulators.shape[2:]
+    half = jax.ShapeDtypeStruct(half, perambulators.dtype)
+    return pl.pallas_call(
+        opposite_kernel,
+        out_shape=(half, half),
+        in_specs=[pl.BlockSpec(memory_space=pl.ANY)],
+        out_specs=(vmem, vmem),
+        scratch_shapes=[pltpu.SemaphoreType.DMA((2,))],
+        compiler_params=pltpu.CompilerParams(vmem_limit_bytes=65000 * 1024),
+        cost_estimate=pl.CostEstimate(flops=1000, bytes_accessed=1000000, transcendentals=0),
+        name="opposite_perambulators",
+    )(perambulators)
+
+
+def order_kernel(place_ref, kept_ref, taken_ref, out_ref, sems):
     slots = kept_ref.shape[0]
-    for o in range(out_ref.shape[0]):
-        at = source_ref[o]
-
-        @pl.when(at < slots)
-        def _(at=at, o=o):
-            out_ref[o] = kept_ref[at]
-
-        @pl.when(at >= slots)
-        def _(at=at, o=o):
-            out_ref[o] = taken_ref[at - slots]
-
-
-def order(source, kept, taken):
+    copies = []
+    for k in range(2 * slots):
+        rows = kept_ref.at[k] if k < slots else taken_ref.at[k - slots]
+        copies.append(pltpu.make_async_copy(rows, out_ref.at[place_ref[k]], sems.at[k]))
+    for copy in copies:
+        copy.start()
+    for copy in copies:
+        copy.wait()
+
+
+def order(places, kept, taken):
     vmem = pl.BlockSpec(memory_space=pltpu.VMEM)
     shape = (2 * kept.shape[0],) + kept.shape[1:]
     return pl.pallas_call(
         order_kernel,
         out_shape=jax.ShapeDtypeStruct(shape, kept.dtype),
         in_specs=[pl.BlockSpec(memory_space=pltpu.SMEM), vmem, vmem],
-        out_specs=vmem,
+        out_specs=pl.BlockSpec(memory_space=pl.ANY),
+        scratch_shapes=[pltpu.SemaphoreType.DMA((2 * kept.shape[0],))],
+        compiler_params=pltpu.CompilerParams(vmem_limit_bytes=4 * 1024 * 1024),
         cost_estimate=pl.CostEstimate(flops=1000, bytes_accessed=8 * kept.size, transcendentals=0),
         name="order",
-    )(source, kept, taken)
-
-
-def ring_pairs(count):
+    )(places, kept, taken)
+
+
+def ring_pairs(count, hops=1):
     around = list(range(0, count, 2)) + list(range(count - 1 - count % 2, 0, -2))
-    ahead = [(around[k], around[(k + 1) % count]) for k in range(count)]
+    ahead = [(around[k], around[(k + hops) % count]) for k in range(count)]
     return ahead, [(b, a) for a, b in ahead]
 
 
 def body(vectors, gauge_links, perambulators, momenta, displacements):
-    side = lax.axis_index("space")
     swap = [(0, 1), (1, 0)]
     half_x, ny, nz, eigen = vectors.shape[3:]
     own = vectors.reshape((6, half_x, ny, nz, eigen))
@@ -441,39 +538,34 @@
     other_links = lax.ppermute(own_links, "space", swap)
     norm_factor = 1.0 / math.sqrt(6.0 * 2 * half_x * ny * nz)
     operators = momenta.shape[0]
+    slots = len(VALUES)
+    count = lax.axis_size("tm")
+    peram = perambulators[0]
+    separations = peram.shape[0]
+    ring = count == separations and count % 4 == 0
+    ahead, behind = ring_pairs(count)
+    if ring:
+        two_ahead, two_behind = ring_pairs(count, count // 4)
+        first, second = opposite_perambulators(peram)
+        first = lax.ppermute(first, "tm", two_ahead)
+        second = lax.ppermute(second, "tm", two_behind)
     phi = elementals(
         norm_factor, displacements.reshape((1, operators)), momenta.T, own, other, own_links, other_links
     )
-    slots = phi.shape[0]
-
-    count = lax.axis_size("tm")
-    peram = perambulators[0]
-    separations = peram.shape[0]
-    ring = count == separations
-    number = jnp.arange(operators)
-    earlier = (displacements[:, None] == displacements[None, :]) & (number[None, :] < number[:, None])
-    mine = jnp.sum(earlier.astype(jnp.int32), axis=1) == side
-    slot_of = jnp.zeros((operators,), jnp.int32)
-    for slot, value in enumerate(VALUES):
-        slot_of = jnp.where(displacements == value, slot, slot_of)
-    source = slot_of + jnp.where(mine, 0, slots)
-    own_place = (source[:, None] == jnp.arange(slots)[None, :])[:, :, None]
-    other_place = (source[:, None] == slots + jnp.arange(slots)[None, :])[:, :, None]
+
+    if ring:
+        phi, first, second = lax.optimization_barrier((phi, first, second))
 
     table = jnp.zeros((slots, separations), jnp.float32)
     one_way = other_way = phi
-    before, met, came = None, [], []
-    ahead, behind = ring_pairs(count)
-    kept, given = turn(phi)
-    for first in range(1, separations, 2):
-        made = [k for k in (first, first + 1) if k < separations]
-        final = len(made) == 1
-        if ring and final:
-            arrivals = [
-                lax.ppermute(one_way[: slots // 2], "tm", ahead),
-                lax.ppermute(other_way[slots // 2 :], "tm", behind),
-            ]
-        elif ring:
+    before, met, came, extra = None, [], [], ()
+    steps = count // 2 if ring else separations // 2 + 1
+    for step in range(1, steps):
+        made = [2 * step - 1, 2 * step]
+        made = [k for k in made if k < separations]
+        if ring:
+            if step == count // 4 + 1:
+                middle = (one_way, other_way)
             one_way = lax.ppermute(one_way, "tm", ahead)
             other_way = lax.ppermute(other_way, "tm", behind)
             arrivals = [one_way, other_way]
@@ -482,25 +574,26 @@
             for _ in made:
                 one_way = lax.ppermute(one_way, "tm", [(i, (i + 1) % count) for i in range(count)])
                 arrivals.append(one_way)
-            if final:
-                arrivals = [one_way[: slots // 2], one_way[slots // 2 :]]
-        worked = [0] + made if first == 1 else made
+        worked = [0] + made if step == 1 else made
+        if ring and step == count // 4 + 1:
+            back, on = far(*middle, first, second, separations)
+            table, back, on = lax.optimization_barrier((table, back, on))
+            extra = (lax.ppermute(back, "tm", two_behind), lax.ppermute(on, "tm", two_ahead))
         table, sands = sandwich_step(table, phi, peram, worked, before, came, met, ring)
         before, met, came = sands, made, arrivals
-        if first == 1:
+        if step == 2:
+            kept, given, places, own_place, other_place = turn(displacements, phi)
             table, kept, given = lax.optimization_barrier((table, kept, given))
             taken = lax.ppermute(given, "space", swap)
-        if first == 5:
-            rows = order(source, kept, taken)
-            table, rows = lax.optimization_barrier((table, rows))
-        if not final:
-            one_way, other_way, table = lax.optimization_barrier((one_way, other_way, table))
+        if step < steps - 1:
+            one_way, other_way, table, phi = lax.optimization_barrier((one_way, other_way, table, phi))
             came = [one_way, other_way] if ring else arrivals
-    (table,) = sandwich_step(table, phi, peram, [], before, came, met, ring)
+    (table,) = sandwich_step(table, phi, peram, [], before, came, met, ring, extra)
     other_table = lax.ppermute(table, "space", swap)
 
+    rows = order(places, kept, taken)
     correlators = jnp.sum(
-        jnp.where(own_place, table[None], 0.0) + jnp.where(other_place, other_table[None], 0.0), axis=1
+        own_place[:, :, None] * table[:, None] + other_place[:, :, None] * other_table[:, None], axis=0
     )
     return (rows[None], correlators[:, None, :])
 

time: 51.6 us -> 48.2 us (0.934)
  local copies, waits for them, and re-layouts: 6.95 us -> 2.56 us
  starting transfers between devices: 12.6 us -> 15.1 us
  waiting for transfers between devices: 4.65 us -> 3.84 us
  other arithmetic: 1.44 us -> 0.67 us
    ppermute x2 -> x4, starting transfers between devices: 1.57 us -> 6.18 us  [the longest x1 3.81 us: body(): first = lax.ppermute(first, 'tm', two_ahead)]
    unnamed x24 -> x10, local copies, waits for them, and re-layouts: 6.92 us -> 2.55 us
    ppermute x1, starting transfers between devices: 2.97 us -> 0.78 us  [body(): other_table = lax.ppermute(table, 'space', swap)]
    pallas_call x1 -> x3, Pallas kernels: 1.84 us -> 3.96 us  [the longest x1 1.69 us: opposite_perambulators(): pl.pallas_call(opposite_kernel, out_shape=(half, half), in_specs=[pl.Bloc...]
    ppermute x2 -> x4, waiting for transfers between devices: 1.82 us -> 0.01 us  [the longest x1 0.01 us: body(): first = lax.ppermute(first, 'tm', two_ahead)]
    pallas_call x5 -> x4, Pallas kernels: 10.4 us -> 9.11 us  [sandwich_step(): pl.pallas_call(functools.partial(sandwich_kernel, tuple(made), tuple(met)...]
    ppermute x3, starting transfers between devices: 5.09 us -> 3.83 us  [body(): one_way = lax.ppermute(one_way, 'tm', ahead)]
    ppermute x1, starting transfers between devices: 1.9 us -> 3.15 us  [body(): taken = lax.ppermute(given, 'space', swap)]
  transfers between devices with their start and end apart: 12 -> 14, of which waited for: 4 -> 3; matrix products, arithmetic and copies ran while one was open for 2% -> 0% of each run, Pallas kernels for 27% -> 52%
where the time goes in v2:
time: 48.2 us; the launch traced here: 48 us
  Pallas kernels  25 us (52%)
  starting transfers between devices  15.1 us (31%)
  waiting for transfers between devices  3.84 us (8%)
  local copies, waits for them, and re-layouts  2.56 us (5%)
  between operations  0.79 us (2%)
  other arithmetic  0.67 us (1%)
    pallas_call x1, Pallas kernels, elementals(): pl.pallas_call(functools.partial(elemental_kernel, norm_factor), out_shap...  10.7 us
    pallas_call x4, Pallas kernels, sandwich_step(): pl.pallas_call(functools.partial(sandwich_kernel, tuple(made), tuple(met)...  9.11 us
    ppermute x3, starting transfers between devices, body(): one_way = lax.ppermute(one_way, 'tm', ahead)  3.83 us
    ppermute x1, starting transfers between devices, body(): first = lax.ppermute(first, 'tm', two_ahead)  3.81 us
    ppermute x1, starting transfers between devices, body(): taken = lax.ppermute(given, 'space', swap)  3.15 us
    unnamed x10, local copies, waits for them, and re-layouts  2.55 us
    ppermute x1, starting transfers between devices, body(): lax.ppermute(on, 'tm', two_ahead)  2.22 us
    ppermute x1, waiting for transfers between devices, body(): other_links = lax.ppermute(own_links, 'space', swap)  1.8 us
  transfers between devices with their start and end apart: 14, of which 3 were waited for; matrix products, arithmetic and copies ran while one was open for 0% of the time, Pallas kernels for 52%

profile of v2, /device:TPU:1, one launch (start us, length us, event | category | flops | bytes accessed | tf_op | source)
XLA Modules:
  0.0 48.0 jit_solution(16009309061349568507)
XLA Ops:
  0.6 0.1 collective-permute-start
  0.8 1.7 %opposite_perambulators.1 = (bf16[2,128,256]{2,1,0:T(8,128)(2,1)}, bf16[2,128,256]{2,1,0:T(8,128)(2,1)}) custom-call(bf16[8,4,128,256]{3,2,1,0:T(8,128)(2,1)} %bitcast.9), custom_call_target="tpu_custom_call" | custom-call | flops 1000 | bytes 1000000 | tf_op jit(solution)/shard_map/opposite_perambulators/pallas_call | solution.py:487
  2.5 3.8 %collective-permute-start.2 = (bf16[2,128,256]{2,1,0:T(8,128)(2,1)}, bf16[2,128,256]{2,1,0:T(8,128)(2,1)S(1)}, u32[]{:S(2)}, u32[]{:S(2)}) collective-permute-start(bf16[2,128,256]{2,1,0:T(8,128)(2,1)} %get-tuple-element.34), channel_id=1, source_target_pairs={{0,8},{4,12},{8,14},{12,10},{14,6},{10,2},{6,0},{2,4},{1,9},{5,13}... | collective-permute-start | bytes 393224 | tf_op jit(solution)/shard_map/ppermute | solution.py:550
  6.3 0.3 collective-permute-start.1
  6.6 1.8 %collective-permute-done.1.other_links_hbm = f32[54,4,4,16]{3,2,1,0:T(4,128)} collective-permute-done((f32[54,4,4,16]{3,2,1,0:T(4,128)}, f32[54,4,4,16]{3,2,1,0:T(4,128)}, u32[]{:S(2)}, u32[]{:S(2)}) %collective-permute-start.1) | collective-permute-done | bytes 55328 | tf_op jit(solution)/shard_map/ppermute | solution.py:538
  8.4 0.0 collective-permute-done.other_hbm
  8.4 10.7 %elementals.1.refs_1_.phi_ref = bf16[4,128,256]{2,1,0:T(8,128)(2,1)} custom-call(s32[1,8]{1,0:T(1,128)} %bitcast.13, s32[3,8]{1,0:T(4,128)} %bitcast.20, bf16[6,4,4,16,128]{4,3,2,1,0:T(8,128)(2,1)} %bitcast.19, bf16[6,4,4,16,128]{4,3,2,1,0:T(8,128)(2,1)} %collective-permute-done.other_hbm, f32[54,4,4,16]{3,2,1,0:T(4,128)} %bitcast.17, ...), custom_call_target="tpu_custom_call" | custom-call | flops 805306368 | bytes 786432 | tf_op jit(solution)/shard_map/elementals/pallas_call | solution.py:225
  19.1 0.0 collective-permute-done.2.first_ref
  19.1 0.2 collective-permute-start.5
  19.3 1.4 %collective-permute-start.4 = (bf16[4,128,256]{2,1,0:T(8,128)(2,1)}, bf16[4,128,256]{2,1,0:T(8,128)(2,1)S(1)}, u32[]{:S(2)}, u32[]{:S(2)}) collective-permute-start(bf16[4,128,256]{2,1,0:T(8,128)(2,1)} %elementals.1.refs_1_.phi_ref), channel_id=1, source_target_pairs={{0,4},{4,8},{8,12},{12,14},{14,10},{10,6},{6,2},{2,0},{1,5},{5,9},... | collective-permute-start | bytes 786440 | tf_op jit(solution)/shard_map/ppermute | solution.py:569
  20.7 1.6 %copy-done = bf16[1,8,4,128,256]{4,3,2,1,0:T(8,128)(2,1)S(1)} copy-done((bf16[1,8,4,128,256]{4,3,2,1,0:T(8,128)(2,1)S(1)}, bf16[1,8,4,128,256]{4,3,2,1,0:T(8,128)(2,1)}, u32[]{:S(2)}) %copy-start) | copy-done | bytes 2097176
  22.3 0.9 %copy-done.2 = bf16[4,128,256]{2,1,0:T(8,128)(2,1)S(1)} copy-done((bf16[4,128,256]{2,1,0:T(8,128)(2,1)S(1)}, bf16[4,128,256]{2,1,0:T(8,128)(2,1)}, u32[]{:S(2)}) %copy-start.2) | copy-done | bytes 262168
  23.2 3.7 %sandwich012_meet.1 = (f32[4,8]{1,0:T(4,128)S(1)}, f32[2,4,128,256]{3,2,1,0:T(8,128)S(1)}) custom-call(f32[4,8]{1,0:T(4,128)S(1)} %broadcast_in_dim.6.refs_0_, bf16[4,128,256]{2,1,0:T(8,128)(2,1)S(1)} %copy-done.2, bf16[8,4,128,256]{3,2,1,0:T(8,128)(2,1)S(1)} %bitcast.10), custom_call_target="tpu_custom_call" | custom-call | flops 1610613760 | bytes 787432 | tf_op jit(solution)/shard_map/sandwich012_meet/pallas_call | solution.py:414
  26.9 0.0 collective-permute-done.5.refs_5_
  26.9 1.3 %collective-permute-start.7 = (bf16[4,128,256]{2,1,0:T(8,128)(2,1)S(1)}, bf16[4,128,256]{2,1,0:T(8,128)(2,1)S(1)}, u32[]{:S(2)}, u32[]{:S(2)}) collective-permute-start(bf16[4,128,256]{2,1,0:T(8,128)(2,1)S(1)} %collective-permute-done.4.refs_4_), channel_id=1, source_target_pairs={{0,4},{4,8},{8,12},{12,14},{14,10},{10,6},{6,2},{2,0},{1,5},{5,9},... | collective-permute-start | bytes 786440 | tf_op jit(solution)/shard_map/ppermute | solution.py:569
  28.2 0.2 collective-permute-start.8
  28.5 1.2 %turn.1 = (bf16[4,64,256]{2,1,0:T(8,128)(2,1)S(1)}, bf16[4,64,256]{2,1,0:T(8,128)(2,1)S(1)}, s32[8]{0:T(128)S(1)}, f32[4,8]{1,0:T(4,128)S(1)}, f32[4,8]{1,0:T(4,128)S(1)}) custom-call(s32[8]{0:T(128)S(1)} %copy-done.4, bf16[4,128,256]{2,1,0:T(8,128)(2,1)S(1)} %copy-done.2), custom_call_target="tpu_custom_call" | custom-call | flops 1000 | bytes 524288 | tf_op jit(solution)/shard_map/turn/pallas_call | solution.py:458
  29.7 0.0 copy-start.3
  29.7 2.6 %sandwich34_meet12.1 = (f32[4,8]{1,0:T(4,128)S(1)}, f32[2,4,128,256]{3,2,1,0:T(8,128)S(1)}) custom-call(f32[4,8]{1,0:T(4,128)S(1)} %get-tuple-element.40.refs_0_, bf16[4,128,256]{2,1,0:T(8,128)(2,1)S(1)} %copy-done.2, bf16[8,4,128,256]{3,2,1,0:T(8,128)(2,1)S(1)} %bitcast.11, f32[2,4,128,256]{3,2,1,0:T(8,128)S(1)} %get-tuple-element.41.refs_3_, ...), custom_call_target="tpu_custom_call" | custom-call | flops 1073742848 | bytes 525288 | tf_op jit(solution)/shard_map/sandwich34_meet12/pallas_call | solution.py:414
  32.4 1.1 %collective-permute-done.7.behind_ref.refs_4_ = bf16[4,128,256]{2,1,0:T(8,128)(2,1)S(1)} collective-permute-done((bf16[4,128,256]{2,1,0:T(8,128)(2,1)S(1)}, bf16[4,128,256]{2,1,0:T(8,128)(2,1)S(1)}, u32[]{:S(2)}, u32[]{:S(2)}) %collective-permute-start.7) | collective-permute-done | bytes 262176 | tf_op jit(solution)/shard_map/ppermute | solution.py:569
  33.5 0.9 %collective-permute-done.8.ahead_ref.refs_5_ = bf16[4,128,256]{2,1,0:T(8,128)(2,1)S(1)} collective-permute-done((bf16[4,128,256]{2,1,0:T(8,128)(2,1)S(1)}, bf16[4,128,256]{2,1,0:T(8,128)(2,1)S(1)}, u32[]{:S(2)}, u32[]{:S(2)}) %collective-permute-start.8) | collective-permute-done | bytes 262176 | tf_op jit(solution)/shard_map/ppermute | solution.py:570
  34.4 1.2 %collective-permute-start.11 = (bf16[4,128,256]{2,1,0:T(8,128)(2,1)S(1)}, bf16[4,128,256]{2,1,0:T(8,128)(2,1)S(1)}, u32[]{:S(2)}, u32[]{:S(2)}) collective-permute-start(bf16[4,128,256]{2,1,0:T(8,128)(2,1)S(1)} %collective-permute-done.7.behind_ref.refs_4_), channel_id=1, source_target_pairs={{0,4},{4,8},{8,12},{12,14},{14,10},{10,6},{6,2},{2,0},{1,5},{5,9},... | collective-permute-start | bytes 786440 | tf_op jit(solution)/shard_map/ppermute | solution.py:569
  35.5 0.3 collective-permute-start.12
  35.8 3.1 %collective-permute-start.6 = (bf16[4,64,256]{2,1,0:T(8,128)(2,1)S(1)}, bf16[4,64,256]{2,1,0:T(8,128)(2,1)S(1)}, u32[]{:S(2)}, u32[]{:S(2)}) collective-permute-start(bf16[4,64,256]{2,1,0:T(8,128)(2,1)S(1)} %get-tuple-element.48), channel_id=1, source_target_pairs={{0,1},{1,0},{2,3},{3,2},{4,5},{5,4},{6,7},{7,6},{8,9},{9,8},{10,11... | collective-permute-start | bytes 393224 | tf_op jit(solution)/shard_map/ppermute | solution.py:587
  39.0 1.0 %far.1 = (f32[4,8]{1,0:T(4,128)S(1)}, f32[4,8]{1,0:T(4,128)S(1)}) custom-call(bf16[4,128,256]{2,1,0:T(8,128)(2,1)S(1)} %collective-permute-done.7.behind_ref.refs_4_, bf16[4,128,256]{2,1,0:T(8,128)(2,1)S(1)} %collective-permute-done.8.ahead_ref.refs_5_, bf16[2,128,256]{2,1,0:T(8,128)(2,1)S(1)} %collective-permute-done.2.first_ref, ...), custom_call_target="tpu_custom_call" | custom-call | flops 536870912 | bytes 524288 | tf_op jit(solution)/shard_map/far/pallas_call | solution.py:332
  40.0 0.1 collective-permute-start.9
  40.2 2.2 %collective-permute-start.10 = (f32[4,8]{1,0:T(4,128)S(1)}, f32[4,8]{1,0:T(4,128)S(1)}, u32[]{:S(2)}, u32[]{:S(2)}) collective-permute-start(f32[4,8]{1,0:T(4,128)S(1)} %get-tuple-element.63), channel_id=1, source_target_pairs={{0,8},{4,12},{8,14},{12,10},{14,6},{10,2},{6,0},{2,4},{1,9},{5,13}... | collective-permute-start | bytes 392 | tf_op jit(solution)/shard_map/ppermute | solution.py:581
  42.4 2.6 %sandwich56_meet34.1 = (f32[4,8]{1,0:T(4,128)S(1)}, f32[2,4,128,256]{3,2,1,0:T(8,128)S(1)}) custom-call(f32[4,8]{1,0:T(4,128)S(1)} %get-tuple-element.58.refs_0_, bf16[4,128,256]{2,1,0:T(8,128)(2,1)S(1)} %copy-done.3, bf16[8,4,128,256]{3,2,1,0:T(8,128)(2,1)S(1)} %bitcast.12, f32[2,4,128,256]{3,2,1,0:T(8,128)S(1)} %get-tuple-element.60.refs_3_, ...), custom_call_target="tpu_custom_call" | custom-call | flops 1073742848 | bytes 525288 | tf_op jit(solution)/shard_map/sandwich56_meet34/pallas_call | solution.py:414
  45.0 0.2 sandwich_meet56.1
  45.2 0.8 %collective-permute-start.13 = (f32[4,8]{1,0:T(4,128)S(1)}, f32[4,8]{1,0:T(4,128)S(1)}, u32[]{:S(2)}, u32[]{:S(2)}) collective-permute-start(f32[4,8]{1,0:T(4,128)S(1)} %sandwich_meet56.1), channel_id=1, source_target_pairs={{0,1},{1,0},{2,3},{3,2},{4,5},{5,4},{6,7},{7,6},{8,9},{9,8},{10,11... | collective-permute-start | bytes 392 | tf_op jit(solution)/shard_map/ppermute | solution.py:592
  46.0 1.3 %order.1 = bf16[8,64,256]{2,1,0:T(8,128)(2,1)} custom-call(s32[8]{0:T(128)S(1)} %get-tuple-element.39.place_ref, bf16[4,64,256]{2,1,0:T(8,128)(2,1)S(1)} %get-tuple-element.47.kept_ref, bf16[4,64,256]{2,1,0:T(8,128)(2,1)S(1)} %collective-permute-done.6.taken_ref), custom_call_target="tpu_custom_call" | custom-call | flops 1000 | bytes 524288 | tf_op jit(solution)/shard_map/order/pallas_call | solution.py:514
  47.3 0.7 %add_reduce_fusion = f32[8,8]{1,0:T(8,128)} fusion(f32[4,8]{1,0:T(4,128)S(1)} %collective-permute-done.13, f32[4,8]{1,0:T(4,128)S(1)} %get-tuple-element.65, f32[4,8]{1,0:T(4,128)S(1)} %sandwich_meet56.1, f32[4,8]{1,0:T(4,128)S(1)} %get-tuple-element.49), kind=kLoop, calls=%fused_computation | loop fusion | flops 960 | bytes 768 | tf_op jit(solution)/shard_map/reduce_sum | solution.py:595
  (17 shorter events, 0.0 us)
Async XLA Ops:
  0.6 7.8 %collective-permute-start = (bf16[6,4,4,16,128]{4,3,2,1,0:T(8,128)(2,1)}, bf16[6,4,4,16,128]{4,3,2,1,0:T(8,128)(2,1)}, u32[]{:S(2)}, u32[]{:S(2)}) collective-permute-start(bf16[6,4,4,16,128]{4,3,2,1,0:T(8,128)(2,1)} %bitcast.18), channel_id=1, source_target_pairs={{0,1},{1,0},{2,3},{3,2},{4,5},{5,4},{6,7},{7,6},{8,9},{9,8},{10,11... | collective-permute-start | bytes 1179656 | tf_op jit(solution)/shard_map/ppermute | solution.py:537
  2.5 16.6 %collective-permute-start.2 = (bf16[2,128,256]{2,1,0:T(8,128)(2,1)}, bf16[2,128,256]{2,1,0:T(8,128)(2,1)S(1)}, u32[]{:S(2)}, u32[]{:S(2)}) collective-permute-start(bf16[2,128,256]{2,1,0:T(8,128)(2,1)} %get-tuple-element.34), channel_id=1, source_target_pairs={{0,8},{4,12},{8,14},{12,10},{14,6},{10,2},{6,0},{2,4},{1,9},{5,13}... | collective-permute-start | bytes 393224 | tf_op jit(solution)/shard_map/ppermute | solution.py:550
  6.3 2.1 %collective-permute-start.1 = (f32[54,4,4,16]{3,2,1,0:T(4,128)}, f32[54,4,4,16]{3,2,1,0:T(4,128)}, u32[]{:S(2)}, u32[]{:S(2)}) collective-permute-start(f32[54,4,4,16]{3,2,1,0:T(4,128)} %bitcast.16), channel_id=1, source_target_pairs={{0,1},{1,0},{2,3},{3,2},{4,5},{5,4},{6,7},{7,6},{8,9},{9,8},{10,11... | collective-permute-start | bytes 165896 | tf_op jit(solution)/shard_map/ppermute | solution.py:538
  6.6 12.5 %collective-permute-start.3 = (bf16[2,128,256]{2,1,0:T(8,128)(2,1)}, bf16[2,128,256]{2,1,0:T(8,128)(2,1)S(1)}, u32[]{:S(2)}, u32[]{:S(2)}) collective-permute-start(bf16[2,128,256]{2,1,0:T(8,128)(2,1)} %get-tuple-element.35), channel_id=1, source_target_pairs={{8,0},{12,4},{14,8},{10,12},{6,14},{2,10},{0,6},{4,2},{9,1},{13,5}... | collective-permute-start | bytes 393224 | tf_op jit(solution)/shard_map/ppermute | solution.py:551
  19.1 7.8 %collective-permute-start.5 = (bf16[4,128,256]{2,1,0:T(8,128)(2,1)}, bf16[4,128,256]{2,1,0:T(8,128)(2,1)S(1)}, u32[]{:S(2)}, u32[]{:S(2)}) collective-permute-start(bf16[4,128,256]{2,1,0:T(8,128)(2,1)} %elementals.1.refs_1_.phi_ref), channel_id=1, source_target_pairs={{4,0},{8,4},{12,8},{14,12},{10,14},{6,10},{2,6},{0,2},{5,1},{9,5},... | collective-permute-start | bytes 786440 | tf_op jit(solution)/shard_map/ppermute | solution.py:570
  19.3 7.6 %collective-permute-start.4 = (bf16[4,128,256]{2,1,0:T(8,128)(2,1)}, bf16[4,128,256]{2,1,0:T(8,128)(2,1)S(1)}, u32[]{:S(2)}, u32[]{:S(2)}) collective-permute-start(bf16[4,128,256]{2,1,0:T(8,128)(2,1)} %elementals.1.refs_1_.phi_ref), channel_id=1, source_target_pairs={{0,4},{4,8},{8,12},{12,14},{14,10},{10,6},{6,2},{2,0},{1,5},{5,9},... | collective-permute-start | bytes 786440 | tf_op jit(solution)/shard_map/ppermute | solution.py:569
  20.7 1.6 %copy-start = (bf16[1,8,4,128,256]{4,3,2,1,0:T(8,128)(2,1)S(1)}, bf16[1,8,4,128,256]{4,3,2,1,0:T(8,128)(2,1)}, u32[]{:S(2)}) copy-start(bf16[1,8,4,128,256]{4,3,2,1,0:T(8,128)(2,1)} %param.7) | copy-start | bytes 6291460
  22.3 0.9 %copy-start.2 = (bf16[4,128,256]{2,1,0:T(8,128)(2,1)S(1)}, bf16[4,128,256]{2,1,0:T(8,128)(2,1)}, u32[]{:S(2)}) copy-start(bf16[4,128,256]{2,1,0:T(8,128)(2,1)} %elementals.1.refs_1_.phi_ref) | copy-start | bytes 786436
  23.2 5.2 %copy-start.4 = (s32[8]{0:T(128)S(1)}, s32[8]{0:T(128)}, u32[]{:S(2)}) copy-start(s32[8]{0:T(128)} %disp_ref.1) | copy-start | bytes 100
  23.2 6.5 %copy-start.1 = (bf16[1,8,4,128,256]{4,3,2,1,0:T(8,128)(2,1)S(1)}, bf16[1,8,4,128,256]{4,3,2,1,0:T(8,128)(2,1)}, u32[]{:S(2)}) copy-start(bf16[1,8,4,128,256]{4,3,2,1,0:T(8,128)(2,1)} %param.7) | copy-start | bytes 6291460
  26.9 6.5 %collective-permute-start.7 = (bf16[4,128,256]{2,1,0:T(8,128)(2,1)S(1)}, bf16[4,128,256]{2,1,0:T(8,128)(2,1)S(1)}, u32[]{:S(2)}, u32[]{:S(2)}) collective-permute-start(bf16[4,128,256]{2,1,0:T(8,128)(2,1)S(1)} %collective-permute-done.4.refs_4_), channel_id=1, source_target_pairs={{0,4},{4,8},{8,12},{12,14},{14,10},{10,6},{6,2},{2,0},{1,5},{5,9},... | collective-permute-start | bytes 786440 | tf_op jit(solution)/shard_map/ppermute | solution.py:569
  28.2 6.1 %collective-permute-start.8 = (bf16[4,128,256]{2,1,0:T(8,128)(2,1)S(1)}, bf16[4,128,256]{2,1,0:T(8,128)(2,1)S(1)}, u32[]{:S(2)}, u32[]{:S(2)}) collective-permute-start(bf16[4,128,256]{2,1,0:T(8,128)(2,1)S(1)} %collective-permute-done.5.refs_5_), channel_id=1, source_target_pairs={{4,0},{8,4},{12,8},{14,12},{10,14},{6,10},{2,6},{0,2},{5,1},{9,5},... | collective-permute-start | bytes 786440 | tf_op jit(solution)/shard_map/ppermute | solution.py:570
  29.7 12.7 %copy-start.3 = (bf16[4,128,256]{2,1,0:T(8,128)(2,1)S(1)}, bf16[4,128,256]{2,1,0:T(8,128)(2,1)}, u32[]{:S(2)}) copy-start(bf16[4,128,256]{2,1,0:T(8,128)(2,1)} %elementals.1.refs_1_.phi_ref) | copy-start | bytes 786436
  34.4 10.6 %collective-permute-start.11 = (bf16[4,128,256]{2,1,0:T(8,128)(2,1)S(1)}, bf16[4,128,256]{2,1,0:T(8,128)(2,1)S(1)}, u32[]{:S(2)}, u32[]{:S(2)}) collective-permute-start(bf16[4,128,256]{2,1,0:T(8,128)(2,1)S(1)} %collective-permute-done.7.behind_ref.refs_4_), channel_id=1, source_target_pairs={{0,4},{4,8},{8,12},{12,14},{14,10},{10,6},{6,2},{2,0},{1,5},{5,9},... | collective-permute-start | bytes 786440 | tf_op jit(solution)/shard_map/ppermute | solution.py:569
  35.5 9.5 %collective-permute-start.12 = (bf16[4,128,256]{2,1,0:T(8,128)(2,1)S(1)}, bf16[4,128,256]{2,1,0:T(8,128)(2,1)S(1)}, u32[]{:S(2)}, u32[]{:S(2)}) collective-permute-start(bf16[4,128,256]{2,1,0:T(8,128)(2,1)S(1)} %collective-permute-done.8.ahead_ref.refs_5_), channel_id=1, source_target_pairs={{4,0},{8,4},{12,8},{14,12},{10,14},{6,10},{2,6},{0,2},{5,1},{9,5},... | collective-permute-start | bytes 786440 | tf_op jit(solution)/shard_map/ppermute | solution.py:570
  35.8 10.2 %collective-permute-start.6 = (bf16[4,64,256]{2,1,0:T(8,128)(2,1)S(1)}, bf16[4,64,256]{2,1,0:T(8,128)(2,1)S(1)}, u32[]{:S(2)}, u32[]{:S(2)}) collective-permute-start(bf16[4,64,256]{2,1,0:T(8,128)(2,1)S(1)} %get-tuple-element.48), channel_id=1, source_target_pairs={{0,1},{1,0},{2,3},{3,2},{4,5},{5,4},{6,7},{7,6},{8,9},{9,8},{10,11... | collective-permute-start | bytes 393224 | tf_op jit(solution)/shard_map/ppermute | solution.py:587
  40.0 5.0 %collective-permute-start.9 = (f32[4,8]{1,0:T(4,128)S(1)}, f32[4,8]{1,0:T(4,128)S(1)}, u32[]{:S(2)}, u32[]{:S(2)}) collective-permute-start(f32[4,8]{1,0:T(4,128)S(1)} %get-tuple-element.62), channel_id=1, source_target_pairs={{8,0},{12,4},{14,8},{10,12},{6,14},{2,10},{0,6},{4,2},{9,1},{13,5}... | collective-permute-start | bytes 392 | tf_op jit(solution)/shard_map/ppermute | solution.py:581
  40.2 4.8 %collective-permute-start.10 = (f32[4,8]{1,0:T(4,128)S(1)}, f32[4,8]{1,0:T(4,128)S(1)}, u32[]{:S(2)}, u32[]{:S(2)}) collective-permute-start(f32[4,8]{1,0:T(4,128)S(1)} %get-tuple-element.63), channel_id=1, source_target_pairs={{0,8},{4,12},{8,14},{12,10},{14,6},{10,2},{6,0},{2,4},{1,9},{5,13}... | collective-permute-start | bytes 392 | tf_op jit(solution)/shard_map/ppermute | solution.py:581
  45.2 2.1 %collective-permute-start.13 = (f32[4,8]{1,0:T(4,128)S(1)}, f32[4,8]{1,0:T(4,128)S(1)}, u32[]{:S(2)}, u32[]{:S(2)}) collective-permute-start(f32[4,8]{1,0:T(4,128)S(1)} %sandwich_meet56.1), channel_id=1, source_target_pairs={{0,1},{1,0},{2,3},{3,2},{4,5},{5,4},{6,7},{7,6},{8,9},{9,8},{10,11... | collective-permute-start | bytes 392 | tf_op jit(solution)/shard_map/ppermute | solution.py:592

commit v3 on v2

--- a/solution.py
+++ b/solution.py
@@ -8,8 +8,6 @@
 from jax.experimental.pallas import tpu as pltpu
 from jax.sharding import PartitionSpec as P
 
-ROWS = 16
-UNROLL = 8
 VALUES = (2, 3, 1, 0)
 
 
@@ -22,26 +20,6 @@
         first_seen = jnp.where(hit, jnp.minimum(first_seen, o), first_seen)
         last_seen = jnp.where(hit, o, last_seen)
     return jnp.where(last == 0, first_seen, last_seen)
-
-
-def link_product(entry, field, adjoint):
-    real_rows, imag_rows = [], []
-    for a in range(3):
-        real_sum = imag_sum = None
-        for b in range(3):
-            if adjoint:
-                u_real, u_imag = entry(0, b, a), entry(1, b, a)
-                real_term = u_real * field[b] + u_imag * field[3 + b]
-                imag_term = u_real * field[3 + b] - u_imag * field[b]
-            else:
-                u_real, u_imag = entry(0, a, b), entry(1, a, b)
-                real_term = u_real * field[b] - u_imag * field[3 + b]
-                imag_term = u_real * field[3 + b] + u_imag * field[b]
-            real_sum = real_term if real_sum is None else real_sum + real_term
-            imag_sum = imag_term if imag_sum is None else imag_sum + imag_term
-        real_rows.append(real_sum)
-        imag_rows.append(imag_sum)
-    return real_rows + imag_rows
 
 
 def elemental_kernel(
@@ -55,48 +33,33 @@
     phi_ref,
     disp_ref,
     mom_ref,
-    own_ref,
-    other_ref,
-    own_links_ref,
-    other_links_ref,
-    vt_ref,
+    field_ref,
     links_ref,
-    back_ref,
+    rows_ref,
+    total_ref,
+    wave_ref,
     left_ref,
     right_ref,
     sems,
 ):
-    half_x, ny, nz, eigen = own_ref.shape[1:]
-    nx = 2 * half_x
-    lanes = nx * nz
+    _, nx, ny, nz, eigen = field_ref.shape
+    half_x = nx // 2
+    sites = nx * nz
     count = len(VALUES)
+    block = 6 * nz
     side = lax.axis_index("space")
-    z_at = lax.broadcasted_iota(jnp.int32, (ROWS, lanes), 1) % nz
+    first_half, second_half = pl.ds(0, half_x), pl.ds(half_x, half_x)
     pairs = (
         (disp_hbm, disp_ref),
         (mom_hbm, mom_ref),
-        (own_links_hbm, own_links_ref),
-        (other_links_hbm, other_links_ref),
-        (own_hbm, own_ref),
-        (other_hbm, other_ref),
+        (own_links_hbm, links_ref.at[:, first_half]),
+        (other_links_hbm, links_ref.at[:, second_half]),
+        (own_hbm, field_ref.at[:, first_half]),
+        (other_hbm, field_ref.at[:, second_half]),
     )
     copies = [pltpu.make_async_copy(s, d, sems.at[k]) for k, (s, d) in enumerate(pairs)]
     for copy in copies:
         copy.start()
-
-    def z_ahead(value):
-        return jnp.where(
-            z_at[: value.shape[0]] == nz - 1,
-            pltpu.roll(value, nz - 1, 1),
-            pltpu.roll(value, lanes - 1, 1),
-        )
-
-    def z_behind(value):
-        return jnp.where(
-            z_at[: value.shape[0]] == 0,
-            pltpu.roll(value, lanes - (nz - 1), 1),
-            pltpu.roll(value, 1, 1),
-        )
 
     copies[0].wait()
     copies[1].wait()
@@ -117,133 +80,168 @@
         spread_out = jnp.broadcast_to(momenta[k : k + 1], (kinds, operators))
         total = jnp.sum(jnp.where(chosen, spread_out, 0.0), axis=1, keepdims=True)
         steps.append(total.astype(jnp.int32) * scale)
-    lane = lax.broadcasted_iota(jnp.int32, (kinds, lanes), 1)
-    kind = lax.broadcasted_iota(jnp.int32, (kinds, lanes), 0)
+    lane = lax.broadcasted_iota(jnp.int32, (kinds, sites), 1)
+    kind = lax.broadcasted_iota(jnp.int32, (kinds, sites), 0)
     x_true = (lane // nz + half_x * side) % nx
     plane = steps[0] * x_true + steps[2] * (lane % nz) - (kind % 2) * (nz // 4)
-    waves = []
     for y in range(ny):
         turns = ((plane + steps[1] * y + nz // 2) & (nz - 1)) - nz // 2
-        waves.append(jnp.cos(turns.astype(jnp.float32) * (2.0 * math.pi / nz)).T)
+        wave_ref[y] = jnp.cos(turns.astype(jnp.float32) * (2.0 * math.pi / nz)).T
 
     copies[2].wait()
     copies[3].wait()
-    pieces = [own_links_ref[:, x] for x in range(half_x)]
-    pieces += [other_links_ref[:, x] for x in range(half_x)]
-    links = jnp.concatenate(pieces, axis=-1)
-    links_ref[...] = links
-    for row in range(18):
-        back_ref[row] = pltpu.roll(links[row], nz, 1)
-        back_ref[18 + row] = z_behind(links[36 + row])
-
-    copies[4].wait()
-    copies[5].wait()
-
-    def lay_out(y):
-        field = []
-        for c in range(6):
-            blocks = [own_ref[c, x, y] for x in range(half_x)]
-            blocks += [other_ref[c, x, y] for x in range(half_x)]
-            field.append(jnp.concatenate(blocks, axis=0).astype(jnp.float32))
-            vt_ref[c, y] = field[c].T
-        for slot in range(count):
-            cosine = jnp.broadcast_to(waves[y][:, 2 * slot : 2 * slot + 1], (lanes, eigen))
-            sine = jnp.broadcast_to(waves[y][:, 2 * slot + 1 : 2 * slot + 2], (lanes, eigen))
-            for a in range(3):
-                real = field[a] * cosine - field[3 + a] * sine
-                imag = field[a] * sine + field[3 + a] * cosine
-                base = (y * 6 + 2 * a) * lanes
-                left_ref[slot, pl.ds(base, lanes), :] = real.astype(jnp.bfloat16)
-                left_ref[slot, pl.ds(base + lanes, lanes), :] = imag.astype(jnp.bfloat16)
-
-    def fields(y):
-        y_ahead = (y + 1) % ny
-        y_behind = (y + ny - 1) % ny
-
-        def chunk(e):
-            rows = pl.ds(pl.multiple_of(e * ROWS, ROWS), ROWS)
-            lower = pl.ds(pl.multiple_of(e * ROWS + eigen, ROWS), ROWS)
-
-            def entries(ref, base, at):
-                return lambda part, a, b: ref[base + part * 9 + a * 3 + b, pl.ds(at, 1), :]
-
-            def put(value, moved):
-                slot = VALUES.index(value)
+    wide = rows_ref.shape[-1]
+    lane_at = lax.broadcasted_iota(jnp.int32, (nx, ny, wide), 2)
+    lower = lane_at < block // 2
+    first_z = lane_at % nz == 0
+    nothing = jnp.zeros((nx, ny, wide - block), jnp.float32)
+    for mu in range(3):
+        for a in range(3):
+            for way in range(2):
+                pieces = []
+                for part in range(2):
+                    for b in range(3):
+                        entry = a * 3 + b if way == 0 else b * 3 + a
+                        pieces.append(links_ref[mu * 18 + part * 9 + entry])
+                row = jnp.concatenate(pieces + [nothing], axis=-1)
+                if way == 1:
+                    row = jnp.where(lower, row, -row)
+                elif mu == 2:
+                    row = jnp.where(
+                        first_z, pltpu.roll(row, wide - (nz - 1), 2), pltpu.roll(row, 1, 2)
+                    )
+                rows_ref[mu, way, a] = row
+
+    z_row = lax.broadcasted_iota(jnp.int32, (nz, wide), 0)
+    z_lane = lax.broadcasted_iota(jnp.int32, (nz, wide), 1)
+    inside = z_lane < block
+    z_lane = z_lane % nz
+    masks = {
+        0: inside & (z_lane == z_row),
+        1: inside & (z_lane == (z_row + 1) % nz),
+        -1: inside & (z_lane == (z_row + nz - 1) % nz),
+    }
+    no_rows = jnp.zeros((wide - block, 2 * eigen), jnp.bfloat16)
+    half = block // 2
+
+    def matrix(mu, way, x, y):
+        mask = masks[0] if mu < 2 else masks[1 - 2 * way]
+        parts = []
+        for a in range(3):
+            entries = rows_ref[mu, way, a, x, pl.ds(y, 1), :]
+            parts.append(jnp.where(mask, entries, 0.0).astype(jnp.bfloat16))
+        return parts
+
+    for copy in copies[4:]:
+        copy.wait()
+
+    def plane_step(x, carry):
+        x_ahead = (x + 1) % nx
+        x_behind = (x + nx - 1) % nx
+        for y in range(ny):
+            y_ahead, y_behind = (y + 1) % ny, (y - 1) % ny
+            base = (x * ny + y) * block
+            parts = [field_ref[c, x, y] for c in range(6)]
+            real, imag = jnp.concatenate(parts[:3], axis=0), jnp.concatenate(parts[3:], axis=0)
+            source = jnp.concatenate(
+                [
+                    jnp.concatenate([real, imag], axis=1),
+                    jnp.concatenate([-imag, real], axis=1),
+                    no_rows,
+                ],
+                axis=0,
+            )
+            targets = ((0, 0, x_behind, y), (1, 0, x, y_behind), (2, 0, x, y))
+            targets += ((0, 1, x_ahead, y), (1, 1, x, y_ahead), (2, 1, x, y))
+            pieces = []
+            for mu, way, tx, ty in targets:
+                pieces += matrix(mu, way, x, y) if way == 1 else matrix(mu, way, tx, ty)
+            given = jnp.dot(
+                jnp.concatenate(pieces, axis=0), source, preferred_element_type=jnp.float32
+            )
+            for k, (mu, way, tx, ty) in enumerate(targets):
+                moved = given[k * half : (k + 1) * half]
+                if way == 0:
+                    at = (tx * ny + ty) * block
+                    reals = pl.ds(pl.multiple_of(at, half), half)
+                    imags = pl.ds(pl.multiple_of(at + half, half), half)
+                    right_ref[VALUES.index(mu + 1), reals, :] = moved[:, :eigen].astype(jnp.bfloat16)
+                    right_ref[VALUES.index(mu + 1), imags, :] = moved[:, eigen:].astype(jnp.bfloat16)
+                total_ref[k, tx, ty] = moved
+            field = [p.astype(jnp.float32) for p in parts]
+            waves = wave_ref[y, pl.ds(pl.multiple_of(x * nz, nz), nz), :]
+            for slot in range(count):
+                cosine = jnp.broadcast_to(waves[:, 2 * slot : 2 * slot + 1], (nz, eigen))
+                sine = jnp.broadcast_to(waves[:, 2 * slot + 1 : 2 * slot + 2], (nz, eigen))
                 for a in range(3):
-                    even = pl.ds((y * 6 + 2 * a) * lanes, lanes)
-                    odd = pl.ds((y * 6 + 2 * a + 1) * lanes, lanes)
-                    real = moved[a].astype(jnp.bfloat16)
-                    imag = moved[3 + a].astype(jnp.bfloat16)
-                    right_ref[slot, rows, even] = real
-                    right_ref[slot, rows, odd] = imag
-                    right_ref[slot, lower, even] = imag
-                    right_ref[slot, lower, odd] = -real
-
-            field = [vt_ref[c, y, rows, :] for c in range(6)]
-            ahead = [pltpu.roll(f, lanes - nz, 1) for f in field]
-            moved = link_product(entries(links_ref, 0, y), ahead, False)
-            put(1, moved)
-            total = moved
-            ahead = [vt_ref[c, y_ahead, rows, :] for c in range(6)]
-            moved = link_product(entries(links_ref, 18, y), ahead, False)
-            put(2, moved)
-            total = [p + q for p, q in zip(total, moved)]
-            ahead = [z_ahead(f) for f in field]
-            moved = link_product(entries(links_ref, 36, y), ahead, False)
-            put(3, moved)
-            total = [p + q for p, q in zip(total, moved)]
-            behind = [pltpu.roll(f, nz, 1) for f in field]
-            moved = link_product(entries(back_ref, 0, y), behind, True)
-            total = [p + q for p, q in zip(total, moved)]
-            behind = [vt_ref[c, y_behind, rows, :] for c in range(6)]
-            moved = link_product(entries(links_ref, 18, y_behind), behind, True)
-            total = [p + q for p, q in zip(total, moved)]
-            behind = [z_behind(f) for f in field]
-            moved = link_product(entries(back_ref, 18, y), behind, True)
-            total = [p + q for p, q in zip(total, moved)]
-            put(0, [f - t * (1.0 / 6.0) for f, t in zip(field, total)])
-
-        lax.fori_loop(0, eigen // ROWS, lambda e, c: (chunk(e), c)[1], 0, unroll=UNROLL)
-
-    for y in range(ny):
-        lay_out(y)
-    for y in range(ny):
-        fields(y)
+                    real = (field[a] * cosine - field[3 + a] * sine).astype(jnp.bfloat16)
+                    imag = (field[a] * sine + field[3 + a] * cosine).astype(jnp.bfloat16)
+                    reals = pl.ds(pl.multiple_of(base + a * nz, nz), nz)
+                    imags = pl.ds(pl.multiple_of(base + (3 + a) * nz, nz), nz)
+                    left_ref[slot, reals, :eigen] = real
+                    left_ref[slot, imags, :eigen] = imag
+                    left_ref[slot, reals, eigen:] = -imag
+                    left_ref[slot, imags, eigen:] = real
+        return carry
+
+    def smear_step(x, carry):
+        for y in range(ny):
+            base = (x * ny + y) * block
+            total = total_ref[0, x, y]
+            for k in range(1, 6):
+                total = total + total_ref[k, x, y]
+            total = total * (1.0 / 6.0)
+            for part in range(2):
+                field = jnp.concatenate([field_ref[3 * part + a, x, y] for a in range(3)], axis=0)
+                smooth = field.astype(jnp.float32) - total[:, part * eigen : (part + 1) * eigen]
+                at = pl.ds(pl.multiple_of(base + part * half, half), half)
+                right_ref[VALUES.index(0), at, :] = smooth.astype(jnp.bfloat16)
+        return carry
+
+    lax.fori_loop(0, nx, plane_step, 0, unroll=4)
+    lax.fori_loop(0, nx, smear_step, 0)
     for slot in range(count):
-        total = jnp.dot(right_ref[slot], left_ref[slot], preferred_element_type=jnp.float32)
-        total = (total * norm_factor).astype(jnp.bfloat16)
-        phi_ref[slot] = jnp.concatenate([total[:eigen], total[eigen:]], axis=1)
+        total = lax.dot_general(
+            right_ref[slot],
+            left_ref[slot],
+            (((0,), (0,)), ((), ())),
+            preferred_element_type=jnp.float32,
+        )
+        phi_ref[slot] = (total * norm_factor).astype(jnp.bfloat16)
 
 
 def elementals(norm_factor, displacements, momenta, own, other, own_links, other_links):
     half_x, ny, nz, eigen = own.shape[1:]
-    lanes = 2 * half_x * nz
+    nx = 2 * half_x
     count = len(VALUES)
+    sites = 6 * nx * ny * nz
     vmem = pl.BlockSpec(memory_space=pltpu.VMEM)
     anywhere = pl.BlockSpec(memory_space=pltpu.HBM)
-    operands = (displacements, momenta, own, other, own_links, other_links)
     return pl.pallas_call(
         functools.partial(elemental_kernel, norm_factor),
         out_shape=jax.ShapeDtypeStruct((count, eigen, 2 * eigen), jnp.bfloat16),
         in_specs=[anywhere] * 6,
         out_specs=vmem,
-        scratch_shapes=[pltpu.VMEM(p.shape, p.dtype) for p in operands]
-        + [
-            pltpu.VMEM((6, ny, eigen, lanes), jnp.float32),
-            pltpu.VMEM((54, ny, lanes), jnp.float32),
-            pltpu.VMEM((36, ny, lanes), jnp.float32),
-            pltpu.VMEM((count, 6 * ny * lanes, eigen), jnp.bfloat16),
-            pltpu.VMEM((count, 2 * eigen, 6 * ny * lanes), jnp.bfloat16),
+        scratch_shapes=[
+            pltpu.VMEM(displacements.shape, displacements.dtype),
+            pltpu.VMEM(momenta.shape, momenta.dtype),
+            pltpu.VMEM((6, nx, ny, nz, eigen), own.dtype),
+            pltpu.VMEM((54, nx, ny, nz), own_links.dtype),
+            pltpu.VMEM((3, 2, 3, nx, ny, 8 * nz), jnp.float32),
+            pltpu.VMEM((6, nx, ny, 3 * nz, 2 * eigen), jnp.float32),
+            pltpu.VMEM((ny, nx * nz, 2 * count), jnp.float32),
+            pltpu.VMEM((count, sites, 2 * eigen), jnp.bfloat16),
+            pltpu.VMEM((count, sites, eigen), jnp.bfloat16),
             pltpu.SemaphoreType.DMA((6,)),
         ],
         compiler_params=pltpu.CompilerParams(vmem_limit_bytes=65000 * 1024),
         cost_estimate=pl.CostEstimate(
-            flops=count * 2 * 6 * ny * lanes * eigen * 2 * eigen,
+            flops=count * 2 * sites * eigen * 2 * eigen,
             bytes_accessed=2 * own.size * 2,
             transcendentals=0,
         ),
         name="elementals",
-    )(*operands)
+    )(displacements, momenta, own, other, own_links, other_links)
 
 
 def slice_behind(hops):
@@ -549,15 +547,15 @@
         first, second = opposite_perambulators(peram)
         first = lax.ppermute(first, "tm", two_ahead)
         second = lax.ppermute(second, "tm", two_behind)
+    other, other_links = lax.optimization_barrier((other, other_links))
     phi = elementals(
         norm_factor, displacements.reshape((1, operators)), momenta.T, own, other, own_links, other_links
     )
 
+    table = jnp.zeros((slots, separations), jnp.float32)
+    one_way = other_way = phi
     if ring:
         phi, first, second = lax.optimization_barrier((phi, first, second))
-
-    table = jnp.zeros((slots, separations), jnp.float32)
-    one_way = other_way = phi
     before, met, came, extra = None, [], [], ()
     steps = count // 2 if ring else separations // 2 + 1
     for step in range(1, steps):

time: 48.2 us -> 43.2 us (0.90)
  Pallas kernels: 25 us -> 21.5 us
  waiting for transfers between devices: 3.84 us -> 2.08 us
    pallas_call x1, Pallas kernels: 10.7 us -> 7.17 us  [elementals(): pl.pallas_call(functools.partial(elemental_kernel, norm_factor), out_shap...]
    ppermute x1, waiting for transfers between devices: 1.8 us -> 0.01 us  [body(): other_links = lax.ppermute(own_links, 'space', swap)]
    ppermute x1, starting transfers between devices: 2.22 us -> 0.89 us  [body(): lax.ppermute(on, 'tm', two_ahead)]
    ppermute x1, starting transfers between devices: 0.15 us -> 1.48 us  [body(): lax.ppermute(back, 'tm', two_behind)]
    ppermute x3, starting transfers between devices: 3.83 us -> 2.62 us  [body(): one_way = lax.ppermute(one_way, 'tm', ahead)]
    ppermute x3, starting transfers between devices: 0.75 us -> 1.83 us  [body(): other_way = lax.ppermute(other_way, 'tm', behind)]
    ppermute x3, waiting for transfers between devices: 0.89 us -> 1.49 us  [body(): other_way = lax.ppermute(other_way, 'tm', behind)]
    ppermute x3, waiting for transfers between devices: 1.13 us -> 0.57 us  [body(): one_way = lax.ppermute(one_way, 'tm', ahead)]
  transfers between devices with their start and end apart: 14 -> 14, of which waited for: 3 -> 3; matrix products, arithmetic and copies ran while one was open for 0% -> 0% of each run, Pallas kernels for 52% -> 50%
where the time goes in v3:
time: 43.2 us; the launch traced here: 43 us
  Pallas kernels  21.5 us (50%)
  starting transfers between devices  15.4 us (36%)
  local copies, waits for them, and re-layouts  2.54 us (6%)
  waiting for transfers between devices  2.08 us (5%)
  between operations  0.77 us (2%)
  other arithmetic  0.67 us (2%)
    pallas_call x4, Pallas kernels, sandwich_step(): pl.pallas_call(functools.partial(sandwich_kernel, tuple(made), tuple(met)...  9.08 us
    pallas_call x1, Pallas kernels, elementals(): pl.pallas_call(functools.partial(elemental_kernel, norm_factor), out_shap...  7.17 us
    ppermute x1, starting transfers between devices, body(): first = lax.ppermute(first, 'tm', two_ahead)  3.44 us
    ppermute x1, starting transfers between devices, body(): taken = lax.ppermute(given, 'space', swap)  3.31 us
    ppermute x3, starting transfers between devices, body(): one_way = lax.ppermute(one_way, 'tm', ahead)  2.62 us
    unnamed x8, local copies, waits for them, and re-layouts  2.54 us
    ppermute x3, starting transfers between devices, body(): other_way = lax.ppermute(other_way, 'tm', behind)  1.83 us
    pallas_call x1, Pallas kernels, opposite_perambulators(): pl.pallas_call(opposite_kernel, out_shape=(half, half), in_specs=[pl.Bloc...  1.7 us
  transfers between devices with their start and end apart: 14, of which 3 were waited for; matrix products, arithmetic and copies ran while one was open for 0% of the time, Pallas kernels for 50%

profile of v3, /device:TPU:1, one launch (start us, length us, event | category | flops | bytes accessed | tf_op | source)
XLA Modules:
  0.0 43.0 jit_solution(533506892035555827)
XLA Ops:
  0.6 0.1 collective-permute-start
  0.8 0.5 %collective-permute-start.1 = (f32[54,4,4,16]{3,2,1,0:T(4,128)}, f32[54,4,4,16]{3,2,1,0:T(4,128)}, u32[]{:S(2)}, u32[]{:S(2)}) collective-permute-start(f32[54,4,4,16]{3,2,1,0:T(4,128)} %bitcast.16), channel_id=1, source_target_pairs={{0,1},{1,0},{2,3},{3,2},{4,5},{5,4},{6,7},{7,6},{8,9},{9,8},{10,11... | collective-permute-start | bytes 165896 | tf_op jit(solution)/shard_map/ppermute | solution.py:536
  1.2 1.7 %opposite_perambulators.1 = (bf16[2,128,256]{2,1,0:T(8,128)(2,1)}, bf16[2,128,256]{2,1,0:T(8,128)(2,1)}) custom-call(bf16[8,4,128,256]{3,2,1,0:T(8,128)(2,1)} %bitcast.9), custom_call_target="tpu_custom_call" | custom-call | flops 1000 | bytes 1000000 | tf_op jit(solution)/shard_map/opposite_perambulators/pallas_call | solution.py:485
  2.9 3.4 %collective-permute-start.4 = (bf16[2,128,256]{2,1,0:T(8,128)(2,1)}, bf16[2,128,256]{2,1,0:T(8,128)(2,1)S(1)}, u32[]{:S(2)}, u32[]{:S(2)}) collective-permute-start(bf16[2,128,256]{2,1,0:T(8,128)(2,1)} %get-tuple-element.38), channel_id=1, source_target_pairs={{0,8},{4,12},{8,14},{12,10},{14,6},{10,2},{6,0},{2,4},{1,9},{5,13}... | collective-permute-start | bytes 393224 | tf_op jit(solution)/shard_map/ppermute | solution.py:548
  6.4 0.0 collective-permute-done.1.other_links_hbm
  6.4 0.0 collective-permute-done.other_hbm
  6.4 7.2 %elementals.1.refs_1_.phi_ref = bf16[4,128,256]{2,1,0:T(8,128)(2,1)} custom-call(s32[1,8]{1,0:T(1,128)} %bitcast.13, s32[3,8]{1,0:T(4,128)} %bitcast.20, bf16[6,4,4,16,128]{4,3,2,1,0:T(8,128)(2,1)} %bitcast.19, bf16[6,4,4,16,128]{4,3,2,1,0:T(8,128)(2,1)} %collective-permute-done.other_hbm, f32[54,4,4,16]{3,2,1,0:T(4,128)} %bitcast.17, ...), custom_call_target="tpu_custom_call" | custom-call | flops 805306368 | bytes 786432 | tf_op jit(solution)/shard_map/elementals/pallas_call | solution.py:220
  13.5 1.3 %collective-permute-start.3 = (bf16[4,128,256]{2,1,0:T(8,128)(2,1)}, bf16[4,128,256]{2,1,0:T(8,128)(2,1)S(1)}, u32[]{:S(2)}, u32[]{:S(2)}) collective-permute-start(bf16[4,128,256]{2,1,0:T(8,128)(2,1)} %elementals.1.refs_1_.phi_ref), channel_id=1, source_target_pairs={{4,0},{8,4},{12,8},{14,12},{10,14},{6,10},{2,6},{0,2},{5,1},{9,5},... | collective-permute-start | bytes 786440 | tf_op jit(solution)/shard_map/ppermute | solution.py:568
  14.9 0.2 collective-permute-start.2
  15.1 0.0 collective-permute-done.4.first_ref
  15.1 0.0 copy-start
  15.1 1.6 %copy-done = bf16[1,8,4,128,256]{4,3,2,1,0:T(8,128)(2,1)S(1)} copy-done((bf16[1,8,4,128,256]{4,3,2,1,0:T(8,128)(2,1)S(1)}, bf16[1,8,4,128,256]{4,3,2,1,0:T(8,128)(2,1)}, u32[]{:S(2)}) %copy-start) | copy-done | bytes 2097176
  16.7 0.9 %copy-done.2 = bf16[4,128,256]{2,1,0:T(8,128)(2,1)S(1)} copy-done((bf16[4,128,256]{2,1,0:T(8,128)(2,1)S(1)}, bf16[4,128,256]{2,1,0:T(8,128)(2,1)}, u32[]{:S(2)}) %copy-start.2) | copy-done | bytes 262168
  17.6 3.7 %sandwich012_meet.1 = (f32[4,8]{1,0:T(4,128)S(1)}, f32[2,4,128,256]{3,2,1,0:T(8,128)S(1)}) custom-call(f32[4,8]{1,0:T(4,128)S(1)} %broadcast_in_dim.6.refs_0_, bf16[4,128,256]{2,1,0:T(8,128)(2,1)S(1)} %copy-done.2, bf16[8,4,128,256]{3,2,1,0:T(8,128)(2,1)S(1)} %bitcast.10), custom_call_target="tpu_custom_call" | custom-call | flops 1610613760 | bytes 787432 | tf_op jit(solution)/shard_map/sandwich012_meet/pallas_call | solution.py:412
  21.3 0.3 collective-permute-done.2.refs_4_
  21.6 1.1 %collective-permute-start.7 = (bf16[4,128,256]{2,1,0:T(8,128)(2,1)S(1)}, bf16[4,128,256]{2,1,0:T(8,128)(2,1)S(1)}, u32[]{:S(2)}, u32[]{:S(2)}) collective-permute-start(bf16[4,128,256]{2,1,0:T(8,128)(2,1)S(1)} %collective-permute-done.2.refs_4_), channel_id=1, source_target_pairs={{0,4},{4,8},{8,12},{12,14},{14,10},{10,6},{6,2},{2,0},{1,5},{5,9},... | collective-permute-start | bytes 786440 | tf_op jit(solution)/shard_map/ppermute | solution.py:567
  22.7 0.3 collective-permute-start.8
  23.1 1.2 %turn.1 = (bf16[4,64,256]{2,1,0:T(8,128)(2,1)S(1)}, bf16[4,64,256]{2,1,0:T(8,128)(2,1)S(1)}, s32[8]{0:T(128)S(1)}, f32[4,8]{1,0:T(4,128)S(1)}, f32[4,8]{1,0:T(4,128)S(1)}) custom-call(s32[8]{0:T(128)S(1)} %copy-done.3, bf16[4,128,256]{2,1,0:T(8,128)(2,1)S(1)} %copy-done.2), custom_call_target="tpu_custom_call" | custom-call | flops 1000 | bytes 524288 | tf_op jit(solution)/shard_map/turn/pallas_call | solution.py:456
  24.3 2.6 %sandwich34_meet12.1 = (f32[4,8]{1,0:T(4,128)S(1)}, f32[2,4,128,256]{3,2,1,0:T(8,128)S(1)}) custom-call(f32[4,8]{1,0:T(4,128)S(1)} %get-tuple-element.44.refs_0_, bf16[4,128,256]{2,1,0:T(8,128)(2,1)S(1)} %copy-done.2, bf16[8,4,128,256]{3,2,1,0:T(8,128)(2,1)S(1)} %bitcast.11, f32[2,4,128,256]{3,2,1,0:T(8,128)S(1)} %get-tuple-element.45.refs_3_, ...), custom_call_target="tpu_custom_call" | custom-call | flops 1073742848 | bytes 525288 | tf_op jit(solution)/shard_map/sandwich34_meet12/pallas_call | solution.py:412
  26.9 0.3 collective-permute-done.7.behind_ref.refs_4_
  27.2 1.5 %collective-permute-done.8.ahead_ref.refs_5_ = bf16[4,128,256]{2,1,0:T(8,128)(2,1)S(1)} collective-permute-done((bf16[4,128,256]{2,1,0:T(8,128)(2,1)S(1)}, bf16[4,128,256]{2,1,0:T(8,128)(2,1)S(1)}, u32[]{:S(2)}, u32[]{:S(2)}) %collective-permute-start.8) | collective-permute-done | bytes 262176 | tf_op jit(solution)/shard_map/ppermute | solution.py:568
  28.7 1.3 %collective-permute-start.11 = (bf16[4,128,256]{2,1,0:T(8,128)(2,1)S(1)}, bf16[4,128,256]{2,1,0:T(8,128)(2,1)S(1)}, u32[]{:S(2)}, u32[]{:S(2)}) collective-permute-start(bf16[4,128,256]{2,1,0:T(8,128)(2,1)S(1)} %collective-permute-done.7.behind_ref.refs_4_), channel_id=1, source_target_pairs={{0,4},{4,8},{8,12},{12,14},{14,10},{10,6},{6,2},{2,0},{1,5},{5,9},... | collective-permute-start | bytes 786440 | tf_op jit(solution)/shard_map/ppermute | solution.py:567
  30.0 0.2 collective-permute-start.12
  30.2 3.3 %collective-permute-start.6 = (bf16[4,64,256]{2,1,0:T(8,128)(2,1)S(1)}, bf16[4,64,256]{2,1,0:T(8,128)(2,1)S(1)}, u32[]{:S(2)}, u32[]{:S(2)}) collective-permute-start(bf16[4,64,256]{2,1,0:T(8,128)(2,1)S(1)} %get-tuple-element.52), channel_id=1, source_target_pairs={{0,1},{1,0},{2,3},{3,2},{4,5},{5,4},{6,7},{7,6},{8,9},{9,8},{10,11... | collective-permute-start | bytes 393224 | tf_op jit(solution)/shard_map/ppermute | solution.py:585
  33.5 1.0 %far.1 = (f32[4,8]{1,0:T(4,128)S(1)}, f32[4,8]{1,0:T(4,128)S(1)}) custom-call(bf16[4,128,256]{2,1,0:T(8,128)(2,1)S(1)} %collective-permute-done.7.behind_ref.refs_4_, bf16[4,128,256]{2,1,0:T(8,128)(2,1)S(1)} %collective-permute-done.8.ahead_ref.refs_5_, bf16[2,128,256]{2,1,0:T(8,128)(2,1)S(1)} %collective-permute-done.4.first_ref, ...), custom_call_target="tpu_custom_call" | custom-call | flops 536870912 | bytes 524288 | tf_op jit(solution)/shard_map/far/pallas_call | solution.py:330
  34.5 1.5 %collective-permute-start.9 = (f32[4,8]{1,0:T(4,128)S(1)}, f32[4,8]{1,0:T(4,128)S(1)}, u32[]{:S(2)}, u32[]{:S(2)}) collective-permute-start(f32[4,8]{1,0:T(4,128)S(1)} %get-tuple-element.66), channel_id=1, source_target_pairs={{8,0},{12,4},{14,8},{10,12},{6,14},{2,10},{0,6},{4,2},{9,1},{13,5}... | collective-permute-start | bytes 392 | tf_op jit(solution)/shard_map/ppermute | solution.py:579
  36.0 0.9 %collective-permute-start.10 = (f32[4,8]{1,0:T(4,128)S(1)}, f32[4,8]{1,0:T(4,128)S(1)}, u32[]{:S(2)}, u32[]{:S(2)}) collective-permute-start(f32[4,8]{1,0:T(4,128)S(1)} %get-tuple-element.67), channel_id=1, source_target_pairs={{0,8},{4,12},{8,14},{12,10},{14,6},{10,2},{6,0},{2,4},{1,9},{5,13}... | collective-permute-start | bytes 392 | tf_op jit(solution)/shard_map/ppermute | solution.py:579
  36.9 2.6 %sandwich56_meet34.1 = (f32[4,8]{1,0:T(4,128)S(1)}, f32[2,4,128,256]{3,2,1,0:T(8,128)S(1)}) custom-call(f32[4,8]{1,0:T(4,128)S(1)} %get-tuple-element.62.refs_0_, bf16[4,128,256]{2,1,0:T(8,128)(2,1)S(1)} %copy-done.2, bf16[8,4,128,256]{3,2,1,0:T(8,128)(2,1)S(1)} %bitcast.12, f32[2,4,128,256]{3,2,1,0:T(8,128)S(1)} %get-tuple-element.64.refs_3_, ...), custom_call_target="tpu_custom_call" | custom-call | flops 1073742848 | bytes 525288 | tf_op jit(solution)/shard_map/sandwich56_meet34/pallas_call | solution.py:412
  39.5 0.2 sandwich_meet56.1
  39.7 1.3 %collective-permute-start.13 = (f32[4,8]{1,0:T(4,128)S(1)}, f32[4,8]{1,0:T(4,128)S(1)}, u32[]{:S(2)}, u32[]{:S(2)}) collective-permute-start(f32[4,8]{1,0:T(4,128)S(1)} %sandwich_meet56.1), channel_id=1, source_target_pairs={{0,1},{1,0},{2,3},{3,2},{4,5},{5,4},{6,7},{7,6},{8,9},{9,8},{10,11... | collective-permute-start | bytes 392 | tf_op jit(solution)/shard_map/ppermute | solution.py:590
  41.0 1.3 %order.1 = bf16[8,64,256]{2,1,0:T(8,128)(2,1)} custom-call(s32[8]{0:T(128)S(1)} %get-tuple-element.43.place_ref, bf16[4,64,256]{2,1,0:T(8,128)(2,1)S(1)} %get-tuple-element.51.kept_ref, bf16[4,64,256]{2,1,0:T(8,128)(2,1)S(1)} %collective-permute-done.6.taken_ref), custom_call_target="tpu_custom_call" | custom-call | flops 1000 | bytes 524288 | tf_op jit(solution)/shard_map/order/pallas_call | solution.py:512
  42.3 0.7 %add_reduce_fusion = f32[8,8]{1,0:T(8,128)} fusion(f32[4,8]{1,0:T(4,128)S(1)} %collective-permute-done.13, f32[4,8]{1,0:T(4,128)S(1)} %get-tuple-element.69, f32[4,8]{1,0:T(4,128)S(1)} %sandwich_meet56.1, f32[4,8]{1,0:T(4,128)S(1)} %get-tuple-element.53), kind=kLoop, calls=%fused_computation | loop fusion | flops 960 | bytes 768 | tf_op jit(solution)/shard_map/reduce_sum | solution.py:593
  (15 shorter events, 0.0 us)
Async XLA Ops:
  0.6 5.7 %collective-permute-start = (bf16[6,4,4,16,128]{4,3,2,1,0:T(8,128)(2,1)}, bf16[6,4,4,16,128]{4,3,2,1,0:T(8,128)(2,1)}, u32[]{:S(2)}, u32[]{:S(2)}) collective-permute-start(bf16[6,4,4,16,128]{4,3,2,1,0:T(8,128)(2,1)} %bitcast.18), channel_id=1, source_target_pairs={{0,1},{1,0},{2,3},{3,2},{4,5},{5,4},{6,7},{7,6},{8,9},{9,8},{10,11... | collective-permute-start | bytes 1179656 | tf_op jit(solution)/shard_map/ppermute | solution.py:535
  0.8 5.6 %collective-permute-start.1 = (f32[54,4,4,16]{3,2,1,0:T(4,128)}, f32[54,4,4,16]{3,2,1,0:T(4,128)}, u32[]{:S(2)}, u32[]{:S(2)}) collective-permute-start(f32[54,4,4,16]{3,2,1,0:T(4,128)} %bitcast.16), channel_id=1, source_target_pairs={{0,1},{1,0},{2,3},{3,2},{4,5},{5,4},{6,7},{7,6},{8,9},{9,8},{10,11... | collective-permute-start | bytes 165896 | tf_op jit(solution)/shard_map/ppermute | solution.py:536
  2.9 12.1 %collective-permute-start.4 = (bf16[2,128,256]{2,1,0:T(8,128)(2,1)}, bf16[2,128,256]{2,1,0:T(8,128)(2,1)S(1)}, u32[]{:S(2)}, u32[]{:S(2)}) collective-permute-start(bf16[2,128,256]{2,1,0:T(8,128)(2,1)} %get-tuple-element.38), channel_id=1, source_target_pairs={{0,8},{4,12},{8,14},{12,10},{14,6},{10,2},{6,0},{2,4},{1,9},{5,13}... | collective-permute-start | bytes 393224 | tf_op jit(solution)/shard_map/ppermute | solution.py:548
  6.3 8.7 %collective-permute-start.5 = (bf16[2,128,256]{2,1,0:T(8,128)(2,1)}, bf16[2,128,256]{2,1,0:T(8,128)(2,1)S(1)}, u32[]{:S(2)}, u32[]{:S(2)}) collective-permute-start(bf16[2,128,256]{2,1,0:T(8,128)(2,1)} %get-tuple-element.39), channel_id=1, source_target_pairs={{8,0},{12,4},{14,8},{10,12},{6,14},{2,10},{0,6},{4,2},{9,1},{13,5}... | collective-permute-start | bytes 393224 | tf_op jit(solution)/shard_map/ppermute | solution.py:549
  13.5 7.8 %collective-permute-start.3 = (bf16[4,128,256]{2,1,0:T(8,128)(2,1)}, bf16[4,128,256]{2,1,0:T(8,128)(2,1)S(1)}, u32[]{:S(2)}, u32[]{:S(2)}) collective-permute-start(bf16[4,128,256]{2,1,0:T(8,128)(2,1)} %elementals.1.refs_1_.phi_ref), channel_id=1, source_target_pairs={{4,0},{8,4},{12,8},{14,12},{10,14},{6,10},{2,6},{0,2},{5,1},{9,5},... | collective-permute-start | bytes 786440 | tf_op jit(solution)/shard_map/ppermute | solution.py:568
  14.9 6.7 %collective-permute-start.2 = (bf16[4,128,256]{2,1,0:T(8,128)(2,1)}, bf16[4,128,256]{2,1,0:T(8,128)(2,1)S(1)}, u32[]{:S(2)}, u32[]{:S(2)}) collective-permute-start(bf16[4,128,256]{2,1,0:T(8,128)(2,1)} %elementals.1.refs_1_.phi_ref), channel_id=1, source_target_pairs={{0,4},{4,8},{8,12},{12,14},{14,10},{10,6},{6,2},{2,0},{1,5},{5,9},... | collective-permute-start | bytes 786440 | tf_op jit(solution)/shard_map/ppermute | solution.py:567
  15.1 1.6 %copy-start = (bf16[1,8,4,128,256]{4,3,2,1,0:T(8,128)(2,1)S(1)}, bf16[1,8,4,128,256]{4,3,2,1,0:T(8,128)(2,1)}, u32[]{:S(2)}) copy-start(bf16[1,8,4,128,256]{4,3,2,1,0:T(8,128)(2,1)} %param.7) | copy-start | bytes 6291460
  16.7 0.9 %copy-start.2 = (bf16[4,128,256]{2,1,0:T(8,128)(2,1)S(1)}, bf16[4,128,256]{2,1,0:T(8,128)(2,1)}, u32[]{:S(2)}) copy-start(bf16[4,128,256]{2,1,0:T(8,128)(2,1)} %elementals.1.refs_1_.phi_ref) | copy-start | bytes 786436
  17.6 5.5 %copy-start.3 = (s32[8]{0:T(128)S(1)}, s32[8]{0:T(128)}, u32[]{:S(2)}) copy-start(s32[8]{0:T(128)} %disp_ref.1) | copy-start | bytes 100
  17.6 6.7 %copy-start.1 = (bf16[1,8,4,128,256]{4,3,2,1,0:T(8,128)(2,1)S(1)}, bf16[1,8,4,128,256]{4,3,2,1,0:T(8,128)(2,1)}, u32[]{:S(2)}) copy-start(bf16[1,8,4,128,256]{4,3,2,1,0:T(8,128)(2,1)} %param.7) | copy-start | bytes 6291460
  21.6 5.6 %collective-permute-start.7 = (bf16[4,128,256]{2,1,0:T(8,128)(2,1)S(1)}, bf16[4,128,256]{2,1,0:T(8,128)(2,1)S(1)}, u32[]{:S(2)}, u32[]{:S(2)}) collective-permute-start(bf16[4,128,256]{2,1,0:T(8,128)(2,1)S(1)} %collective-permute-done.2.refs_4_), channel_id=1, source_target_pairs={{0,4},{4,8},{8,12},{12,14},{14,10},{10,6},{6,2},{2,0},{1,5},{5,9},... | collective-permute-start | bytes 786440 | tf_op jit(solution)/shard_map/ppermute | solution.py:567
  22.7 6.0 %collective-permute-start.8 = (bf16[4,128,256]{2,1,0:T(8,128)(2,1)S(1)}, bf16[4,128,256]{2,1,0:T(8,128)(2,1)S(1)}, u32[]{:S(2)}, u32[]{:S(2)}) collective-permute-start(bf16[4,128,256]{2,1,0:T(8,128)(2,1)S(1)} %collective-permute-done.3.refs_5_), channel_id=1, source_target_pairs={{4,0},{8,4},{12,8},{14,12},{10,14},{6,10},{2,6},{0,2},{5,1},{9,5},... | collective-permute-start | bytes 786440 | tf_op jit(solution)/shard_map/ppermute | solution.py:568
  28.7 10.8 %collective-permute-start.11 = (bf16[4,128,256]{2,1,0:T(8,128)(2,1)S(1)}, bf16[4,128,256]{2,1,0:T(8,128)(2,1)S(1)}, u32[]{:S(2)}, u32[]{:S(2)}) collective-permute-start(bf16[4,128,256]{2,1,0:T(8,128)(2,1)S(1)} %collective-permute-done.7.behind_ref.refs_4_), channel_id=1, source_target_pairs={{0,4},{4,8},{8,12},{12,14},{14,10},{10,6},{6,2},{2,0},{1,5},{5,9},... | collective-permute-start | bytes 786440 | tf_op jit(solution)/shard_map/ppermute | solution.py:567
  30.0 9.5 %collective-permute-start.12 = (bf16[4,128,256]{2,1,0:T(8,128)(2,1)S(1)}, bf16[4,128,256]{2,1,0:T(8,128)(2,1)S(1)}, u32[]{:S(2)}, u32[]{:S(2)}) collective-permute-start(bf16[4,128,256]{2,1,0:T(8,128)(2,1)S(1)} %collective-permute-done.8.ahead_ref.refs_5_), channel_id=1, source_target_pairs={{4,0},{8,4},{12,8},{14,12},{10,14},{6,10},{2,6},{0,2},{5,1},{9,5},... | collective-permute-start | bytes 786440 | tf_op jit(solution)/shard_map/ppermute | solution.py:568
  30.2 10.9 %collective-permute-start.6 = (bf16[4,64,256]{2,1,0:T(8,128)(2,1)S(1)}, bf16[4,64,256]{2,1,0:T(8,128)(2,1)S(1)}, u32[]{:S(2)}, u32[]{:S(2)}) collective-permute-start(bf16[4,64,256]{2,1,0:T(8,128)(2,1)S(1)} %get-tuple-element.52), channel_id=1, source_target_pairs={{0,1},{1,0},{2,3},{3,2},{4,5},{5,4},{6,7},{7,6},{8,9},{9,8},{10,11... | collective-permute-start | bytes 393224 | tf_op jit(solution)/shard_map/ppermute | solution.py:585
  34.5 5.0 %collective-permute-start.9 = (f32[4,8]{1,0:T(4,128)S(1)}, f32[4,8]{1,0:T(4,128)S(1)}, u32[]{:S(2)}, u32[]{:S(2)}) collective-permute-start(f32[4,8]{1,0:T(4,128)S(1)} %get-tuple-element.66), channel_id=1, source_target_pairs={{8,0},{12,4},{14,8},{10,12},{6,14},{2,10},{0,6},{4,2},{9,1},{13,5}... | collective-permute-start | bytes 392 | tf_op jit(solution)/shard_map/ppermute | solution.py:579
  36.0 3.5 %collective-permute-start.10 = (f32[4,8]{1,0:T(4,128)S(1)}, f32[4,8]{1,0:T(4,128)S(1)}, u32[]{:S(2)}, u32[]{:S(2)}) collective-permute-start(f32[4,8]{1,0:T(4,128)S(1)} %get-tuple-element.67), channel_id=1, source_target_pairs={{0,8},{4,12},{8,14},{12,10},{14,6},{10,2},{6,0},{2,4},{1,9},{5,13}... | collective-permute-start | bytes 392 | tf_op jit(solution)/shard_map/ppermute | solution.py:579
  39.7 2.6 %collective-permute-start.13 = (f32[4,8]{1,0:T(4,128)S(1)}, f32[4,8]{1,0:T(4,128)S(1)}, u32[]{:S(2)}, u32[]{:S(2)}) collective-permute-start(f32[4,8]{1,0:T(4,128)S(1)} %sandwich_meet56.1), channel_id=1, source_target_pairs={{0,1},{1,0},{2,3},{3,2},{4,5},{5,4},{6,7},{7,6},{8,9},{9,8},{10,11... | collective-permute-start | bytes 392 | tf_op jit(solution)/shard_map/ppermute | solution.py:590

commit v4 on v3

--- a/solution.py
+++ b/solution.py
@@ -110,7 +110,9 @@
                     row = jnp.where(
                         first_z, pltpu.roll(row, wide - (nz - 1), 2), pltpu.roll(row, 1, 2)
                     )
-                rows_ref[mu, way, a] = row
+                high = row.astype(jnp.bfloat16).astype(jnp.float32)
+                rows_ref[0, mu, way, a] = high
+                rows_ref[1, mu, way, a] = row - high
 
     z_row = lax.broadcasted_iota(jnp.int32, (nz, wide), 0)
     z_lane = lax.broadcasted_iota(jnp.int32, (nz, wide), 1)
@@ -128,8 +130,11 @@
         mask = masks[0] if mu < 2 else masks[1 - 2 * way]
         parts = []
         for a in range(3):
-            entries = rows_ref[mu, way, a, x, pl.ds(y, 1), :]
-            parts.append(jnp.where(mask, entries, 0.0).astype(jnp.bfloat16))
+            both = []
+            for part in range(2):
+                entries = rows_ref[part, mu, way, a, x, pl.ds(y, 1), :]
+                both.append(jnp.where(mask, entries, 0.0).astype(jnp.bfloat16))
+            parts.append(jnp.concatenate(both, axis=1))
         return parts
 
     for copy in copies[4:]:
@@ -151,6 +156,7 @@
                 ],
                 axis=0,
             )
+            source = jnp.concatenate([source, source], axis=0)
             targets = ((0, 0, x_behind, y), (1, 0, x, y_behind), (2, 0, x, y))
             targets += ((0, 1, x_ahead, y), (1, 1, x, y_ahead), (2, 1, x, y))
             pieces = []
@@ -161,14 +167,21 @@
             )
             for k, (mu, way, tx, ty) in enumerate(targets):
                 moved = given[k * half : (k + 1) * half]
+                if k == 2:
+                    local = moved
                 if way == 0:
                     at = (tx * ny + ty) * block
                     reals = pl.ds(pl.multiple_of(at, half), half)
                     imags = pl.ds(pl.multiple_of(at + half, half), half)
                     right_ref[VALUES.index(mu + 1), reals, :] = moved[:, :eigen].astype(jnp.bfloat16)
                     right_ref[VALUES.index(mu + 1), imags, :] = moved[:, eigen:].astype(jnp.bfloat16)
-                total_ref[k, tx, ty] = moved
+                if mu < 2:
+                    total_ref[mu + 2 * way, tx, ty] = moved
             field = [p.astype(jnp.float32) for p in parts]
+            here = jnp.concatenate(
+                [jnp.concatenate(field[:3], axis=0), jnp.concatenate(field[3:], axis=0)], axis=1
+            )
+            total_ref[4, x, y] = here - (local + moved) * (1.0 / 6.0)
             waves = wave_ref[y, pl.ds(pl.multiple_of(x * nz, nz), nz), :]
             for slot in range(count):
                 cosine = jnp.broadcast_to(waves[:, 2 * slot : 2 * slot + 1], (nz, eigen))
@@ -184,23 +197,7 @@
                     left_ref[slot, imags, eigen:] = real
         return carry
 
-    def smear_step(x, carry):
-        for y in range(ny):
-            base = (x * ny + y) * block
-            total = total_ref[0, x, y]
-            for k in range(1, 6):
-                total = total + total_ref[k, x, y]
-            total = total * (1.0 / 6.0)
-            for part in range(2):
-                field = jnp.concatenate([field_ref[3 * part + a, x, y] for a in range(3)], axis=0)
-                smooth = field.astype(jnp.float32) - total[:, part * eigen : (part + 1) * eigen]
-                at = pl.ds(pl.multiple_of(base + part * half, half), half)
-                right_ref[VALUES.index(0), at, :] = smooth.astype(jnp.bfloat16)
-        return carry
-
-    lax.fori_loop(0, nx, plane_step, 0, unroll=4)
-    lax.fori_loop(0, nx, smear_step, 0)
-    for slot in range(count):
+    def project(slot):
         total = lax.dot_general(
             right_ref[slot],
             left_ref[slot],
@@ -208,6 +205,23 @@
             preferred_element_type=jnp.float32,
         )
         phi_ref[slot] = (total * norm_factor).astype(jnp.bfloat16)
+
+    lax.fori_loop(0, nx, plane_step, 0, unroll=8)
+    smeared = VALUES.index(0)
+    for slot in range(count):
+        if slot != smeared:
+            project(slot)
+    for x in range(nx):
+        for y in range(ny):
+            base = (x * ny + y) * block
+            total = total_ref[0, x, y]
+            for k in range(1, 4):
+                total = total + total_ref[k, x, y]
+            smooth = (total_ref[4, x, y] - total * (1.0 / 6.0)).astype(jnp.bfloat16)
+            for part in range(2):
+                rows = smooth[:, part * eigen : (part + 1) * eigen]
+                right_ref[smeared, pl.ds(base + part * half, half), :] = rows
+    project(smeared)
 
 
 def elementals(norm_factor, displacements, momenta, own, other, own_links, other_links):
@@ -227,8 +241,8 @@
             pltpu.VMEM(momenta.shape, momenta.dtype),
             pltpu.VMEM((6, nx, ny, nz, eigen), own.dtype),
             pltpu.VMEM((54, nx, ny, nz), own_links.dtype),
-            pltpu.VMEM((3, 2, 3, nx, ny, 8 * nz), jnp.float32),
-            pltpu.VMEM((6, nx, ny, 3 * nz, 2 * eigen), jnp.float32),
+            pltpu.VMEM((2, 3, 2, 3, nx, ny, 8 * nz), jnp.float32),
+            pltpu.VMEM((5, nx, ny, 3 * nz, 2 * eigen), jnp.float32),
             pltpu.VMEM((ny, nx * nz, 2 * count), jnp.float32),
             pltpu.VMEM((count, sites, 2 * eigen), jnp.bfloat16),
             pltpu.VMEM((count, sites, eigen), jnp.bfloat16),
@@ -305,42 +319,37 @@
     return result.reshape(len(blocks), eigen, 2 * eigen)
 
 
-def far_kernel(behind_ref, ahead_ref, first_ref, second_ref, back_out, on_out, mixed_ref):
+def far_kernel(behind_ref, ahead_ref, some_ref, rest_ref, back_out, mixed_ref):
     count = lax.axis_size("tm")
-    behind = slice_behind(count // 4)
-    ahead = slice_behind(-(count // 4))
-    for sink_ref, source_ref, peram_ref, out, column in (
-        (behind_ref, ahead_ref, first_ref, back_out, apart(behind, ahead)),
-        (ahead_ref, behind_ref, second_ref, on_out, apart(ahead, behind)),
-    ):
-        perams = [peram_ref[a] for a in range(peram_ref.shape[0])]
-        result = sandwich_block(elemental_blocks(sink_ref), perams, mixed_ref)
-        table = jnp.zeros(out.shape, jnp.float32)
-        for slot in range(sink_ref.shape[0]):
-            product = source_ref[slot].astype(jnp.float32) * result[slot]
-            table = add_to_table(table, product, slot, column)
-        out[...] = table
-
-
-def far(behind, ahead, first, second, separations):
+    hops = count // 4
+    column = apart(slice_behind(hops), slice_behind(-hops))
+    perams = [ref[a] for ref in (some_ref, rest_ref) for a in range(ref.shape[0])]
+    result = sandwich_block(elemental_blocks(behind_ref), perams, mixed_ref)
+    table = jnp.zeros(back_out.shape, jnp.float32)
+    for slot in range(behind_ref.shape[0]):
+        product = ahead_ref[slot].astype(jnp.float32) * result[slot]
+        table = add_to_table(table, product, slot, column)
+    back_out[...] = table
+
+
+def far(behind, ahead, some, rest, separations):
     slots, eigen, columns = behind.shape
-    spins = first.shape[0]
+    spins = 2 * some.shape[0]
     vmem = pl.BlockSpec(memory_space=pltpu.VMEM)
-    table = jax.ShapeDtypeStruct((slots, separations), jnp.float32)
     return pl.pallas_call(
         far_kernel,
-        out_shape=(table, table),
+        out_shape=jax.ShapeDtypeStruct((slots, separations), jnp.float32),
         in_specs=[vmem] * 4,
-        out_specs=(vmem, vmem),
+        out_specs=vmem,
         scratch_shapes=[pltpu.VMEM((slots * eigen, spins * columns), jnp.bfloat16)],
         compiler_params=pltpu.CompilerParams(vmem_limit_bytes=16 * 1024 * 1024),
         cost_estimate=pl.CostEstimate(
-            flops=8 * spins * slots * eigen * columns * columns,
+            flops=4 * spins * slots * eigen * columns * columns,
             bytes_accessed=4 * behind.size,
             transcendentals=0,
         ),
         name="far",
-    )(behind, ahead, first, second)
+    )(behind, ahead, some, rest)
 
 
 def sandwich_kernel(made, met, ring, extra, *refs):
@@ -465,35 +474,6 @@
     )(displacements, phi)
 
 
-def opposite_kernel(peram_hbm, first_ref, second_ref, sems):
-    count = lax.axis_size("tm")
-    opposite = apart(lax.axis_index("tm"), slice_behind(count // 2))
-    spins = first_ref.shape[0]
-    copies = []
-    for k, out in enumerate((first_ref, second_ref)):
-        rows = peram_hbm.at[opposite, pl.ds(k * spins, spins)]
-        copies.append(pltpu.make_async_copy(rows, out, sems.at[k]))
-        copies[-1].start()
-    for copy in copies:
-        copy.wait()
-
-
-def opposite_perambulators(perambulators):
-    vmem = pl.BlockSpec(memory_space=pltpu.VMEM)
-    half = (perambulators.shape[1] // 2,) + perambulators.shape[2:]
-    half = jax.ShapeDtypeStruct(half, perambulators.dtype)
-    return pl.pallas_call(
-        opposite_kernel,
-        out_shape=(half, half),
-        in_specs=[pl.BlockSpec(memory_space=pl.ANY)],
-        out_specs=(vmem, vmem),
-        scratch_shapes=[pltpu.SemaphoreType.DMA((2,))],
-        compiler_params=pltpu.CompilerParams(vmem_limit_bytes=65000 * 1024),
-        cost_estimate=pl.CostEstimate(flops=1000, bytes_accessed=1000000, transcendentals=0),
-        name="opposite_perambulators",
-    )(perambulators)
-
-
 def order_kernel(place_ref, kept_ref, taken_ref, out_ref, sems):
     slots = kept_ref.shape[0]
     copies = []
@@ -544,9 +524,11 @@
     ahead, behind = ring_pairs(count)
     if ring:
         two_ahead, two_behind = ring_pairs(count, count // 4)
-        first, second = opposite_perambulators(peram)
-        first = lax.ppermute(first, "tm", two_ahead)
-        second = lax.ppermute(second, "tm", two_behind)
+        opposite = apart(lax.axis_index("tm"), slice_behind(count // 2))
+        spins = peram.shape[1] // 2
+        start = (opposite, lax.axis_index("space") * spins, 0, 0)
+        some = lax.dynamic_slice(peram, start, (1, spins) + peram.shape[2:])[0]
+        some = lax.ppermute(some, "tm", two_ahead)
     other, other_links = lax.optimization_barrier((other, other_links))
     phi = elementals(
         norm_factor, displacements.reshape((1, operators)), momenta.T, own, other, own_links, other_links
@@ -555,7 +537,8 @@
     table = jnp.zeros((slots, separations), jnp.float32)
     one_way = other_way = phi
     if ring:
-        phi, first, second = lax.optimization_barrier((phi, first, second))
+        phi, some = lax.optimization_barrier((phi, some))
+        rest = lax.ppermute(some, "space", swap)
     before, met, came, extra = None, [], [], ()
     steps = count // 2 if ring else separations // 2 + 1
     for step in range(1, steps):
@@ -574,9 +557,9 @@
                 arrivals.append(one_way)
         worked = [0] + made if step == 1 else made
         if ring and step == count // 4 + 1:
-            back, on = far(*middle, first, second, separations)
-            table, back, on = lax.optimization_barrier((table, back, on))
-            extra = (lax.ppermute(back, "tm", two_behind), lax.ppermute(on, "tm", two_ahead))
+            back = far(*middle, some, rest, separations)
+            table, back = lax.optimization_barrier((table, back))
+            extra = (lax.ppermute(back, "tm", two_behind),)
         table, sands = sandwich_step(table, phi, peram, worked, before, came, met, ring)
         before, met, came = sands, made, arrivals
         if step == 2:

time: 43.2 us -> 40.4 us (0.935)
  Pallas kernels: 21.5 us -> 18.9 us
  waiting for transfers between devices: 2.08 us -> 0.42 us
  local copies, waits for them, and re-layouts: 2.54 us -> 3.5 us
    pallas_call x2 -> x1, Pallas kernels: 2.75 us -> 1.24 us  [far(): pl.pallas_call(far_kernel, out_shape=jax.ShapeDtypeStruct((slots, separat...]
    ppermute x3, starting transfers between devices: 2.62 us -> 3.76 us  [body(): one_way = lax.ppermute(one_way, 'tm', ahead)]
    ppermute x3, waiting for transfers between devices: 1.49 us -> 0.39 us  [body(): other_way = lax.ppermute(other_way, 'tm', behind)]
    ppermute x3, starting transfers between devices: 1.83 us -> 0.74 us  [body(): other_way = lax.ppermute(other_way, 'tm', behind)]
    pallas_call x1, Pallas kernels: 7.17 us -> 6.12 us  [elementals(): pl.pallas_call(functools.partial(elemental_kernel, norm_factor), out_shap...]
    squeeze x0 -> x1, local copies, waits for them, and re-layouts: none -> 0.91 us  [body(): some = lax.dynamic_slice(peram, start, (1, spins) + peram.shape[2:])[0]]
    ppermute x3, waiting for transfers between devices: 0.57 us -> 0.01 us  [body(): one_way = lax.ppermute(one_way, 'tm', ahead)]
    ppermute x4 -> x3, starting transfers between devices: 5.81 us -> 6.21 us  [the longest x1 3.44 us: body(): some = lax.ppermute(some, 'tm', two_ahead)]
  transfers between devices with their start and end apart: 14 -> 13, of which waited for: 3 -> 1; matrix products, arithmetic and copies ran while one was open for 0% -> 2% of each run, Pallas kernels for 50% -> 47%
where the time goes in v4:
time: 40.4 us; the launch traced here: 40.1 us
  Pallas kernels  18.9 us (47%)
  starting transfers between devices  15.8 us (39%)
  local copies, waits for them, and re-layouts  3.5 us (9%)
  between operations  0.77 us (2%)
  other arithmetic  0.67 us (2%)
  waiting for transfers between devices  0.42 us (1%)
    pallas_call x4, Pallas kernels, sandwich_step(): pl.pallas_call(functools.partial(sandwich_kernel, tuple(made), tuple(met)...  9.06 us
    pallas_call x1, Pallas kernels, elementals(): pl.pallas_call(functools.partial(elemental_kernel, norm_factor), out_shap...  6.12 us
    ppermute x3, starting transfers between devices, body(): one_way = lax.ppermute(one_way, 'tm', ahead)  3.76 us
    ppermute x1, starting transfers between devices, body(): some = lax.ppermute(some, 'tm', two_ahead)  3.44 us
    ppermute x1, starting transfers between devices, body(): taken = lax.ppermute(given, 'space', swap)  3.04 us
    unnamed x10, local copies, waits for them, and re-layouts  2.58 us
    ppermute x1, starting transfers between devices, body(): rest = lax.ppermute(some, 'space', swap)  1.84 us
    ppermute x1, starting transfers between devices, body(): other_table = lax.ppermute(table, 'space', swap)  1.51 us
  transfers between devices with their start and end apart: 13, of which 1 were waited for; matrix products, arithmetic and copies ran while one was open for 2% of the time, Pallas kernels for 47%

profile of v4, /device:TPU:1, one launch (start us, length us, event | category | flops | bytes accessed | tf_op | source)
XLA Modules:
  0.0 40.1 jit_solution(9926141258763029795)
XLA Ops:
  0.6 0.1 collective-permute-start
  0.8 0.5 %collective-permute-start.1 = (f32[54,4,4,16]{3,2,1,0:T(4,128)}, f32[54,4,4,16]{3,2,1,0:T(4,128)}, u32[]{:S(2)}, u32[]{:S(2)}) collective-permute-start(f32[54,4,4,16]{3,2,1,0:T(4,128)} %bitcast.17), channel_id=1, source_target_pairs={{0,1},{1,0},{2,3},{3,2},{4,5},{5,4},{6,7},{7,6},{8,9},{9,8},{10,11... | collective-permute-start | bytes 165896 | tf_op jit(solution)/shard_map/ppermute | solution.py:516
  1.2 0.9 %dynamic-slice_bitcast_fusion = bf16[2,128,256]{2,1,0:T(8,128)(2,1)S(1)} fusion(bf16[1,8,4,128,256]{4,3,2,1,0:T(8,128)(2,1)} %param.7, s32[]{:T(128)S(6)} %select_n.41, s32[]{:T(128)S(6)} %select_n.42), kind=kLoop, calls=%fused_computation | loop fusion | bytes 262152 | tf_op jit(solution)/shard_map/squeeze | solution.py:530
  2.1 3.4 %collective-permute-start.4 = (bf16[2,128,256]{2,1,0:T(8,128)(2,1)S(1)}, bf16[2,128,256]{2,1,0:T(8,128)(2,1)S(1)}, u32[]{:S(2)}, u32[]{:S(2)}) collective-permute-start(bf16[2,128,256]{2,1,0:T(8,128)(2,1)S(1)} %dynamic-slice_bitcast_fusion), channel_id=1, source_target_pairs={{0,8},{4,12},{8,14},{12,10},{14,6},{10,2},{6,0},{2,4},{1,9},{5,13}... | collective-permute-start | bytes 393224 | tf_op jit(solution)/shard_map/ppermute | solution.py:531
  5.6 6.1 %elementals.1.refs_1_.phi_ref = bf16[4,128,256]{2,1,0:T(8,128)(2,1)} custom-call(s32[1,8]{1,0:T(1,128)} %bitcast.14, s32[3,8]{1,0:T(4,128)} %bitcast.21, bf16[6,4,4,16,128]{4,3,2,1,0:T(8,128)(2,1)} %bitcast.20, bf16[6,4,4,16,128]{4,3,2,1,0:T(8,128)(2,1)} %collective-permute-done.other_hbm, f32[54,4,4,16]{3,2,1,0:T(4,128)} %bitcast.18, ...), custom_call_target="tpu_custom_call" | custom-call | flops 805306368 | bytes 786432 | tf_op jit(solution)/shard_map/elementals/pallas_call | solution.py:234
  11.7 0.2 collective-permute-start.3
  11.9 1.3 %collective-permute-start.2 = (bf16[4,128,256]{2,1,0:T(8,128)(2,1)}, bf16[4,128,256]{2,1,0:T(8,128)(2,1)S(1)}, u32[]{:S(2)}, u32[]{:S(2)}) collective-permute-start(bf16[4,128,256]{2,1,0:T(8,128)(2,1)} %elementals.1.refs_1_.phi_ref), channel_id=1, source_target_pairs={{0,4},{4,8},{8,12},{12,14},{14,10},{10,6},{6,2},{2,0},{1,5},{5,9},... | collective-permute-start | bytes 786440 | tf_op jit(solution)/shard_map/ppermute | solution.py:550
  13.2 0.0 collective-permute-done.4.some_ref
  13.2 1.0 %copy-done = bf16[4,128,256]{2,1,0:T(8,128)(2,1)S(1)} copy-done((bf16[4,128,256]{2,1,0:T(8,128)(2,1)S(1)}, bf16[4,128,256]{2,1,0:T(8,128)(2,1)}, u32[]{:S(2)}) %copy-start) | copy-done | bytes 262168
  14.2 1.6 %copy-done.2 = bf16[1,8,4,128,256]{4,3,2,1,0:T(8,128)(2,1)S(1)} copy-done((bf16[1,8,4,128,256]{4,3,2,1,0:T(8,128)(2,1)S(1)}, bf16[1,8,4,128,256]{4,3,2,1,0:T(8,128)(2,1)}, u32[]{:S(2)}) %copy-start.2) | copy-done | bytes 2097176
  15.8 3.7 %sandwich012_meet.1 = (f32[4,8]{1,0:T(4,128)S(1)}, f32[2,4,128,256]{3,2,1,0:T(8,128)S(1)}) custom-call(f32[4,8]{1,0:T(4,128)S(1)} %broadcast_in_dim.6.refs_0_, bf16[4,128,256]{2,1,0:T(8,128)(2,1)S(1)} %copy-done, bf16[8,4,128,256]{3,2,1,0:T(8,128)(2,1)S(1)} %bitcast.11), custom_call_target="tpu_custom_call" | custom-call | flops 1610613760 | bytes 787432 | tf_op jit(solution)/shard_map/sandwich012_meet/pallas_call | solution.py:421
  19.5 0.0 copy-start.4
  19.5 0.0 collective-permute-done.3.refs_5_
  19.5 0.0 collective-permute-done.2.refs_4_
  19.5 1.3 %collective-permute-start.6 = (bf16[4,128,256]{2,1,0:T(8,128)(2,1)S(1)}, bf16[4,128,256]{2,1,0:T(8,128)(2,1)S(1)}, u32[]{:S(2)}, u32[]{:S(2)}) collective-permute-start(bf16[4,128,256]{2,1,0:T(8,128)(2,1)S(1)} %collective-permute-done.2.refs_4_), channel_id=1, source_target_pairs={{0,4},{4,8},{8,12},{12,14},{14,10},{10,6},{6,2},{2,0},{1,5},{5,9},... | collective-permute-start | bytes 786440 | tf_op jit(solution)/shard_map/ppermute | solution.py:550
  20.9 0.2 collective-permute-start.7
  21.0 1.8 %collective-permute-start.8 = (bf16[2,128,256]{2,1,0:T(8,128)(2,1)S(1)}, bf16[2,128,256]{2,1,0:T(8,128)(2,1)S(1)}, u32[]{:S(2)}, u32[]{:S(2)}) collective-permute-start(bf16[2,128,256]{2,1,0:T(8,128)(2,1)S(1)} %collective-permute-done.4.some_ref), channel_id=1, source_target_pairs={{0,1},{1,0},{2,3},{3,2},{4,5},{5,4},{6,7},{7,6},{8,9},{9,8},{10,11... | collective-permute-start | bytes 393224 | tf_op jit(solution)/shard_map/ppermute | solution.py:541
  22.9 2.6 %sandwich34_meet12.1 = (f32[4,8]{1,0:T(4,128)S(1)}, f32[2,4,128,256]{3,2,1,0:T(8,128)S(1)}) custom-call(f32[4,8]{1,0:T(4,128)S(1)} %get-tuple-element.36.refs_0_, bf16[4,128,256]{2,1,0:T(8,128)(2,1)S(1)} %copy-done.1, bf16[8,4,128,256]{3,2,1,0:T(8,128)(2,1)S(1)} %bitcast.12, f32[2,4,128,256]{3,2,1,0:T(8,128)S(1)} %get-tuple-element.37.refs_3_, ...), custom_call_target="tpu_custom_call" | custom-call | flops 1073742848 | bytes 525288 | tf_op jit(solution)/shard_map/sandwich34_meet12/pallas_call | solution.py:421
  25.5 0.0 copy-start.3
  25.5 1.2 %turn.1 = (bf16[4,64,256]{2,1,0:T(8,128)(2,1)S(1)}, bf16[4,64,256]{2,1,0:T(8,128)(2,1)S(1)}, s32[8]{0:T(128)S(1)}, f32[4,8]{1,0:T(4,128)S(1)}, f32[4,8]{1,0:T(4,128)S(1)}) custom-call(s32[8]{0:T(128)S(1)} %copy-done.4, bf16[4,128,256]{2,1,0:T(8,128)(2,1)S(1)} %copy-done.1), custom_call_target="tpu_custom_call" | custom-call | flops 1000 | bytes 524288 | tf_op jit(solution)/shard_map/turn/pallas_call | solution.py:465
  26.7 0.4 collective-permute-done.7.ahead_ref.refs_5_
  27.1 1.1 %collective-permute-start.10 = (bf16[4,128,256]{2,1,0:T(8,128)(2,1)S(1)}, bf16[4,128,256]{2,1,0:T(8,128)(2,1)S(1)}, u32[]{:S(2)}, u32[]{:S(2)}) collective-permute-start(bf16[4,128,256]{2,1,0:T(8,128)(2,1)S(1)} %collective-permute-done.6.behind_ref.refs_4_), channel_id=1, source_target_pairs={{0,4},{4,8},{8,12},{12,14},{14,10},{10,6},{6,2},{2,0},{1,5},{5,9},... | collective-permute-start | bytes 786440 | tf_op jit(solution)/shard_map/ppermute | solution.py:550
  28.2 0.3 collective-permute-start.11
  28.6 3.0 %collective-permute-start.5 = (bf16[4,64,256]{2,1,0:T(8,128)(2,1)S(1)}, bf16[4,64,256]{2,1,0:T(8,128)(2,1)S(1)}, u32[]{:S(2)}, u32[]{:S(2)}) collective-permute-start(bf16[4,64,256]{2,1,0:T(8,128)(2,1)S(1)} %get-tuple-element.44), channel_id=1, source_target_pairs={{0,1},{1,0},{2,3},{3,2},{4,5},{5,4},{6,7},{7,6},{8,9},{9,8},{10,11... | collective-permute-start | bytes 393224 | tf_op jit(solution)/shard_map/ppermute | solution.py:568
  31.6 1.2 %far.1 = f32[4,8]{1,0:T(4,128)S(1)} custom-call(bf16[4,128,256]{2,1,0:T(8,128)(2,1)S(1)} %collective-permute-done.6.behind_ref.refs_4_, bf16[4,128,256]{2,1,0:T(8,128)(2,1)S(1)} %collective-permute-done.7.ahead_ref.refs_5_, bf16[2,128,256]{2,1,0:T(8,128)(2,1)S(1)} %collective-permute-done.4.some_ref, bf16[2,128,256]{2,1,0:T(8,128)(2,1)S(1)} %collective-permute-done.8.rest_ref), custom_call_target="tpu_custom_call" | custom-call | flops 536870912 | bytes 524288 | tf_op jit(solution)/shard_map/far/pallas_call | solution.py:339
  32.9 0.9 %collective-permute-start.9 = (f32[4,8]{1,0:T(4,128)S(1)}, f32[4,8]{1,0:T(4,128)S(1)}, u32[]{:S(2)}, u32[]{:S(2)}) collective-permute-start(f32[4,8]{1,0:T(4,128)S(1)} %far.1), channel_id=1, source_target_pairs={{8,0},{12,4},{14,8},{10,12},{6,14},{2,10},{0,6},{4,2},{9,1},{13,5}... | collective-permute-start | bytes 392 | tf_op jit(solution)/shard_map/ppermute | solution.py:562
  33.8 2.6 %sandwich56_meet34.1 = (f32[4,8]{1,0:T(4,128)S(1)}, f32[2,4,128,256]{3,2,1,0:T(8,128)S(1)}) custom-call(f32[4,8]{1,0:T(4,128)S(1)} %get-tuple-element.51.refs_0_, bf16[4,128,256]{2,1,0:T(8,128)(2,1)S(1)} %copy-done.1, bf16[8,4,128,256]{3,2,1,0:T(8,128)(2,1)S(1)} %bitcast.13, f32[2,4,128,256]{3,2,1,0:T(8,128)S(1)} %get-tuple-element.53.refs_3_, ...), custom_call_target="tpu_custom_call" | custom-call | flops 1073742848 | bytes 525288 | tf_op jit(solution)/shard_map/sandwich56_meet34/pallas_call | solution.py:421
  36.4 0.0 collective-permute-done.10.refs_3_
  36.4 0.2 sandwich_meet56.1
  36.6 1.5 %collective-permute-start.12 = (f32[4,8]{1,0:T(4,128)S(1)}, f32[4,8]{1,0:T(4,128)S(1)}, u32[]{:S(2)}, u32[]{:S(2)}) collective-permute-start(f32[4,8]{1,0:T(4,128)S(1)} %sandwich_meet56.1), channel_id=1, source_target_pairs={{0,1},{1,0},{2,3},{3,2},{4,5},{5,4},{6,7},{7,6},{8,9},{9,8},{10,11... | collective-permute-start | bytes 392 | tf_op jit(solution)/shard_map/ppermute | solution.py:573
  38.1 1.3 %order.1 = bf16[8,64,256]{2,1,0:T(8,128)(2,1)} custom-call(s32[8]{0:T(128)S(1)} %get-tuple-element.35.place_ref, bf16[4,64,256]{2,1,0:T(8,128)(2,1)S(1)} %get-tuple-element.43.kept_ref, bf16[4,64,256]{2,1,0:T(8,128)(2,1)S(1)} %collective-permute-done.5.taken_ref), custom_call_target="tpu_custom_call" | custom-call | flops 1000 | bytes 524288 | tf_op jit(solution)/shard_map/order/pallas_call | solution.py:492
  39.5 0.7 %add_reduce_fusion = f32[8,8]{1,0:T(8,128)} fusion(f32[4,8]{1,0:T(4,128)S(1)} %collective-permute-done.12, f32[4,8]{1,0:T(4,128)S(1)} %get-tuple-element.57, f32[4,8]{1,0:T(4,128)S(1)} %sandwich_meet56.1, f32[4,8]{1,0:T(4,128)S(1)} %get-tuple-element.45), kind=kLoop, calls=%fused_computation.1 | loop fusion | flops 960 | bytes 768 | tf_op jit(solution)/shard_map/reduce_sum | solution.py:576
  (15 shorter events, 0.0 us)
Async XLA Ops:
  0.6 4.9 %collective-permute-start = (bf16[6,4,4,16,128]{4,3,2,1,0:T(8,128)(2,1)}, bf16[6,4,4,16,128]{4,3,2,1,0:T(8,128)(2,1)}, u32[]{:S(2)}, u32[]{:S(2)}) collective-permute-start(bf16[6,4,4,16,128]{4,3,2,1,0:T(8,128)(2,1)} %bitcast.19), channel_id=1, source_target_pairs={{0,1},{1,0},{2,3},{3,2},{4,5},{5,4},{6,7},{7,6},{8,9},{9,8},{10,11... | collective-permute-start | bytes 1179656 | tf_op jit(solution)/shard_map/ppermute | solution.py:515
  0.8 4.8 %collective-permute-start.1 = (f32[54,4,4,16]{3,2,1,0:T(4,128)}, f32[54,4,4,16]{3,2,1,0:T(4,128)}, u32[]{:S(2)}, u32[]{:S(2)}) collective-permute-start(f32[54,4,4,16]{3,2,1,0:T(4,128)} %bitcast.17), channel_id=1, source_target_pairs={{0,1},{1,0},{2,3},{3,2},{4,5},{5,4},{6,7},{7,6},{8,9},{9,8},{10,11... | collective-permute-start | bytes 165896 | tf_op jit(solution)/shard_map/ppermute | solution.py:516
  2.1 11.1 %collective-permute-start.4 = (bf16[2,128,256]{2,1,0:T(8,128)(2,1)S(1)}, bf16[2,128,256]{2,1,0:T(8,128)(2,1)S(1)}, u32[]{:S(2)}, u32[]{:S(2)}) collective-permute-start(bf16[2,128,256]{2,1,0:T(8,128)(2,1)S(1)} %dynamic-slice_bitcast_fusion), channel_id=1, source_target_pairs={{0,8},{4,12},{8,14},{12,10},{14,6},{10,2},{6,0},{2,4},{1,9},{5,13}... | collective-permute-start | bytes 393224 | tf_op jit(solution)/shard_map/ppermute | solution.py:531
  11.7 7.8 %collective-permute-start.3 = (bf16[4,128,256]{2,1,0:T(8,128)(2,1)}, bf16[4,128,256]{2,1,0:T(8,128)(2,1)S(1)}, u32[]{:S(2)}, u32[]{:S(2)}) collective-permute-start(bf16[4,128,256]{2,1,0:T(8,128)(2,1)} %elementals.1.refs_1_.phi_ref), channel_id=1, source_target_pairs={{4,0},{8,4},{12,8},{14,12},{10,14},{6,10},{2,6},{0,2},{5,1},{9,5},... | collective-permute-start | bytes 786440 | tf_op jit(solution)/shard_map/ppermute | solution.py:551
  11.9 7.6 %collective-permute-start.2 = (bf16[4,128,256]{2,1,0:T(8,128)(2,1)}, bf16[4,128,256]{2,1,0:T(8,128)(2,1)S(1)}, u32[]{:S(2)}, u32[]{:S(2)}) collective-permute-start(bf16[4,128,256]{2,1,0:T(8,128)(2,1)} %elementals.1.refs_1_.phi_ref), channel_id=1, source_target_pairs={{0,4},{4,8},{8,12},{12,14},{14,10},{10,6},{6,2},{2,0},{1,5},{5,9},... | collective-permute-start | bytes 786440 | tf_op jit(solution)/shard_map/ppermute | solution.py:550
  13.2 1.0 %copy-start = (bf16[4,128,256]{2,1,0:T(8,128)(2,1)S(1)}, bf16[4,128,256]{2,1,0:T(8,128)(2,1)}, u32[]{:S(2)}) copy-start(bf16[4,128,256]{2,1,0:T(8,128)(2,1)} %elementals.1.refs_1_.phi_ref) | copy-start | bytes 786436
  14.2 1.6 %copy-start.2 = (bf16[1,8,4,128,256]{4,3,2,1,0:T(8,128)(2,1)S(1)}, bf16[1,8,4,128,256]{4,3,2,1,0:T(8,128)(2,1)}, u32[]{:S(2)}) copy-start(bf16[1,8,4,128,256]{4,3,2,1,0:T(8,128)(2,1)} %param.7) | copy-start | bytes 6291460
  15.8 7.1 %copy-start.1 = (bf16[4,128,256]{2,1,0:T(8,128)(2,1)S(1)}, bf16[4,128,256]{2,1,0:T(8,128)(2,1)}, u32[]{:S(2)}) copy-start(bf16[4,128,256]{2,1,0:T(8,128)(2,1)} %elementals.1.refs_1_.phi_ref) | copy-start | bytes 786436
  19.5 6.0 %copy-start.4 = (s32[8]{0:T(128)S(1)}, s32[8]{0:T(128)}, u32[]{:S(2)}) copy-start(s32[8]{0:T(128)} %disp_ref.1) | copy-start | bytes 100
  19.5 7.2 %collective-permute-start.6 = (bf16[4,128,256]{2,1,0:T(8,128)(2,1)S(1)}, bf16[4,128,256]{2,1,0:T(8,128)(2,1)S(1)}, u32[]{:S(2)}, u32[]{:S(2)}) collective-permute-start(bf16[4,128,256]{2,1,0:T(8,128)(2,1)S(1)} %collective-permute-done.2.refs_4_), channel_id=1, source_target_pairs={{0,4},{4,8},{8,12},{12,14},{14,10},{10,6},{6,2},{2,0},{1,5},{5,9},... | collective-permute-start | bytes 786440 | tf_op jit(solution)/shard_map/ppermute | solution.py:550
  20.9 6.2 %collective-permute-start.7 = (bf16[4,128,256]{2,1,0:T(8,128)(2,1)S(1)}, bf16[4,128,256]{2,1,0:T(8,128)(2,1)S(1)}, u32[]{:S(2)}, u32[]{:S(2)}) collective-permute-start(bf16[4,128,256]{2,1,0:T(8,128)(2,1)S(1)} %collective-permute-done.3.refs_5_), channel_id=1, source_target_pairs={{4,0},{8,4},{12,8},{14,12},{10,14},{6,10},{2,6},{0,2},{5,1},{9,5},... | collective-permute-start | bytes 786440 | tf_op jit(solution)/shard_map/ppermute | solution.py:551
  21.0 10.6 %collective-permute-start.8 = (bf16[2,128,256]{2,1,0:T(8,128)(2,1)S(1)}, bf16[2,128,256]{2,1,0:T(8,128)(2,1)S(1)}, u32[]{:S(2)}, u32[]{:S(2)}) collective-permute-start(bf16[2,128,256]{2,1,0:T(8,128)(2,1)S(1)} %collective-permute-done.4.some_ref), channel_id=1, source_target_pairs={{0,1},{1,0},{2,3},{3,2},{4,5},{5,4},{6,7},{7,6},{8,9},{9,8},{10,11... | collective-permute-start | bytes 393224 | tf_op jit(solution)/shard_map/ppermute | solution.py:541
  25.5 8.3 %copy-start.3 = (bf16[1,8,4,128,256]{4,3,2,1,0:T(8,128)(2,1)S(1)}, bf16[1,8,4,128,256]{4,3,2,1,0:T(8,128)(2,1)}, u32[]{:S(2)}) copy-start(bf16[1,8,4,128,256]{4,3,2,1,0:T(8,128)(2,1)} %param.7) | copy-start | bytes 6291460
  27.1 9.3 %collective-permute-start.10 = (bf16[4,128,256]{2,1,0:T(8,128)(2,1)S(1)}, bf16[4,128,256]{2,1,0:T(8,128)(2,1)S(1)}, u32[]{:S(2)}, u32[]{:S(2)}) collective-permute-start(bf16[4,128,256]{2,1,0:T(8,128)(2,1)S(1)} %collective-permute-done.6.behind_ref.refs_4_), channel_id=1, source_target_pairs={{0,4},{4,8},{8,12},{12,14},{14,10},{10,6},{6,2},{2,0},{1,5},{5,9},... | collective-permute-start | bytes 786440 | tf_op jit(solution)/shard_map/ppermute | solution.py:550
  28.2 8.2 %collective-permute-start.11 = (bf16[4,128,256]{2,1,0:T(8,128)(2,1)S(1)}, bf16[4,128,256]{2,1,0:T(8,128)(2,1)S(1)}, u32[]{:S(2)}, u32[]{:S(2)}) collective-permute-start(bf16[4,128,256]{2,1,0:T(8,128)(2,1)S(1)} %collective-permute-done.7.ahead_ref.refs_5_), channel_id=1, source_target_pairs={{4,0},{8,4},{12,8},{14,12},{10,14},{6,10},{2,6},{0,2},{5,1},{9,5},... | collective-permute-start | bytes 786440 | tf_op jit(solution)/shard_map/ppermute | solution.py:551
  28.6 9.6 %collective-permute-start.5 = (bf16[4,64,256]{2,1,0:T(8,128)(2,1)S(1)}, bf16[4,64,256]{2,1,0:T(8,128)(2,1)S(1)}, u32[]{:S(2)}, u32[]{:S(2)}) collective-permute-start(bf16[4,64,256]{2,1,0:T(8,128)(2,1)S(1)} %get-tuple-element.44), channel_id=1, source_target_pairs={{0,1},{1,0},{2,3},{3,2},{4,5},{5,4},{6,7},{7,6},{8,9},{9,8},{10,11... | collective-permute-start | bytes 393224 | tf_op jit(solution)/shard_map/ppermute | solution.py:568
  32.9 3.5 %collective-permute-start.9 = (f32[4,8]{1,0:T(4,128)S(1)}, f32[4,8]{1,0:T(4,128)S(1)}, u32[]{:S(2)}, u32[]{:S(2)}) collective-permute-start(f32[4,8]{1,0:T(4,128)S(1)} %far.1), channel_id=1, source_target_pairs={{8,0},{12,4},{14,8},{10,12},{6,14},{2,10},{0,6},{4,2},{9,1},{13,5}... | collective-permute-start | bytes 392 | tf_op jit(solution)/shard_map/ppermute | solution.py:562
  36.6 2.8 %collective-permute-start.12 = (f32[4,8]{1,0:T(4,128)S(1)}, f32[4,8]{1,0:T(4,128)S(1)}, u32[]{:S(2)}, u32[]{:S(2)}) collective-permute-start(f32[4,8]{1,0:T(4,128)S(1)} %sandwich_meet56.1), channel_id=1, source_target_pairs={{0,1},{1,0},{2,3},{3,2},{4,5},{5,4},{6,7},{7,6},{8,9},{9,8},{10,11... | collective-permute-start | bytes 392 | tf_op jit(solution)/shard_map/ppermute | solution.py:573

commit v5 on v4

--- a/solution.py
+++ b/solution.py
@@ -250,7 +250,7 @@
         ],
         compiler_params=pltpu.CompilerParams(vmem_limit_bytes=65000 * 1024),
         cost_estimate=pl.CostEstimate(
-            flops=count * 2 * sites * eigen * 2 * eigen,
+            flops=16 * count * sites * eigen * 2 * eigen,
             bytes_accessed=2 * own.size * 2,
             transcendentals=0,
         ),
@@ -567,7 +567,8 @@
             table, kept, given = lax.optimization_barrier((table, kept, given))
             taken = lax.ppermute(given, "space", swap)
         if step < steps - 1:
-            one_way, other_way, table, phi = lax.optimization_barrier((one_way, other_way, table, phi))
+            one_way, _ = lax.optimization_barrier((one_way, table))
+            other_way, _ = lax.optimization_barrier((other_way, table))
             came = [one_way, other_way] if ring else arrivals
     (table,) = sandwich_step(table, phi, peram, [], before, came, met, ring, extra)
     other_table = lax.ppermute(table, "space", swap)

time: 40.4 us -> 39.6 us (0.980)
  starting transfers between devices: 15.8 us -> 15.3 us
    ppermute x1, starting transfers between devices: 0.93 us -> 2.3 us  [body(): extra = (lax.ppermute(back, 'tm', two_behind),)]
    ppermute x1, starting transfers between devices: 1.51 us -> 0.32 us  [body(): other_table = lax.ppermute(table, 'space', swap)]
    ppermute x1, starting transfers between devices: 3.04 us -> 2.22 us  [body(): taken = lax.ppermute(given, 'space', swap)]
  transfers between devices with their start and end apart: 13 -> 13, of which waited for: 1 -> 0; matrix products, arithmetic and copies ran while one was open for 2% -> 2% of each run, Pallas kernels for 47% -> 48%
where the time goes in v5:
time: 39.6 us; the launch traced here: 39.2 us
  Pallas kernels  18.9 us (48%)
  starting transfers between devices  15.3 us (39%)
  local copies, waits for them, and re-layouts  3.49 us (9%)
  between operations  0.75 us (2%)
  other arithmetic  0.67 us (2%)
    pallas_call x4, Pallas kernels, sandwich_step(): pl.pallas_call(functools.partial(sandwich_kernel, tuple(made), tuple(met)...  9.06 us
    pallas_call x1, Pallas kernels, elementals(): pl.pallas_call(functools.partial(elemental_kernel, norm_factor), out_shap...  6.12 us
    ppermute x3, starting transfers between devices, body(): one_way = lax.ppermute(one_way, 'tm', ahead)  3.44 us
    ppermute x1, starting transfers between devices, body(): some = lax.ppermute(some, 'tm', two_ahead)  3.44 us
    unnamed x10, local copies, waits for them, and re-layouts  2.58 us
    ppermute x1, starting transfers between devices, body(): extra = (lax.ppermute(back, 'tm', two_behind),)  2.3 us
    ppermute x1, starting transfers between devices, body(): taken = lax.ppermute(given, 'space', swap)  2.22 us
    ppermute x1, starting transfers between devices, body(): rest = lax.ppermute(some, 'space', swap)  1.89 us
  transfers between devices with their start and end apart: 13, of which 0 were waited for; matrix products, arithmetic and copies ran while one was open for 2% of the time, Pallas kernels for 48%

profile of v5, /device:TPU:1, one launch (start us, length us, event | category | flops | bytes accessed | tf_op | source)
XLA Modules:
  0.0 39.2 jit_solution(10992199553532004214)
XLA Ops:
  0.6 0.1 collective-permute-start
  0.8 0.5 %collective-permute-start.1 = (f32[54,4,4,16]{3,2,1,0:T(4,128)}, f32[54,4,4,16]{3,2,1,0:T(4,128)}, u32[]{:S(2)}, u32[]{:S(2)}) collective-permute-start(f32[54,4,4,16]{3,2,1,0:T(4,128)} %bitcast.17), channel_id=1, source_target_pairs={{0,1},{1,0},{2,3},{3,2},{4,5},{5,4},{6,7},{7,6},{8,9},{9,8},{10,11... | collective-permute-start | bytes 165896 | tf_op jit(solution)/shard_map/ppermute | solution.py:516
  1.2 0.9 %dynamic-slice_bitcast_fusion = bf16[2,128,256]{2,1,0:T(8,128)(2,1)S(1)} fusion(bf16[1,8,4,128,256]{4,3,2,1,0:T(8,128)(2,1)} %param.7, s32[]{:T(128)S(6)} %select_n.41, s32[]{:T(128)S(6)} %select_n.42), kind=kLoop, calls=%fused_computation | loop fusion | bytes 262152 | tf_op jit(solution)/shard_map/squeeze | solution.py:530
  2.1 3.4 %collective-permute-start.2 = (bf16[2,128,256]{2,1,0:T(8,128)(2,1)S(1)}, bf16[2,128,256]{2,1,0:T(8,128)(2,1)S(1)}, u32[]{:S(2)}, u32[]{:S(2)}) collective-permute-start(bf16[2,128,256]{2,1,0:T(8,128)(2,1)S(1)} %dynamic-slice_bitcast_fusion), channel_id=1, source_target_pairs={{0,8},{4,12},{8,14},{12,10},{14,6},{10,2},{6,0},{2,4},{1,9},{5,13}... | collective-permute-start | bytes 393224 | tf_op jit(solution)/shard_map/ppermute | solution.py:531
  5.6 0.0 collective-permute-done.1.other_links_hbm
  5.6 0.0 collective-permute-done.other_hbm
  5.6 6.1 %elementals.1.phi_ref.refs_1_ = bf16[4,128,256]{2,1,0:T(8,128)(2,1)} custom-call(s32[1,8]{1,0:T(1,128)} %bitcast.14, s32[3,8]{1,0:T(4,128)} %bitcast.21, bf16[6,4,4,16,128]{4,3,2,1,0:T(8,128)(2,1)} %bitcast.20, bf16[6,4,4,16,128]{4,3,2,1,0:T(8,128)(2,1)} %collective-permute-done.other_hbm, f32[54,4,4,16]{3,2,1,0:T(4,128)} %bitcast.18, ...), custom_call_target="tpu_custom_call" | custom-call | flops 6442450944 | bytes 786432 | tf_op jit(solution)/shard_map/elementals/pallas_call | solution.py:234
  11.7 0.2 collective-permute-start.4
  11.9 1.3 %collective-permute-start.3 = (bf16[4,128,256]{2,1,0:T(8,128)(2,1)}, bf16[4,128,256]{2,1,0:T(8,128)(2,1)S(1)}, u32[]{:S(2)}, u32[]{:S(2)}) collective-permute-start(bf16[4,128,256]{2,1,0:T(8,128)(2,1)} %elementals.1.phi_ref.refs_1_), channel_id=1, source_target_pairs={{0,4},{4,8},{8,12},{12,14},{14,10},{10,6},{6,2},{2,0},{1,5},{5,9},... | collective-permute-start | bytes 786440 | tf_op jit(solution)/shard_map/ppermute | solution.py:550
  13.2 1.0 %copy-done = bf16[4,128,256]{2,1,0:T(8,128)(2,1)S(1)} copy-done((bf16[4,128,256]{2,1,0:T(8,128)(2,1)S(1)}, bf16[4,128,256]{2,1,0:T(8,128)(2,1)}, u32[]{:S(2)}) %copy-start) | copy-done | bytes 262168
  14.2 1.6 %copy-done.2 = bf16[1,8,4,128,256]{4,3,2,1,0:T(8,128)(2,1)S(1)} copy-done((bf16[1,8,4,128,256]{4,3,2,1,0:T(8,128)(2,1)S(1)}, bf16[1,8,4,128,256]{4,3,2,1,0:T(8,128)(2,1)}, u32[]{:S(2)}) %copy-start.2) | copy-done | bytes 2097176
  15.8 3.7 %sandwich012_meet.1 = (f32[4,8]{1,0:T(4,128)S(1)}, f32[2,4,128,256]{3,2,1,0:T(8,128)S(1)}) custom-call(f32[4,8]{1,0:T(4,128)S(1)} %broadcast_in_dim.6.refs_0_, bf16[4,128,256]{2,1,0:T(8,128)(2,1)S(1)} %copy-done, bf16[8,4,128,256]{3,2,1,0:T(8,128)(2,1)S(1)} %bitcast.11), custom_call_target="tpu_custom_call" | custom-call | flops 1610613760 | bytes 787432 | tf_op jit(solution)/shard_map/sandwich012_meet/pallas_call | solution.py:421
  19.5 0.0 collective-permute-done.4.refs_5_
  19.5 0.2 collective-permute-start.7
  19.7 1.3 %collective-permute-start.6 = (bf16[4,128,256]{2,1,0:T(8,128)(2,1)S(1)}, bf16[4,128,256]{2,1,0:T(8,128)(2,1)S(1)}, u32[]{:S(2)}, u32[]{:S(2)}) collective-permute-start(bf16[4,128,256]{2,1,0:T(8,128)(2,1)S(1)} %collective-permute-done.3.refs_4_), channel_id=1, source_target_pairs={{0,4},{4,8},{8,12},{12,14},{14,10},{10,6},{6,2},{2,0},{1,5},{5,9},... | collective-permute-start | bytes 786440 | tf_op jit(solution)/shard_map/ppermute | solution.py:550
  21.0 1.2 %turn.1 = (bf16[4,64,256]{2,1,0:T(8,128)(2,1)S(1)}, bf16[4,64,256]{2,1,0:T(8,128)(2,1)S(1)}, s32[8]{0:T(128)S(1)}, f32[4,8]{1,0:T(4,128)S(1)}, f32[4,8]{1,0:T(4,128)S(1)}) custom-call(s32[8]{0:T(128)S(1)} %copy-done.4, bf16[4,128,256]{2,1,0:T(8,128)(2,1)S(1)} %copy-done), custom_call_target="tpu_custom_call" | custom-call | flops 1000 | bytes 524288 | tf_op jit(solution)/shard_map/turn/pallas_call | solution.py:465
  22.2 1.9 %collective-permute-start.8 = (bf16[2,128,256]{2,1,0:T(8,128)(2,1)S(1)}, bf16[2,128,256]{2,1,0:T(8,128)(2,1)S(1)}, u32[]{:S(2)}, u32[]{:S(2)}) collective-permute-start(bf16[2,128,256]{2,1,0:T(8,128)(2,1)S(1)} %collective-permute-done.2.some_ref), channel_id=1, source_target_pairs={{0,1},{1,0},{2,3},{3,2},{4,5},{5,4},{6,7},{7,6},{8,9},{9,8},{10,11... | collective-permute-start | bytes 393224 | tf_op jit(solution)/shard_map/ppermute | solution.py:541
  24.1 2.6 %sandwich34_meet12.1 = (f32[4,8]{1,0:T(4,128)S(1)}, f32[2,4,128,256]{3,2,1,0:T(8,128)S(1)}) custom-call(f32[4,8]{1,0:T(4,128)S(1)} %get-tuple-element.30.refs_0_, bf16[4,128,256]{2,1,0:T(8,128)(2,1)S(1)} %copy-done.1, bf16[8,4,128,256]{3,2,1,0:T(8,128)(2,1)S(1)} %bitcast.12, f32[2,4,128,256]{3,2,1,0:T(8,128)S(1)} %get-tuple-element.31.refs_3_, ...), custom_call_target="tpu_custom_call" | custom-call | flops 1073742848 | bytes 525288 | tf_op jit(solution)/shard_map/sandwich34_meet12/pallas_call | solution.py:421
  26.7 0.0 collective-permute-done.6.behind_ref.refs_4_
  26.7 0.7 %collective-permute-start.11 = (bf16[4,128,256]{2,1,0:T(8,128)(2,1)S(1)}, bf16[4,128,256]{2,1,0:T(8,128)(2,1)S(1)}, u32[]{:S(2)}, u32[]{:S(2)}) collective-permute-start(bf16[4,128,256]{2,1,0:T(8,128)(2,1)S(1)} %collective-permute-done.7.ahead_ref.refs_5_), channel_id=1, source_target_pairs={{4,0},{8,4},{12,8},{14,12},{10,14},{6,10},{2,6},{0,2},{5,1},{9,5},... | collective-permute-start | bytes 786440 | tf_op jit(solution)/shard_map/ppermute | solution.py:551
  27.4 0.9 %collective-permute-start.10 = (bf16[4,128,256]{2,1,0:T(8,128)(2,1)S(1)}, bf16[4,128,256]{2,1,0:T(8,128)(2,1)S(1)}, u32[]{:S(2)}, u32[]{:S(2)}) collective-permute-start(bf16[4,128,256]{2,1,0:T(8,128)(2,1)S(1)} %collective-permute-done.6.behind_ref.refs_4_), channel_id=1, source_target_pairs={{0,4},{4,8},{8,12},{12,14},{14,10},{10,6},{6,2},{2,0},{1,5},{5,9},... | collective-permute-start | bytes 786440 | tf_op jit(solution)/shard_map/ppermute | solution.py:550
  28.3 2.2 %collective-permute-start.5 = (bf16[4,64,256]{2,1,0:T(8,128)(2,1)S(1)}, bf16[4,64,256]{2,1,0:T(8,128)(2,1)S(1)}, u32[]{:S(2)}, u32[]{:S(2)}) collective-permute-start(bf16[4,64,256]{2,1,0:T(8,128)(2,1)S(1)} %get-tuple-element.38), channel_id=1, source_target_pairs={{0,1},{1,0},{2,3},{3,2},{4,5},{5,4},{6,7},{7,6},{8,9},{9,8},{10,11... | collective-permute-start | bytes 393224 | tf_op jit(solution)/shard_map/ppermute | solution.py:568
  30.5 0.0 collective-permute-done.8.rest_ref
  30.5 1.2 %far.1 = f32[4,8]{1,0:T(4,128)S(1)} custom-call(bf16[4,128,256]{2,1,0:T(8,128)(2,1)S(1)} %collective-permute-done.6.behind_ref.refs_4_, bf16[4,128,256]{2,1,0:T(8,128)(2,1)S(1)} %collective-permute-done.7.ahead_ref.refs_5_, bf16[2,128,256]{2,1,0:T(8,128)(2,1)S(1)} %collective-permute-done.2.some_ref, bf16[2,128,256]{2,1,0:T(8,128)(2,1)S(1)} %collective-permute-done.8.rest_ref), custom_call_target="tpu_custom_call" | custom-call | flops 536870912 | bytes 524288 | tf_op jit(solution)/shard_map/far/pallas_call | solution.py:339
  31.7 2.3 %collective-permute-start.9 = (f32[4,8]{1,0:T(4,128)S(1)}, f32[4,8]{1,0:T(4,128)S(1)}, u32[]{:S(2)}, u32[]{:S(2)}) collective-permute-start(f32[4,8]{1,0:T(4,128)S(1)} %far.1), channel_id=1, source_target_pairs={{8,0},{12,4},{14,8},{10,12},{6,14},{2,10},{0,6},{4,2},{9,1},{13,5}... | collective-permute-start | bytes 392 | tf_op jit(solution)/shard_map/ppermute | solution.py:562
  34.0 2.6 %sandwich56_meet34.1 = (f32[4,8]{1,0:T(4,128)S(1)}, f32[2,4,128,256]{3,2,1,0:T(8,128)S(1)}) custom-call(f32[4,8]{1,0:T(4,128)S(1)} %get-tuple-element.44.refs_0_, bf16[4,128,256]{2,1,0:T(8,128)(2,1)S(1)} %copy-done.1, bf16[8,4,128,256]{3,2,1,0:T(8,128)(2,1)S(1)} %bitcast.13, f32[2,4,128,256]{3,2,1,0:T(8,128)S(1)} %get-tuple-element.45.refs_3_, ...), custom_call_target="tpu_custom_call" | custom-call | flops 1073742848 | bytes 525288 | tf_op jit(solution)/shard_map/sandwich56_meet34/pallas_call | solution.py:421
  36.6 0.0 collective-permute-done.9.refs_1_
  36.6 0.0 collective-permute-done.11.refs_4_
  36.6 0.2 sandwich_meet56.1
  36.9 0.3 collective-permute-start.12
  37.2 1.3 %order.1 = bf16[8,64,256]{2,1,0:T(8,128)(2,1)} custom-call(s32[8]{0:T(128)S(1)} %get-tuple-element.29.place_ref, bf16[4,64,256]{2,1,0:T(8,128)(2,1)S(1)} %get-tuple-element.37.kept_ref, bf16[4,64,256]{2,1,0:T(8,128)(2,1)S(1)} %collective-permute-done.5.taken_ref), custom_call_target="tpu_custom_call" | custom-call | flops 1000 | bytes 524288 | tf_op jit(solution)/shard_map/order/pallas_call | solution.py:492
  38.5 0.7 %add_reduce_fusion = f32[8,8]{1,0:T(8,128)} fusion(f32[4,8]{1,0:T(4,128)S(1)} %collective-permute-done.12, f32[4,8]{1,0:T(4,128)S(1)} %get-tuple-element.49, f32[4,8]{1,0:T(4,128)S(1)} %sandwich_meet56.1, f32[4,8]{1,0:T(4,128)S(1)} %get-tuple-element.39), kind=kLoop, calls=%fused_computation.1 | loop fusion | flops 960 | bytes 768 | tf_op jit(solution)/shard_map/reduce_sum | solution.py:577
  (15 shorter events, 0.0 us)
Async XLA Ops:
  0.6 4.9 %collective-permute-start = (bf16[6,4,4,16,128]{4,3,2,1,0:T(8,128)(2,1)}, bf16[6,4,4,16,128]{4,3,2,1,0:T(8,128)(2,1)}, u32[]{:S(2)}, u32[]{:S(2)}) collective-permute-start(bf16[6,4,4,16,128]{4,3,2,1,0:T(8,128)(2,1)} %bitcast.19), channel_id=1, source_target_pairs={{0,1},{1,0},{2,3},{3,2},{4,5},{5,4},{6,7},{7,6},{8,9},{9,8},{10,11... | collective-permute-start | bytes 1179656 | tf_op jit(solution)/shard_map/ppermute | solution.py:515
  0.8 4.8 %collective-permute-start.1 = (f32[54,4,4,16]{3,2,1,0:T(4,128)}, f32[54,4,4,16]{3,2,1,0:T(4,128)}, u32[]{:S(2)}, u32[]{:S(2)}) collective-permute-start(f32[54,4,4,16]{3,2,1,0:T(4,128)} %bitcast.17), channel_id=1, source_target_pairs={{0,1},{1,0},{2,3},{3,2},{4,5},{5,4},{6,7},{7,6},{8,9},{9,8},{10,11... | collective-permute-start | bytes 165896 | tf_op jit(solution)/shard_map/ppermute | solution.py:516
  2.1 11.1 %collective-permute-start.2 = (bf16[2,128,256]{2,1,0:T(8,128)(2,1)S(1)}, bf16[2,128,256]{2,1,0:T(8,128)(2,1)S(1)}, u32[]{:S(2)}, u32[]{:S(2)}) collective-permute-start(bf16[2,128,256]{2,1,0:T(8,128)(2,1)S(1)} %dynamic-slice_bitcast_fusion), channel_id=1, source_target_pairs={{0,8},{4,12},{8,14},{12,10},{14,6},{10,2},{6,0},{2,4},{1,9},{5,13}... | collective-permute-start | bytes 393224 | tf_op jit(solution)/shard_map/ppermute | solution.py:531
  11.7 7.8 %collective-permute-start.4 = (bf16[4,128,256]{2,1,0:T(8,128)(2,1)}, bf16[4,128,256]{2,1,0:T(8,128)(2,1)S(1)}, u32[]{:S(2)}, u32[]{:S(2)}) collective-permute-start(bf16[4,128,256]{2,1,0:T(8,128)(2,1)} %elementals.1.phi_ref.refs_1_), channel_id=1, source_target_pairs={{4,0},{8,4},{12,8},{14,12},{10,14},{6,10},{2,6},{0,2},{5,1},{9,5},... | collective-permute-start | bytes 786440 | tf_op jit(solution)/shard_map/ppermute | solution.py:551
  11.9 7.8 %collective-permute-start.3 = (bf16[4,128,256]{2,1,0:T(8,128)(2,1)}, bf16[4,128,256]{2,1,0:T(8,128)(2,1)S(1)}, u32[]{:S(2)}, u32[]{:S(2)}) collective-permute-start(bf16[4,128,256]{2,1,0:T(8,128)(2,1)} %elementals.1.phi_ref.refs_1_), channel_id=1, source_target_pairs={{0,4},{4,8},{8,12},{12,14},{14,10},{10,6},{6,2},{2,0},{1,5},{5,9},... | collective-permute-start | bytes 786440 | tf_op jit(solution)/shard_map/ppermute | solution.py:550
  13.2 1.0 %copy-start = (bf16[4,128,256]{2,1,0:T(8,128)(2,1)S(1)}, bf16[4,128,256]{2,1,0:T(8,128)(2,1)}, u32[]{:S(2)}) copy-start(bf16[4,128,256]{2,1,0:T(8,128)(2,1)} %elementals.1.phi_ref.refs_1_) | copy-start | bytes 786436
  14.2 1.6 %copy-start.2 = (bf16[1,8,4,128,256]{4,3,2,1,0:T(8,128)(2,1)S(1)}, bf16[1,8,4,128,256]{4,3,2,1,0:T(8,128)(2,1)}, u32[]{:S(2)}) copy-start(bf16[1,8,4,128,256]{4,3,2,1,0:T(8,128)(2,1)} %param.7) | copy-start | bytes 6291460
  15.8 5.2 %copy-start.4 = (s32[8]{0:T(128)S(1)}, s32[8]{0:T(128)}, u32[]{:S(2)}) copy-start(s32[8]{0:T(128)} %disp_ref.1) | copy-start | bytes 100
  15.8 8.3 %copy-start.1 = (bf16[4,128,256]{2,1,0:T(8,128)(2,1)S(1)}, bf16[4,128,256]{2,1,0:T(8,128)(2,1)}, u32[]{:S(2)}) copy-start(bf16[4,128,256]{2,1,0:T(8,128)(2,1)} %elementals.1.phi_ref.refs_1_) | copy-start | bytes 786436
  19.5 7.2 %collective-permute-start.7 = (bf16[4,128,256]{2,1,0:T(8,128)(2,1)S(1)}, bf16[4,128,256]{2,1,0:T(8,128)(2,1)S(1)}, u32[]{:S(2)}, u32[]{:S(2)}) collective-permute-start(bf16[4,128,256]{2,1,0:T(8,128)(2,1)S(1)} %collective-permute-done.4.refs_5_), channel_id=1, source_target_pairs={{4,0},{8,4},{12,8},{14,12},{10,14},{6,10},{2,6},{0,2},{5,1},{9,5},... | collective-permute-start | bytes 786440 | tf_op jit(solution)/shard_map/ppermute | solution.py:551
  19.7 7.0 %collective-permute-start.6 = (bf16[4,128,256]{2,1,0:T(8,128)(2,1)S(1)}, bf16[4,128,256]{2,1,0:T(8,128)(2,1)S(1)}, u32[]{:S(2)}, u32[]{:S(2)}) collective-permute-start(bf16[4,128,256]{2,1,0:T(8,128)(2,1)S(1)} %collective-permute-done.3.refs_4_), channel_id=1, source_target_pairs={{0,4},{4,8},{8,12},{12,14},{14,10},{10,6},{6,2},{2,0},{1,5},{5,9},... | collective-permute-start | bytes 786440 | tf_op jit(solution)/shard_map/ppermute | solution.py:550
  22.2 8.2 %collective-permute-start.8 = (bf16[2,128,256]{2,1,0:T(8,128)(2,1)S(1)}, bf16[2,128,256]{2,1,0:T(8,128)(2,1)S(1)}, u32[]{:S(2)}, u32[]{:S(2)}) collective-permute-start(bf16[2,128,256]{2,1,0:T(8,128)(2,1)S(1)} %collective-permute-done.2.some_ref), channel_id=1, source_target_pairs={{0,1},{1,0},{2,3},{3,2},{4,5},{5,4},{6,7},{7,6},{8,9},{9,8},{10,11... | collective-permute-start | bytes 393224 | tf_op jit(solution)/shard_map/ppermute | solution.py:541
  24.1 9.9 %copy-start.3 = (bf16[1,8,4,128,256]{4,3,2,1,0:T(8,128)(2,1)S(1)}, bf16[1,8,4,128,256]{4,3,2,1,0:T(8,128)(2,1)}, u32[]{:S(2)}) copy-start(bf16[1,8,4,128,256]{4,3,2,1,0:T(8,128)(2,1)} %param.7) | copy-start | bytes 6291460
  26.7 9.9 %collective-permute-start.11 = (bf16[4,128,256]{2,1,0:T(8,128)(2,1)S(1)}, bf16[4,128,256]{2,1,0:T(8,128)(2,1)S(1)}, u32[]{:S(2)}, u32[]{:S(2)}) collective-permute-start(bf16[4,128,256]{2,1,0:T(8,128)(2,1)S(1)} %collective-permute-done.7.ahead_ref.refs_5_), channel_id=1, source_target_pairs={{4,0},{8,4},{12,8},{14,12},{10,14},{6,10},{2,6},{0,2},{5,1},{9,5},... | collective-permute-start | bytes 786440 | tf_op jit(solution)/shard_map/ppermute | solution.py:551
  27.4 9.2 %collective-permute-start.10 = (bf16[4,128,256]{2,1,0:T(8,128)(2,1)S(1)}, bf16[4,128,256]{2,1,0:T(8,128)(2,1)S(1)}, u32[]{:S(2)}, u32[]{:S(2)}) collective-permute-start(bf16[4,128,256]{2,1,0:T(8,128)(2,1)S(1)} %collective-permute-done.6.behind_ref.refs_4_), channel_id=1, source_target_pairs={{0,4},{4,8},{8,12},{12,14},{14,10},{10,6},{6,2},{2,0},{1,5},{5,9},... | collective-permute-start | bytes 786440 | tf_op jit(solution)/shard_map/ppermute | solution.py:550
  28.3 8.9 %collective-permute-start.5 = (bf16[4,64,256]{2,1,0:T(8,128)(2,1)S(1)}, bf16[4,64,256]{2,1,0:T(8,128)(2,1)S(1)}, u32[]{:S(2)}, u32[]{:S(2)}) collective-permute-start(bf16[4,64,256]{2,1,0:T(8,128)(2,1)S(1)} %get-tuple-element.38), channel_id=1, source_target_pairs={{0,1},{1,0},{2,3},{3,2},{4,5},{5,4},{6,7},{7,6},{8,9},{9,8},{10,11... | collective-permute-start | bytes 393224 | tf_op jit(solution)/shard_map/ppermute | solution.py:568
  31.7 4.9 %collective-permute-start.9 = (f32[4,8]{1,0:T(4,128)S(1)}, f32[4,8]{1,0:T(4,128)S(1)}, u32[]{:S(2)}, u32[]{:S(2)}) collective-permute-start(f32[4,8]{1,0:T(4,128)S(1)} %far.1), channel_id=1, source_target_pairs={{8,0},{12,4},{14,8},{10,12},{6,14},{2,10},{0,6},{4,2},{9,1},{13,5}... | collective-permute-start | bytes 392 | tf_op jit(solution)/shard_map/ppermute | solution.py:562
  36.9 1.6 %collective-permute-start.12 = (f32[4,8]{1,0:T(4,128)S(1)}, f32[4,8]{1,0:T(4,128)S(1)}, u32[]{:S(2)}, u32[]{:S(2)}) collective-permute-start(f32[4,8]{1,0:T(4,128)S(1)} %sandwich_meet56.1), channel_id=1, source_target_pairs={{0,1},{1,0},{2,3},{3,2},{4,5},{5,4},{6,7},{7,6},{8,9},{9,8},{10,11... | collective-permute-start | bytes 392 | tf_op jit(solution)/shard_map/ppermute | solution.py:574
